TPU v7x, 256 devices: a whole 4x4x8 slice. The times are simulated.
256 devices in a mesh: inst: 8 (over y, core), tp: 32 (over z, x).
Axes of the slice: x: 4, y: 4, z: 8, core: 2. Of those that a mesh axis runs over, the one named last changes fastest.
Arguments:
- queries: bfloat16 [2, 64, 8192], P(None, 'inst', 'tp'), may hold values from -32 to 32
- new_keys: bfloat16 [2, 64, 1024], P(None, 'inst'), may hold values from -6 to 6
- new_values: bfloat16 [2, 64, 1024], P(None, 'inst'), may hold values from -6 to 6
- k_cache: bfloat16 [4096, 128, 1024], P(('inst', 'tp')), may hold values from -4 to 4
- v_cache: bfloat16 [4096, 128, 1024], P(('inst', 'tp')), may hold values from -6 to 6
- block_req: int32 [4096], P(('inst', 'tp')), may hold values from 0 to 63
- block_fill: int32 [4096], P(('inst', 'tp')), may hold values from 1 to 128
Outputs:
- attended: bfloat16 [2, 64, 8192], P(None, 'inst', 'tp')
All inputs are finite; a program needn't handle non-finite values.
Results may differ from a plain program's by a relative error of at most 0.0041.
Values may be sent and summed in bfloat16 or wider, within the bound.
No kernel may reach another device: no remote copies, remote signals or barrier semaphores. Data moves between devices by JAX's collectives and lax.ppermute only.
A program may use at most 64 MiB of HBM per device.

v0:
```python
import jax
import jax.numpy as jnp
from jax import lax
from jax.sharding import PartitionSpec as P

H = 64
KVH = 8
DH = 128
BLK = 128


far_below = -1e30


def finish(own_q, new_keys, new_values, peak_own, numerators, denominators, kv_index):
    n_steps = own_q.shape[0]
    own_rows = own_q.shape[1]
    own_heads = kv_index.shape[0]
    query_b = own_q.reshape(n_steps, own_rows, own_heads, DH)
    keys_b = jnp.take(new_keys.reshape(n_steps, own_rows, KVH, DH), kv_index, axis=2)
    values_f = jnp.take(new_values.reshape(n_steps, own_rows, KVH, DH), kv_index, axis=2).astype(
        jnp.float32
    )
    fresh_scores = jnp.einsum(
        "srhd,jrhd->sjrh", query_b, keys_b, preferred_element_type=jnp.float32
    ) * DH ** (-0.5)
    causal = (
        jnp.arange(n_steps, dtype=jnp.int32)[None, :]
        <= jnp.arange(n_steps, dtype=jnp.int32)[:, None]
    )
    fresh_scores = jnp.where(causal[:, :, None, None], fresh_scores, far_below)
    highest = jnp.maximum(peak_own, jnp.max(fresh_scores, axis=1))
    retain = jnp.exp(peak_own - highest)
    fresh_w = jnp.exp(fresh_scores - highest[:, None])
    numerator = numerators * retain[..., None] + jnp.sum(
        fresh_w[..., None] * values_f[None], axis=1
    )
    denominator = denominators * retain + jnp.sum(fresh_w, axis=1)
    return (
        (numerator / denominator[..., None])
        .reshape(n_steps, own_rows, own_heads * DH)
        .astype(jnp.bfloat16)
    )


def body(queries, new_keys, new_values, k_cache, v_cache, block_req, block_fill):
    q_group = lax.all_gather(queries, "tp", axis=2, tiled=True)
    q_every = lax.all_gather(q_group, "inst", axis=1, tiled=True)
    n_steps = queries.shape[0]
    requests = q_every.shape[1]
    slot_count = k_cache.shape[0]
    per_kv = H // KVH
    picked = q_every[:, block_req].reshape(n_steps, slot_count, KVH, per_kv, DH)
    keys_b = k_cache.reshape(slot_count, BLK, KVH, DH)
    values_b = v_cache.reshape(slot_count, BLK, KVH, DH)
    scores = jnp.einsum(
        "sbgqd,btgd->sbgqt", picked, keys_b, preferred_element_type=jnp.float32
    ) * DH ** (-0.5)
    in_block = jnp.arange(BLK, dtype=jnp.int32)[None, :] < block_fill[:, None]
    scores = jnp.where(in_block[None, :, None, None, :], scores, far_below)
    highest = jnp.max(scores, axis=-1)
    chances = jnp.exp(scores - highest[..., None])
    totals = jnp.sum(chances, axis=-1).reshape(n_steps, slot_count, H)
    rounded = chances.astype(jnp.bfloat16)
    mixed_out = jnp.einsum(
        "sbgqt,btgd->sbgqd", rounded, values_b, preferred_element_type=jnp.float32
    )
    mixed_out = mixed_out.reshape(n_steps, slot_count, H, DH)
    highest = highest.reshape(n_steps, slot_count, H)
    owner_hot = block_req[None, :] == jnp.arange(requests, dtype=jnp.int32)[:, None]
    local_peak = jnp.max(
        jnp.where(owner_hot[None, :, :, None], highest[:, None, :, :], far_below), axis=2
    )
    peak_all = lax.pmax(local_peak.astype(jnp.bfloat16), ("inst", "tp")).astype(local_peak.dtype)
    factor = jnp.exp(highest - peak_all[:, block_req])
    scaled_out = mixed_out * factor[..., None]
    scaled_tot = totals * factor
    hot_f = owner_hot.astype(jnp.float32)
    numerators = jnp.einsum("rb,sbhd->srhd", hot_f, scaled_out, precision=lax.Precision.HIGHEST)
    numerators = numerators.reshape(n_steps, requests, H * DH)
    denominators = jnp.einsum("rb,sbh->srh", hot_f, scaled_tot, precision=lax.Precision.HIGHEST)
    numer_heads, denom_heads = (
        lax.psum_scatter(numerators, "tp", scatter_dimension=2, tiled=True),
        lax.psum_scatter(denominators, "tp", scatter_dimension=2, tiled=True),
    )
    numer_own, denom_own = (
        lax.psum_scatter(numer_heads, "inst", scatter_dimension=1, tiled=True),
        lax.psum_scatter(denom_heads, "inst", scatter_dimension=1, tiled=True),
    )
    own_rows = queries.shape[1]
    own_heads = queries.shape[2] // DH
    first_row = lax.axis_index("inst") * own_rows
    first_head = lax.axis_index("tp") * own_heads
    peak_own = lax.dynamic_slice(
        peak_all, (jnp.int32(0), first_row, first_head), (n_steps, own_rows, own_heads)
    )
    kv_index = (first_head + jnp.arange(own_heads, dtype=jnp.int32)) // per_kv
    return finish(
        queries,
        new_keys,
        new_values,
        peak_own,
        numer_own.reshape(n_steps, own_rows, own_heads, DH),
        denom_own,
        kv_index,
    )


def solution(mesh):
    return jax.shard_map(
        body,
        mesh=mesh,
        in_specs=(
            P(None, "inst", "tp"),
            P(None, "inst", None),
            P(None, "inst", None),
            P(("inst", "tp"), None, None),
            P(("inst", "tp"), None, None),
            P(("inst", "tp")),
            P(("inst", "tp")),
        ),
        out_specs=P(None, "inst", "tp"),
        check_vma=False,
    )
```

profile of v0, /device:TPU:1, one launch (start us, length us, event | category | flops | bytes accessed | tf_op | source)
XLA Modules:
  0.0 436.5 jit_solution(12047110906661455659)
XLA Ops:
  6.5 0.7 copy.108
  7.3 41.6 %all_gather.6 = bf16[2,8,8192]{2,0,1:T(2,128)(2,1)} all-gather(bf16[2,8,256]{2,0,1:T(2,128)(2,1)S(1)} %copy.108), channel_id=1, replica_groups=mesh['inst'=8,'tp'=32] {'tp'}, dimensions={2}, use_global_device_ids=true | all-gather | bytes 270336 | tf_op jit(solution)/shard_map/all_gather | solution.py:47
  48.9 0.0 reduce-scatter.5.cloned.1.call-start
  48.9 0.7 iota_compare_fusion
  49.7 0.1 copy.114
  49.8 3.5 copy.143
  53.3 1.1 copy.144
  54.4 0.1 iota_compare_fusion.1
  54.5 2.2 bitcast_bitcast_fusion.1
  56.7 2.3 bitcast_bitcast_fusion
  59.0 25.6 %all-gather.2.cloned.1.call-done = bf16[2,64,8192]{2,0,1:T(2,128)(2,1)} async-done(((bf16[2,8,8192]{2,0,1:T(2,128)(2,1)}), bf16[2,64,8192]{2,0,1:T(2,128)(2,1)}) %all-gather.2.cloned.1.call-update) | async-done | bytes 2097168 | tf_op jit(solution)/shard_map/all_gather | solution.py:48
  84.6 3.2 gather_fusion
  87.8 0.4 reshape.106
  88.2 4.6 %fusion.36 = (f32[2,16,8,8]{3,0,2,1:T(2,128)S(1)}, f32[2,16,8,8,128]{4,3,0,2,1:T(8,128)S(1)}) fusion(bf16[16,128,8,128,1]{3,2,1,0,4:T(8,128)(2,1)} %bitcast_bitcast_fusion.1, bf16[2,16,8,8,128]{4,3,2,0,1:T(8,128)(2,1)S(1)} %reshape.106, pred[16,128]{1,0:T(8,128)(4,1)S(1)} %iota_compare_fusion.1), kind=kOutput, calls=%fused_computation.64 | convolution fusion | flops 67893248 | bytes 5777408 | tf_op jit(solution)/shard_map/sbgqd,btgd->sbgqt/dot_general | solution.py:56
  92.8 0.1 copy.113
  93.0 0.1 copy.119
  93.0 0.3 select_reduce_fusion
  93.4 0.1 copy.116
  93.5 76.9 %pmax.7 = bf16[2,64,64]{1,2,0:T(8,128)(2,1)S(1)} all-reduce(bf16[2,64,64]{1,2,0:T(8,128)(2,1)S(1)} %copy.116), channel_id=1, replica_groups=mesh['inst'=8,'tp'=32] {'inst','tp'}, use_global_device_ids=true, to_apply=%region_2.3 | all-reduce | flops 8192 | bytes 32768 | tf_op jit(solution)/shard_map/pmax | solution.py:74
  170.4 0.1 copy.117
  170.5 0.6 gather_fusion.1
  171.1 3.4 fusion.13
  174.5 0.3 bitcast_multiply_fusion
  174.9 2.1 convolution_bitcast_fusion
  177.0 2.3 copy.178
  179.4 0.6 copy-done.6
  180.0 0.6 dynamic-slice.2
  180.6 0.6 dynamic-slice
  181.3 0.6 gather_fusion.3
  181.8 1.3 gather_fusion.2
  183.2 0.1 select_bitcast_fusion
  183.3 0.2 fusion.35
  183.4 0.1 copy.124
  184.8 0.1 dynamic-slice_maximum_fusion
  184.9 0.1 copy.125
  185.0 0.1 copy.126
  185.1 0.8 fusion.19
  185.9 0.1 copy.128
  186.1 0.1 copy.129
  186.1 0.3 convolution_bitcast_fusion.1
  186.4 113.2 %all-reduce = f32[2,64,64]{1,2,0:T(8,128)S(1)} all-reduce(f32[2,64,64]{1,2,0:T(8,128)S(1)} %convolution_bitcast_fusion.1), channel_id=4, replica_groups=mesh['inst'=8,'tp'=32] {'tp'}, use_global_device_ids=true, to_apply=%region_8.10.clone | all-reduce | flops 8192 | bytes 65536
  299.6 0.1 multiply_reduce_fusion
  299.7 92.3 %reduce-scatter.5.cloned.1.call-done = f32[2,64,256]{2,1,0:T(8,128)} async-done(((f32[2,64,8192]{2,1,0:T(8,128)}), f32[2,64,256]{2,1,0:T(8,128)}) %reduce-scatter.5.cloned.1.call-update) | async-done | bytes 131088 | tf_op jit(solution)/shard_map/reduce_scatter | solution.py:83
  392.0 0.1 copy.130
  392.1 17.6 %all-reduce.1 = f32[2,64,2]{1,2,0:T(2,128)S(1)} all-reduce(f32[2,64,2]{1,2,0:T(2,128)S(1)} %constant_dynamic-slice_fusion), channel_id=5, replica_groups=mesh['inst'=8,'tp'=32] {'inst'}, use_global_device_ids=true, to_apply=%region_9.11.clone | all-reduce | flops 256 | bytes 2048
  409.7 0.1 fusion.33
  409.8 18.8 %reduce-scatter.7.cloned.1.call-done = f32[2,8,256]{2,1,0:T(8,128)} async-done(((f32[2,64,256]{2,1,0:T(8,128)}), f32[2,8,256]{2,1,0:T(8,128)}) %reduce-scatter.7.cloned.1.call-update) | async-done | bytes 16400 | tf_op jit(solution)/shard_map/reduce_scatter | solution.py:87
  428.5 1.4 fusion.24
  (28 shorter events, 0.3 us)
Async XLA Ops:
  6.5 174.7 %copy-start = (bf16[2,8,1024]{2,1,0:T(8,128)(2,1)S(1)}, bf16[2,8,1024]{2,1,0:T(8,128)(2,1)}, u32[]{:S(2)}) copy-start(bf16[2,8,1024]{2,1,0:T(8,128)(2,1)} %param.11) | copy-start | bytes 98308
  6.5 78.1 %all-gather.2.cloned.1.call-start = ((), (), s32[]{:S(2)}) async-start(), calls=%async_computation.2 | async-start | bytes 2359296 | tf_op jit(solution)/shard_map/all_gather | solution.py:48
  48.9 343.1 %reduce-scatter.5.cloned.1.call-start = ((), (), s32[]{:S(2)}) async-start(), calls=%async_computation.3 | async-start | bytes 4325376 | tf_op jit(solution)/shard_map/reduce_scatter | solution.py:83
  49.8 3.5 copy-start.1
  53.3 1.1 copy-start.3
  53.3 1.1 copy-start.4
  179.4 0.7 copy-start.6
  179.4 1.3 copy-start.5
  179.4 3.9 copy-start.2
  179.4 249.1 %reduce-scatter.7.cloned.1.call-start = ((), (), s32[]{:S(2)}) async-start(), calls=%async_computation.4 | async-start | bytes 147456 | tf_op jit(solution)/shard_map/reduce_scatter | solution.py:87
Sparse Core Ops, SparseCore 0:
  49.0 35.5 all-gather.1
  179.5 212.3 reduce-scatter.4
  394.6 33.8 reduce-scatter.6
where the time goes:
time: 438 us; the launch traced here: 436 us
  blocking collectives  249 us (57%)
  waiting for transfers between devices  137 us (31%)
  local copies, waits for them, and re-layouts  21.1 us (5%)
  between operations  14.6 us (3%)
  matrix products  10.6 us (2%)
    unnamed x2, blocking collectives  131 us
    reduce_scatter x1, waiting for transfers between devices, body(): lax.psum_scatter(numerators, 'tp', scatter_dimension=2, tiled=True)  92.3 us
    pmax x1, blocking collectives, body(): lax.pmax(local_peak.astype(jnp.bfloat16), ('inst', 'tp'))  76.9 us
    all_gather x1, blocking collectives, body(): q_group = lax.all_gather(queries, 'tp', axis=2, tiled=True)  41.6 us
    all_gather x1, waiting for transfers between devices, body(): q_every = lax.all_gather(q_group, 'inst', axis=1, tiled=True)  25.6 us
    reduce_scatter x1, waiting for transfers between devices, body(): lax.psum_scatter(numer_heads, 'inst', scatter_dimension=1, tiled=True)  18.8 us
  transfers between devices with their start and end apart: 3, of which 3 were waited for; matrix products, arithmetic and copies ran while one was open for 4% of the time, Pallas kernels for 0%

commit v1 on v0

v1 whole, which is shorter than its diff:
```python
import jax
import jax.numpy as jnp
from jax import lax
from jax.experimental import pallas as pl
from jax.experimental.pallas import tpu as pltpu
from jax.sharding import Mesh, PartitionSpec as P

H = 64
KVH = 8
DH = 128
BLK = 128
SCALE = DH ** (-0.5)

far_below = -1e30


def split_three(x):
    hi = x.astype(jnp.bfloat16)
    rest = x - hi.astype(jnp.float32)
    mid = rest.astype(jnp.bfloat16)
    lo = (rest - mid.astype(jnp.float32)).astype(jnp.bfloat16)
    return hi, mid, lo


def lay_kernel(here, *refs):
    pieces, out_ref, ordered = refs[:-2], refs[-2], refs[-1]
    for m, piece in enumerate(pieces):
        ordered[here[0] ^ m] = piece[...]
    for z in range(out_ref.shape[0]):
        out_ref[z] = jnp.concatenate([ordered[x, z] for x in range(len(pieces))], axis=1)


def lay(here, pieces):
    n_z, rows, depth, width = pieces[0].shape
    return pl.pallas_call(
        lay_kernel,
        out_shape=jax.ShapeDtypeStruct((n_z, rows, len(pieces) * depth, width), pieces[0].dtype),
        in_specs=[pl.BlockSpec(memory_space=pltpu.SMEM)]
        + [pl.BlockSpec(memory_space=pltpu.VMEM)] * len(pieces),
        out_specs=pl.BlockSpec(memory_space=pltpu.VMEM),
        scratch_shapes=[pltpu.VMEM((len(pieces), n_z, rows, depth, width), pieces[0].dtype)],
        name="lay",
    )(here, *pieces)


def block_kernel(here, owner, fill, k_hbm, v_hbm, *refs):
    pieces = refs[:-6]
    out_ref, k_all, v_all, picked, stats, sem = refs[-6:]
    slots, n_kv, per, _ = picked.shape
    cols = n_kv * per
    n_tp = out_ref.shape[0]
    together = 8
    rows = pieces[0].shape[1]
    n_core = 2
    n_y = len(pieces) // n_core

    def fetch(b):
        home = owner[b] // rows
        row = lax.rem(owner[b], rows)
        which = (home // n_core ^ here[0]) + (lax.rem(home, n_core) ^ here[1]) * n_y
        for p, piece in enumerate(pieces):

            @pl.when(which == p)
            def _(piece=piece):
                pltpu.make_async_copy(piece.at[:, row], picked.at[b], sem.at[2, b]).start()

    def copies(b):
        return (
            pltpu.make_async_copy(k_hbm.at[b], k_all.at[b], sem.at[0, b]),
            pltpu.make_async_copy(v_hbm.at[b], v_all.at[b], sem.at[1, b]),
        )

    def start(b, _):
        fetch(b)
        for c in copies(b):
            c.start()
        return 0

    lax.fori_loop(0, slots, start, 0)
    stats[...] = jnp.zeros_like(stats)
    slot_at = lax.broadcasted_iota(jnp.int32, (BLK, cols), 0)
    nothing = jnp.zeros((per, DH), jnp.bfloat16)

    def score(b):
        spread = []
        for g in range(n_kv):
            mine = picked[b, g]
            spread.append(
                jnp.concatenate([nothing] * g + [mine] + [nothing] * (n_kv - 1 - g), axis=1)
            )
        scores = lax.dot_general(
            k_all[b],
            jnp.concatenate(spread, axis=0),
            (((1,), (1,)), ((), ())),
            preferred_element_type=jnp.float32,
        )
        return jnp.where(slot_at < fill[b], scores * SCALE, far_below)

    def soften(b, scores):
        peak = jnp.max(scores, axis=0, keepdims=True)
        chances = jnp.exp(scores - peak)
        total = jnp.sum(chances, axis=0, keepdims=True)
        for p, piece in enumerate(split_three(peak) + split_three(total)):
            stats[pl.ds(p * slots + b, 1)] = piece.astype(jnp.float32)
        stats[pl.ds(6 * slots + b, 1)] = jnp.broadcast_to(owner[b].astype(jnp.float32), (1, cols))
        return chances.astype(jnp.bfloat16).T

    def mix(b, rounded):
        mixed = []
        for g in range(n_kv):
            mixed.append(
                jnp.dot(
                    rounded[g * per : (g + 1) * per],
                    v_all[b, :, g * DH : (g + 1) * DH],
                    preferred_element_type=jnp.float32,
                ).astype(jnp.bfloat16)
            )
        mixed = jnp.concatenate(mixed, axis=0)
        out_ref[:, pl.ds(b, 1)] = mixed.reshape(n_tp, 1, cols // n_tp, DH)

    def some_blocks(i, _):
        first = i * together
        for j in range(together):
            for c in copies(first + j):
                c.wait()
            pltpu.make_async_copy(pieces[0].at[:, 0], picked.at[first + j], sem.at[2, first + j]).wait()
        scores = [score(first + j) for j in range(together)]
        rounded = [soften(first + j, scores[j]) for j in range(together)]
        for j in range(together):
            mix(first + j, rounded[j])
        return 0

    lax.fori_loop(0, slots // together, some_blocks, 0)
    packed = stats[...].T.astype(jnp.bfloat16)
    out_ref[:, pl.ds(slots, 1)] = packed.reshape(n_tp, 1, cols // n_tp, DH)


def blocks(here, pieces, k_cache, v_cache, block_req, block_fill, n_tp):
    slots = k_cache.shape[0]
    n_kv, _, per, _ = pieces[0].shape
    cols = n_kv * per
    return pl.pallas_call(
        block_kernel,
        out_shape=jax.ShapeDtypeStruct((n_tp, slots + 1, cols // n_tp, DH), jnp.bfloat16),
        in_specs=[pl.BlockSpec(memory_space=pltpu.SMEM)] * 3
        + [pl.BlockSpec(memory_space=pl.ANY)] * (2 + len(pieces)),
        out_specs=pl.BlockSpec(memory_space=pltpu.VMEM),
        scratch_shapes=[
            pltpu.VMEM(k_cache.shape, k_cache.dtype),
            pltpu.VMEM(v_cache.shape, v_cache.dtype),
            pltpu.VMEM((slots, n_kv, per, DH), pieces[0].dtype),
            pltpu.VMEM((DH, cols), jnp.float32),
            pltpu.SemaphoreType.DMA((3, slots)),
        ],
        compiler_params=pltpu.CompilerParams(vmem_limit_bytes=56 * 1024 * 1024),
        cost_estimate=pl.CostEstimate(
            flops=4 * slots * BLK * DH * 128, bytes_accessed=9 * 1024 * 1024, transcendentals=slots * BLK * 128
        ),
        name="blocks",
    )(here, block_req, block_fill, k_cache, v_cache, *pieces)


def combine(got, requests):
    n_src = got.shape[0]
    slots = got.shape[1] - 1
    n_cols = got.shape[2]
    out = got[:, :slots].reshape(n_src * slots, n_cols, DH)
    stats = got[:, slots, :, : 7 * slots].astype(jnp.float32)
    stats = stats.reshape(n_src, n_cols, 7, slots).transpose(2, 1, 0, 3)
    stats = stats.reshape(7, n_cols, n_src * slots)
    peak = stats[0] + stats[1] + stats[2]
    total = stats[3] + stats[4] + stats[5]
    owner = stats[6, 0].astype(jnp.int32)
    hot = owner[None, :] == jnp.arange(requests, dtype=jnp.int32)[:, None]
    masked = jnp.where(hot[None], peak[:, None, :], far_below)
    top = jnp.max(masked, axis=-1, keepdims=True)
    weight = jnp.where(hot[None], jnp.exp(masked - top), 0.0)
    den = jnp.sum(weight * total[:, None], axis=-1, keepdims=True)
    w_hi = lax.reduce_precision(weight, 8, 7)
    w_lo = (weight - w_hi).astype(jnp.bfloat16)
    w_hi = w_hi.astype(jnp.bfloat16)
    num = jnp.einsum("crj,jcd->crd", w_hi, out, preferred_element_type=jnp.float32) + jnp.einsum(
        "crj,jcd->crd", w_lo, out, preferred_element_type=jnp.float32
    )
    some = den > 0.0
    safe = jnp.where(some, den, 1.0)
    return num / safe, jnp.where(some, top + jnp.log(safe), far_below)


def fresh_kernel(q_ref, keys_ref, values_ref, out_ref):
    n_steps, own_rows, width = q_ref.shape
    n_heads = width // DH
    lane = lax.broadcasted_iota(jnp.int32, (own_rows, DH), 1)
    levels = jnp.zeros((own_rows, DH), jnp.float32)
    for s in range(n_steps):
        for h in range(n_heads):
            c = s * n_heads + h
            query = q_ref[s, :, h * DH : (h + 1) * DH].astype(jnp.float32)
            fresh = [
                jnp.sum(query * keys_ref[j].astype(jnp.float32), axis=1, keepdims=True) * SCALE
                for j in range(s + 1)
            ]
            top = fresh[0]
            for x in fresh[1:]:
                top = jnp.maximum(top, x)
            num = jnp.zeros((own_rows, DH), jnp.float32)
            den = jnp.zeros((own_rows, 1), jnp.float32)
            for j in range(s + 1):
                weight = jnp.exp(fresh[j] - top)
                num = num + weight * values_ref[j].astype(jnp.float32)
                den = den + weight
            out_ref[c] = num / den
            levels = jnp.where(lane == c, top + jnp.log(den), levels)
    out_ref[n_steps * n_heads] = levels


def fresh_part(queries, keys, values):
    n_steps, own_rows, width = queries.shape
    return pl.pallas_call(
        fresh_kernel,
        out_shape=jax.ShapeDtypeStruct((n_steps * (width // DH) + 1, own_rows, DH), jnp.float32),
        in_specs=[pl.BlockSpec(memory_space=pltpu.VMEM)] * 3,
        out_specs=pl.BlockSpec(memory_space=pltpu.VMEM),
        cost_estimate=pl.CostEstimate(flops=1 << 17, bytes_accessed=1 << 16, transcendentals=1 << 8),
        name="fresh",
    )(queries, keys, values)


def finish_kernel(got, fresh, out_ref):
    n_steps, own_rows, width = out_ref.shape
    n_heads = width // DH
    last = n_steps * n_heads
    parts = [got.at[i] for i in range(got.shape[0])] + [fresh]
    levels = [part[last] for part in parts]
    top = levels[0]
    for x in levels[1:]:
        top = jnp.maximum(top, x)
    weights = [jnp.exp(x - top) for x in levels]
    den = weights[0]
    for x in weights[1:]:
        den = den + x
    inverse = 1.0 / den
    weights = [x * inverse for x in weights]
    for s in range(n_steps):
        for h in range(n_heads):
            c = s * n_heads + h
            num = jnp.zeros((own_rows, DH), jnp.float32)
            for weight, part in zip(weights, parts):
                num = num + weight[:, c : c + 1] * part[c]
            out_ref[s, :, h * DH : (h + 1) * DH] = num.astype(out_ref.dtype)


def finish(got, fresh, n_steps):
    own_rows = got.shape[2]
    width = (got.shape[1] - 1) // n_steps * DH
    return pl.pallas_call(
        finish_kernel,
        out_shape=jax.ShapeDtypeStruct((n_steps, own_rows, width), jnp.bfloat16),
        in_specs=[pl.BlockSpec(memory_space=pltpu.VMEM)] * 2,
        out_specs=pl.BlockSpec(memory_space=pltpu.VMEM),
        name="finish",
    )(got, fresh)


def body(queries, new_keys, new_values, k_cache, v_cache, block_req, block_fill):
    n_steps, own_rows, width = queries.shape
    own_heads = width // DH
    n_y, n_core = lax.axis_size("y"), lax.axis_size("core")
    n_z, n_x = lax.axis_size("z"), lax.axis_size("x")
    n_inst = n_y * n_core

    def from_other(value, axis, m):
        return lax.ppermute(value, axis, [(j, j ^ m) for j in range(lax.axis_size(axis))])

    rows = queries.reshape(n_steps, own_rows, own_heads, DH).transpose(1, 0, 2, 3)
    rows = rows.reshape(own_rows, n_steps * own_heads, DH)
    rows = lax.all_to_all(
        jnp.broadcast_to(rows[None], (n_z,) + rows.shape), "z", 0, 0, tiled=True
    )
    at_x = lax.axis_index("x").astype(jnp.int32).reshape(1)
    own = lay(at_x, [rows] + [from_other(rows, "x", m) for m in range(1, n_x)])
    at_kv = lax.axis_index("z") * DH
    keys = lax.dynamic_slice_in_dim(new_keys, at_kv, DH, axis=2)
    values = lax.dynamic_slice_in_dim(new_values, at_kv, DH, axis=2)
    own, keys, values = lax.optimization_barrier((own, keys, values))
    pieces = [own] + [from_other(own, "y", m) for m in range(1, n_y)]
    pieces = pieces + [from_other(p, "core", 1) for p in pieces]
    here = jnp.stack([lax.axis_index("y"), lax.axis_index("core")]).astype(jnp.int32)
    sent = blocks(here, pieces, k_cache, v_cache, block_req, block_fill, n_z * n_x)
    sent, keys, values = lax.optimization_barrier((sent, keys, values))
    got = lax.all_to_all(sent, ("z", "x"), split_axis=0, concat_axis=0, tiled=True)
    got, fresh = lax.optimization_barrier((got, fresh_part(queries, keys, values)))
    part, level = combine(got, n_inst * own_rows)
    level = level[..., 0].reshape(4, n_inst, own_rows).transpose(1, 2, 0)
    level = jnp.pad(level, ((0, 0), (0, 0), (0, DH - 4)))[:, None]
    part = part.reshape(4, n_inst, own_rows, DH).transpose(1, 0, 2, 3)
    both = lax.all_to_all(
        jnp.concatenate([part, level], axis=1), ("y", "core"), 0, 0, tiled=True
    )
    return finish(both, fresh, n_steps)


def solution(mesh):
    n_inst, n_tp = mesh.devices.shape
    split = Mesh(
        mesh.devices.reshape(n_inst // 2, 2, KVH, n_tp // KVH), ("y", "core", "z", "x")
    )
    inst, tp = ("y", "core"), ("z", "x")
    return jax.shard_map(
        body,
        mesh=split,
        in_specs=(
            P(None, inst, tp),
            P(None, inst, None),
            P(None, inst, None),
            P(inst + tp, None, None),
            P(inst + tp, None, None),
            P(inst + tp),
            P(inst + tp),
        ),
        out_specs=P(None, inst, tp),
        check_vma=False,
    )
```

time: 438 us -> 90.6 us (0.21)
  blocking collectives: 249 us -> 11.8 us
  waiting for transfers between devices: 137 us -> 32.3 us
  starting transfers between devices: 0.09 us -> 26.6 us
  local copies, waits for them, and re-layouts: 21.1 us -> 5.7 us
  between operations: 14.6 us -> 0.17 us
  Pallas kernels: 0 us -> 11.7 us
  matrix products: 10.6 us -> 0.65 us
    unnamed x2 -> x0, blocking collectives: 131 us -> none
    reduce_scatter x2 -> x0, waiting for transfers between devices: 111 us -> none  [the longest x1 92.3 us: body(): lax.psum_scatter(numerators, 'tp', scatter_dimension=2, tiled=True)]
    pmax x1 -> x0, blocking collectives: 76.9 us -> none  [body(): lax.pmax(local_peak.astype(jnp.bfloat16), ('inst', 'tp'))]
    all_gather x1 -> x0, blocking collectives: 41.6 us -> none  [body(): q_group = lax.all_gather(queries, 'tp', axis=2, tiled=True)]
    all_gather x1 -> x0, waiting for transfers between devices: 25.6 us -> none  [body(): q_every = lax.all_gather(q_group, 'inst', axis=1, tiled=True)]
    all_to_all x0 -> x2, waiting for transfers between devices: none -> 23.1 us  [the longest x1 15.9 us: body(): lax.all_to_all(sent, ('z', 'x'), split_axis=0, concat_axis=0, tiled=True)]
    ppermute x0 -> x10, starting transfers between devices: none -> 13.7 us  [from_other(): lax.ppermute(value, axis, [(j, j ^ m) for j in range(lax.axis_size(axis))])]
    all_to_all x0 -> x2, starting transfers between devices: none -> 12.9 us  [the longest x1 9.01 us: body(): lax.all_to_all(jnp.broadcast_to(rows[None], (n_z,) + rows.shape), 'z', 0,...]
  transfers between devices with their start and end apart: 3 -> 12, of which waited for: 3 -> 6; matrix products, arithmetic and copies ran while one was open for 4% -> 2% of each run, Pallas kernels for 0% -> 2%
where the time goes in v1:
time: 90.6 us; the launch traced here: 90.1 us
  waiting for transfers between devices  32.3 us (36%)
  starting transfers between devices  26.6 us (29%)
  blocking collectives  11.8 us (13%)
  Pallas kernels  11.7 us (13%)
  local copies, waits for them, and re-layouts  5.7 us (6%)
  other arithmetic  1.08 us (1%)
    all_to_all x1, waiting for transfers between devices, body(): lax.all_to_all(sent, ('z', 'x'), split_axis=0, concat_axis=0, tiled=True)  15.9 us
    ppermute x10, starting transfers between devices, from_other(): lax.ppermute(value, axis, [(j, j ^ m) for j in range(lax.axis_size(axis))])  13.7 us
    all_to_all x1, blocking collectives, body(): lax.all_to_all(jnp.concatenate([part, level], axis=1), ('y', 'core'), 0,...  11.8 us
    ppermute x10, waiting for transfers between devices, from_other(): lax.ppermute(value, axis, [(j, j ^ m) for j in range(lax.axis_size(axis))])  9.21 us
    all_to_all x1, starting transfers between devices, body(): lax.all_to_all(jnp.broadcast_to(rows[None], (n_z,) + rows.shape), 'z', 0,...  9.01 us
    all_to_all x1, waiting for transfers between devices, body(): lax.all_to_all(jnp.broadcast_to(rows[None], (n_z,) + rows.shape), 'z', 0,...  7.24 us
    pallas_call x1, Pallas kernels, blocks(): pl.pallas_call(block_kernel, out_shape=jax.ShapeDtypeStruct((n_tp, slots...  6.92 us
    all_to_all x1, starting transfers between devices, body(): lax.all_to_all(sent, ('z', 'x'), split_axis=0, concat_axis=0, tiled=True)  3.9 us
  transfers between devices with their start and end apart: 12, of which 6 were waited for; matrix products, arithmetic and copies ran while one was open for 2% of the time, Pallas kernels for 2%

profile of v1, /device:TPU:1, one launch (start us, length us, event | category | flops | bytes accessed | tf_op | source)
XLA Modules:
  0.0 90.1 jit_solution(2409059666260521729)
XLA Ops:
  0.0 0.7 copy.33
  0.7 0.6 broadcast_in_dim.58
  1.3 9.0 %all-to-all-start = ((bf16[8,8,4,128]{3,2,1,0:T(4,128)(2,1)}), bf16[8,8,4,128]{3,2,1,0:T(4,128)(2,1)S(1)}, u32[]{:S(2)}, u32[]{:S(2)}) async-start(bf16[8,8,4,128]{3,2,1,0:T(4,128)(2,1)} %broadcast_in_dim.58), calls=%async_computation | async-start | bytes 131072 | tf_op jit(solution)/shard_map/all_to_all | solution.py:277
  10.4 7.2 %all-to-all-done.refs_0_ = bf16[8,8,4,128]{3,2,1,0:T(4,128)(2,1)S(1)} async-done(((bf16[8,8,4,128]{3,2,1,0:T(4,128)(2,1)}), bf16[8,8,4,128]{3,2,1,0:T(4,128)(2,1)S(1)}, u32[]{:S(2)}, u32[]{:S(2)}) %all-to-all-start) | async-done | bytes 65568 | tf_op jit(solution)/shard_map/all_to_all | solution.py:277
  17.6 2.5 %collective-permute-start.2 = (bf16[8,8,4,128]{3,2,1,0:T(4,128)(2,1)S(1)}, bf16[8,8,4,128]{3,2,1,0:T(4,128)(2,1)S(1)}, u32[]{:S(2)}, u32[]{:S(2)}) collective-permute-start(bf16[8,8,4,128]{3,2,1,0:T(4,128)(2,1)S(1)} %all-to-all-done.refs_0_), channel_id=1, source_target_pairs={{0,3},{1,2},{2,1},{3,0},{4,7},{5,6},{6,5},{7,4},{8,11},{9,10},{10,... | collective-permute-start | bytes 196616 | tf_op jit(solution)/shard_map/ppermute | solution.py:273
  20.1 0.5 collective-permute-start.1
  20.6 0.3 collective-permute-start
  20.9 1.3 %constant_dynamic-slice_fusion = (bf16[2,8,128]{2,1,0:T(8,128)(2,1)}, bf16[2,8,128]{2,1,0:T(8,128)(2,1)}) fusion(bf16[2,8,1024]{2,1,0:T(8,128)(2,1)} %param.9, s32[]{:T(128)S(6)} %select_n.31, bf16[2,8,1024]{2,1,0:T(8,128)(2,1)} %param.8), kind=kLoop, calls=%fused_computation.42 | loop fusion | bytes 16388 | tf_op jit(solution)/shard_map/dynamic_slice | solution.py:284
  22.2 0.0 collective-permute-done.2.refs_3_
  22.2 2.6 %collective-permute-done.1.refs_2_ = bf16[8,8,4,128]{3,2,1,0:T(4,128)(2,1)S(1)} collective-permute-done((bf16[8,8,4,128]{3,2,1,0:T(4,128)(2,1)S(1)}, bf16[8,8,4,128]{3,2,1,0:T(4,128)(2,1)S(1)}, u32[]{:S(2)}, u32[]{:S(2)}) %collective-permute-start.1) | collective-permute-done | bytes 65568 | tf_op jit(solution)/shard_map/ppermute | solution.py:273
  24.8 0.6 copy-done.9
  25.4 0.0 copy-done.10
  25.4 1.8 %lay.1.refs_0_ = bf16[8,8,16,128]{3,2,1,0:T(8,128)(2,1)} custom-call(s32[1]{0:T(128)} %bitcast.2.here, bf16[8,8,4,128]{3,2,1,0:T(4,128)(2,1)} %copy-done.7, bf16[8,8,4,128]{3,2,1,0:T(4,128)(2,1)} %copy-done.10, bf16[8,8,4,128]{3,2,1,0:T(4,128)(2,1)} %copy-done.9, bf16[8,8,4,128]{3,2,1,0:T(4,128)(2,1)} %copy-done.8), custom_call_target="tpu_custom_call" | custom-call | tf_op jit(solution)/shard_map/lay/pallas_call | solution.py:35
  27.2 2.7 %collective-permute-start.5 = (bf16[8,8,16,128]{3,2,1,0:T(8,128)(2,1)}, bf16[8,8,16,128]{3,2,1,0:T(8,128)(2,1)S(1)}, u32[]{:S(2)}, u32[]{:S(2)}) collective-permute-start(bf16[8,8,16,128]{3,2,1,0:T(8,128)(2,1)} %lay.1.refs_0_), channel_id=1, source_target_pairs={{0,192},{64,128},{128,64},{192,0},{1,193},{65,129},{129,65},{193,1... | collective-permute-start | bytes 786440 | tf_op jit(solution)/shard_map/ppermute | solution.py:273
  29.9 0.3 collective-permute-start.4
  30.3 0.2 collective-permute-start.3
  30.5 4.2 %collective-permute-start.6 = (bf16[8,8,16,128]{3,2,1,0:T(8,128)(2,1)}, bf16[8,8,16,128]{3,2,1,0:T(8,128)(2,1)S(1)}, u32[]{:S(2)}, u32[]{:S(2)}) collective-permute-start(bf16[8,8,16,128]{3,2,1,0:T(8,128)(2,1)} %lay.1.refs_0_), channel_id=1, source_target_pairs={{0,32},{32,0},{1,33},{33,1},{2,34},{34,2},{3,35},{35,3},{4,36},{36... | collective-permute-start | bytes 786440 | tf_op jit(solution)/shard_map/ppermute | solution.py:273
  34.7 6.0 %collective-permute-done.5.refs_3_ = bf16[8,8,16,128]{3,2,1,0:T(8,128)(2,1)S(1)} collective-permute-done((bf16[8,8,16,128]{3,2,1,0:T(8,128)(2,1)}, bf16[8,8,16,128]{3,2,1,0:T(8,128)(2,1)S(1)}, u32[]{:S(2)}, u32[]{:S(2)}) %collective-permute-start.5) | collective-permute-done | bytes 262176 | tf_op jit(solution)/shard_map/ppermute | solution.py:273
  40.7 1.7 %collective-permute-start.9 = (bf16[8,8,16,128]{3,2,1,0:T(8,128)(2,1)S(1)}, bf16[8,8,16,128]{3,2,1,0:T(8,128)(2,1)S(1)}, u32[]{:S(2)}, u32[]{:S(2)}) collective-permute-start(bf16[8,8,16,128]{3,2,1,0:T(8,128)(2,1)S(1)} %collective-permute-done.5.refs_3_), channel_id=1, source_target_pairs={{0,32},{32,0},{1,33},{33,1},{2,34},{34,2},{3,35},{35,3},{4,36},{36... | collective-permute-start | bytes 786440 | tf_op jit(solution)/shard_map/ppermute | solution.py:273
  42.4 0.8 collective-permute-start.8
  43.2 0.5 collective-permute-start.7
  43.7 0.6 pad_add_fusion.here
  44.3 0.1 collective-permute-done.8.refs_6_
  44.4 0.5 collective-permute-done.7.refs_5_
  44.9 0.1 copy-done.3
  45.0 0.1 copy-done.4
  45.1 0.1 copy-done.5
  45.2 0.7 copy-done.6
  45.9 6.9 %blocks.1 = bf16[32,17,4,128]{3,2,1,0:T(4,128)(2,1)} custom-call(s32[2]{0:T(128)} %pad_add_fusion.here, s32[16]{0:T(128)} %owner.1, s32[16]{0:T(128)} %fill.1, bf16[16,128,1024]{2,1,0:T(8,128)(2,1)} %k_hbm.1, bf16[16,128,1024]{2,1,0:T(8,128)(2,1)} %v_hbm.1, bf16[8,8,16,128]{3,2,1,0:T(8,128)(2,1)} %lay.1.refs_0_, bf16[8,8,16,128]{3,2,1,0:T(8,128)(2,1)} %copy-done.2, ...), custom_call_target="tpu_custom_call" | custom-call | flops 134217728 | bytes 9437184 | tf_op jit(solution)/shard_map/blocks/pallas_call | solution.py:142
  52.8 3.9 %all-to-all-start.1 = ((bf16[32,17,4,128]{3,2,1,0:T(4,128)(2,1)}), bf16[32,17,4,128]{3,2,1,0:T(4,128)(2,1)S(1)}, u32[]{:S(2)}, u32[]{:S(2)}) async-start(bf16[32,17,4,128]{3,2,1,0:T(4,128)(2,1)} %blocks.1), calls=%async_computation.1 | async-start | bytes 1114112 | tf_op jit(solution)/shard_map/all_to_all | solution.py:291
  56.7 1.4 %fresh.1 = f32[5,8,128]{2,1,0:T(8,128)} custom-call(bf16[2,8,256]{2,1,0:T(8,128)(2,1)} %q_ref.1, bf16[2,8,128]{2,1,0:T(8,128)(2,1)} %get-tuple-element.17.keys_ref, bf16[2,8,128]{2,1,0:T(8,128)(2,1)} %get-tuple-element.18.values_ref), custom_call_target="tpu_custom_call" | custom-call | flops 131072 | bytes 65536 | tf_op jit(solution)/shard_map/fresh/pallas_call | solution.py:219
  58.1 15.9 %all-to-all-done.1 = bf16[32,17,4,128]{3,2,1,0:T(4,128)(2,1)S(1)} async-done(((bf16[32,17,4,128]{3,2,1,0:T(4,128)(2,1)}), bf16[32,17,4,128]{3,2,1,0:T(4,128)(2,1)S(1)}, u32[]{:S(2)}, u32[]{:S(2)}) %all-to-all-start.1) | async-done | bytes 557088 | tf_op jit(solution)/shard_map/all_to_all | solution.py:291
  74.0 0.3 slice.38
  74.3 0.1 copy.34
  74.4 0.2 copy.35
  74.6 0.1 copy.39
  74.7 0.1 add.58
  74.8 0.1 copy.36
  74.9 0.1 add.54
  75.0 0.3 reshape.106
  75.3 0.1 select_reduce_fusion
  75.4 0.3 fusion.5
  75.7 0.1 copy.41
  75.8 0.1 copy.42
  76.0 0.3 fusion.8
  76.3 0.3 fusion.1
  76.7 11.8 %all_to_all.15.got = f32[8,5,8,128]{3,2,1,0:T(8,128)} all-to-all(f32[8,5,8,128]{3,2,1,0:T(8,128)S(1)} %pad_maximum_fusion), channel_id=1, replica_groups=mesh['y'=4,'core'=2,'z'=8,'x'=4] {'y','core'}, dimensions={0} | all-to-all | bytes 327680 | tf_op jit(solution)/shard_map/all_to_all | solution.py:297
  88.4 1.7 %finish.1 = bf16[2,8,256]{2,1,0:T(8,128)(2,1)} custom-call(f32[8,5,8,128]{3,2,1,0:T(8,128)} %all_to_all.15.got, f32[5,8,128]{2,1,0:T(8,128)} %fresh.1), custom_call_target="tpu_custom_call" | custom-call | tf_op jit(solution)/shard_map/finish/pallas_call | solution.py:256
  (30 shorter events, 0.1 us)
Async XLA Ops:
  1.3 16.3 %all-to-all-start = ((bf16[8,8,4,128]{3,2,1,0:T(4,128)(2,1)}), bf16[8,8,4,128]{3,2,1,0:T(4,128)(2,1)S(1)}, u32[]{:S(2)}, u32[]{:S(2)}) async-start(bf16[8,8,4,128]{3,2,1,0:T(4,128)(2,1)} %broadcast_in_dim.58), calls=%async_computation | async-start | bytes 131072 | tf_op jit(solution)/shard_map/all_to_all | solution.py:277
  17.6 7.2 %copy-start.7 = (bf16[8,8,4,128]{3,2,1,0:T(4,128)(2,1)}, bf16[8,8,4,128]{3,2,1,0:T(4,128)(2,1)S(1)}, u32[]{:S(2)}) copy-start(bf16[8,8,4,128]{3,2,1,0:T(4,128)(2,1)S(1)} %all-to-all-done.refs_0_) | copy-start | bytes 196612
  17.6 4.6 %collective-permute-start.2 = (bf16[8,8,4,128]{3,2,1,0:T(4,128)(2,1)S(1)}, bf16[8,8,4,128]{3,2,1,0:T(4,128)(2,1)S(1)}, u32[]{:S(2)}, u32[]{:S(2)}) collective-permute-start(bf16[8,8,4,128]{3,2,1,0:T(4,128)(2,1)S(1)} %all-to-all-done.refs_0_), channel_id=1, source_target_pairs={{0,3},{1,2},{2,1},{3,0},{4,7},{5,6},{6,5},{7,4},{8,11},{9,10},{10,... | collective-permute-start | bytes 196616 | tf_op jit(solution)/shard_map/ppermute | solution.py:273
  20.1 4.7 %collective-permute-start.1 = (bf16[8,8,4,128]{3,2,1,0:T(4,128)(2,1)S(1)}, bf16[8,8,4,128]{3,2,1,0:T(4,128)(2,1)S(1)}, u32[]{:S(2)}, u32[]{:S(2)}) collective-permute-start(bf16[8,8,4,128]{3,2,1,0:T(4,128)(2,1)S(1)} %all-to-all-done.refs_0_), channel_id=1, source_target_pairs={{0,2},{1,3},{2,0},{3,1},{4,6},{5,7},{6,4},{7,5},{8,10},{9,11},{10,... | collective-permute-start | bytes 196616 | tf_op jit(solution)/shard_map/ppermute | solution.py:273
  20.6 4.2 %collective-permute-start = (bf16[8,8,4,128]{3,2,1,0:T(4,128)(2,1)S(1)}, bf16[8,8,4,128]{3,2,1,0:T(4,128)(2,1)S(1)}, u32[]{:S(2)}, u32[]{:S(2)}) collective-permute-start(bf16[8,8,4,128]{3,2,1,0:T(4,128)(2,1)S(1)} %all-to-all-done.refs_0_), channel_id=1, source_target_pairs={{0,1},{1,0},{2,3},{3,2},{4,5},{5,4},{6,7},{7,6},{8,9},{9,8},{10,11... | collective-permute-start | bytes 196616 | tf_op jit(solution)/shard_map/ppermute | solution.py:273
  22.2 2.7 %copy-start.8 = (bf16[8,8,4,128]{3,2,1,0:T(4,128)(2,1)}, bf16[8,8,4,128]{3,2,1,0:T(4,128)(2,1)S(1)}, u32[]{:S(2)}) copy-start(bf16[8,8,4,128]{3,2,1,0:T(4,128)(2,1)S(1)} %collective-permute-done.2.refs_3_) | copy-start | bytes 196612
  24.8 0.6 copy-start.9
  24.8 0.6 copy-start.10
  27.2 13.5 %collective-permute-start.5 = (bf16[8,8,16,128]{3,2,1,0:T(8,128)(2,1)}, bf16[8,8,16,128]{3,2,1,0:T(8,128)(2,1)S(1)}, u32[]{:S(2)}, u32[]{:S(2)}) collective-permute-start(bf16[8,8,16,128]{3,2,1,0:T(8,128)(2,1)} %lay.1.refs_0_), channel_id=1, source_target_pairs={{0,192},{64,128},{128,64},{192,0},{1,193},{65,129},{129,65},{193,1... | collective-permute-start | bytes 786440 | tf_op jit(solution)/shard_map/ppermute | solution.py:273
  29.9 12.5 %collective-permute-start.4 = (bf16[8,8,16,128]{3,2,1,0:T(8,128)(2,1)}, bf16[8,8,16,128]{3,2,1,0:T(8,128)(2,1)S(1)}, u32[]{:S(2)}, u32[]{:S(2)}) collective-permute-start(bf16[8,8,16,128]{3,2,1,0:T(8,128)(2,1)} %lay.1.refs_0_), channel_id=1, source_target_pairs={{0,128},{64,192},{128,0},{192,64},{1,129},{65,193},{129,1},{193,65... | collective-permute-start | bytes 786440 | tf_op jit(solution)/shard_map/ppermute | solution.py:273
  30.3 12.9 %collective-permute-start.3 = (bf16[8,8,16,128]{3,2,1,0:T(8,128)(2,1)}, bf16[8,8,16,128]{3,2,1,0:T(8,128)(2,1)S(1)}, u32[]{:S(2)}, u32[]{:S(2)}) collective-permute-start(bf16[8,8,16,128]{3,2,1,0:T(8,128)(2,1)} %lay.1.refs_0_), channel_id=1, source_target_pairs={{0,64},{64,0},{128,192},{192,128},{1,65},{65,1},{129,193},{193,129... | collective-permute-start | bytes 786440 | tf_op jit(solution)/shard_map/ppermute | solution.py:273
  30.5 13.8 %collective-permute-start.6 = (bf16[8,8,16,128]{3,2,1,0:T(8,128)(2,1)}, bf16[8,8,16,128]{3,2,1,0:T(8,128)(2,1)S(1)}, u32[]{:S(2)}, u32[]{:S(2)}) collective-permute-start(bf16[8,8,16,128]{3,2,1,0:T(8,128)(2,1)} %lay.1.refs_0_), channel_id=1, source_target_pairs={{0,32},{32,0},{1,33},{33,1},{2,34},{34,2},{3,35},{35,3},{4,36},{36... | collective-permute-start | bytes 786440 | tf_op jit(solution)/shard_map/ppermute | solution.py:273
  40.7 4.1 %copy-start = (bf16[8,8,16,128]{3,2,1,0:T(8,128)(2,1)}, bf16[8,8,16,128]{3,2,1,0:T(8,128)(2,1)S(1)}, u32[]{:S(2)}) copy-start(bf16[8,8,16,128]{3,2,1,0:T(8,128)(2,1)S(1)} %collective-permute-done.5.refs_3_) | copy-start | bytes 786436
  40.7 3.6 %collective-permute-start.9 = (bf16[8,8,16,128]{3,2,1,0:T(8,128)(2,1)S(1)}, bf16[8,8,16,128]{3,2,1,0:T(8,128)(2,1)S(1)}, u32[]{:S(2)}, u32[]{:S(2)}) collective-permute-start(bf16[8,8,16,128]{3,2,1,0:T(8,128)(2,1)S(1)} %collective-permute-done.5.refs_3_), channel_id=1, source_target_pairs={{0,32},{32,0},{1,33},{33,1},{2,34},{34,2},{3,35},{35,3},{4,36},{36... | collective-permute-start | bytes 786440 | tf_op jit(solution)/shard_map/ppermute | solution.py:273
  42.4 2.5 %copy-start.1 = (bf16[8,8,16,128]{3,2,1,0:T(8,128)(2,1)}, bf16[8,8,16,128]{3,2,1,0:T(8,128)(2,1)S(1)}, u32[]{:S(2)}) copy-start(bf16[8,8,16,128]{3,2,1,0:T(8,128)(2,1)S(1)} %collective-permute-done.4.refs_2_) | copy-start | bytes 786436
  42.4 2.0 %collective-permute-start.8 = (bf16[8,8,16,128]{3,2,1,0:T(8,128)(2,1)S(1)}, bf16[8,8,16,128]{3,2,1,0:T(8,128)(2,1)S(1)}, u32[]{:S(2)}, u32[]{:S(2)}) collective-permute-start(bf16[8,8,16,128]{3,2,1,0:T(8,128)(2,1)S(1)} %collective-permute-done.4.refs_2_), channel_id=1, source_target_pairs={{0,32},{32,0},{1,33},{33,1},{2,34},{34,2},{3,35},{35,3},{4,36},{36... | collective-permute-start | bytes 786440 | tf_op jit(solution)/shard_map/ppermute | solution.py:273
  43.2 1.6 %copy-start.2 = (bf16[8,8,16,128]{3,2,1,0:T(8,128)(2,1)}, bf16[8,8,16,128]{3,2,1,0:T(8,128)(2,1)S(1)}, u32[]{:S(2)}) copy-start(bf16[8,8,16,128]{3,2,1,0:T(8,128)(2,1)S(1)} %collective-permute-done.3.refs_1_) | copy-start | bytes 786436
  43.2 1.6 %collective-permute-start.7 = (bf16[8,8,16,128]{3,2,1,0:T(8,128)(2,1)S(1)}, bf16[8,8,16,128]{3,2,1,0:T(8,128)(2,1)S(1)}, u32[]{:S(2)}, u32[]{:S(2)}) collective-permute-start(bf16[8,8,16,128]{3,2,1,0:T(8,128)(2,1)S(1)} %collective-permute-done.3.refs_1_), channel_id=1, source_target_pairs={{0,32},{32,0},{1,33},{33,1},{2,34},{34,2},{3,35},{35,3},{4,36},{36... | collective-permute-start | bytes 786440 | tf_op jit(solution)/shard_map/ppermute | solution.py:273
  44.3 0.7 copy-start.3
  44.3 0.8 copy-start.4
  44.4 0.8 copy-start.5
  45.2 0.7 copy-start.6
  52.8 21.2 %all-to-all-start.1 = ((bf16[32,17,4,128]{3,2,1,0:T(4,128)(2,1)}), bf16[32,17,4,128]{3,2,1,0:T(4,128)(2,1)S(1)}, u32[]{:S(2)}, u32[]{:S(2)}) async-start(bf16[32,17,4,128]{3,2,1,0:T(4,128)(2,1)} %blocks.1), calls=%async_computation.1 | async-start | bytes 1114112 | tf_op jit(solution)/shard_map/all_to_all | solution.py:291

commit v2 on v1

--- a/solution.py
+++ b/solution.py
@@ -22,42 +22,23 @@
     return hi, mid, lo
 
 
-def lay_kernel(here, *refs):
-    pieces, out_ref, ordered = refs[:-2], refs[-2], refs[-1]
-    for m, piece in enumerate(pieces):
-        ordered[here[0] ^ m] = piece[...]
-    for z in range(out_ref.shape[0]):
-        out_ref[z] = jnp.concatenate([ordered[x, z] for x in range(len(pieces))], axis=1)
-
-
-def lay(here, pieces):
-    n_z, rows, depth, width = pieces[0].shape
-    return pl.pallas_call(
-        lay_kernel,
-        out_shape=jax.ShapeDtypeStruct((n_z, rows, len(pieces) * depth, width), pieces[0].dtype),
-        in_specs=[pl.BlockSpec(memory_space=pltpu.SMEM)]
-        + [pl.BlockSpec(memory_space=pltpu.VMEM)] * len(pieces),
-        out_specs=pl.BlockSpec(memory_space=pltpu.VMEM),
-        scratch_shapes=[pltpu.VMEM((len(pieces), n_z, rows, depth, width), pieces[0].dtype)],
-        name="lay",
-    )(here, *pieces)
-
-
-def block_kernel(here, owner, fill, k_hbm, v_hbm, *refs):
+def block_kernel(owner, fill, k_hbm, v_hbm, *refs):
     pieces = refs[:-6]
     out_ref, k_all, v_all, picked, stats, sem = refs[-6:]
-    slots, n_kv, per, _ = picked.shape
-    cols = n_kv * per
-    n_tp = out_ref.shape[0]
-    together = 8
+    slots, n_tp, depth, _ = picked.shape
+    cols = n_tp * depth
+    n_kv = KVH
+    per, n_x = cols // n_kv, n_tp // n_kv
+    together = 4
     rows = pieces[0].shape[1]
     n_core = 2
     n_y = len(pieces) // n_core
+    here_y, here_core = lax.axis_index("y"), lax.axis_index("core")
 
     def fetch(b):
         home = owner[b] // rows
         row = lax.rem(owner[b], rows)
-        which = (home // n_core ^ here[0]) + (lax.rem(home, n_core) ^ here[1]) * n_y
+        which = (home // n_core ^ here_y) + (lax.rem(home, n_core) ^ here_core) * n_y
         for p, piece in enumerate(pieces):
 
             @pl.when(which == p)
@@ -84,7 +65,7 @@
     def score(b):
         spread = []
         for g in range(n_kv):
-            mine = picked[b, g]
+            mine = picked[b, g * n_x : (g + 1) * n_x].reshape(per, DH)
             spread.append(
                 jnp.concatenate([nothing] * g + [mine] + [nothing] * (n_kv - 1 - g), axis=1)
             )
@@ -107,14 +88,13 @@
 
     def mix(b, rounded):
         mixed = []
-        for g in range(n_kv):
-            mixed.append(
-                jnp.dot(
-                    rounded[g * per : (g + 1) * per],
-                    v_all[b, :, g * DH : (g + 1) * DH],
-                    preferred_element_type=jnp.float32,
-                ).astype(jnp.bfloat16)
-            )
+        for g in range(0, n_kv, 2):
+            two = jnp.dot(
+                rounded[g * per : (g + 2) * per],
+                v_all[b, :, g * DH : (g + 2) * DH],
+                preferred_element_type=jnp.float32,
+            ).astype(jnp.bfloat16)
+            mixed = mixed + [two[:per, :DH], two[per:, DH:]]
         mixed = jnp.concatenate(mixed, axis=0)
         out_ref[:, pl.ds(b, 1)] = mixed.reshape(n_tp, 1, cols // n_tp, DH)
 
@@ -135,20 +115,19 @@
     out_ref[:, pl.ds(slots, 1)] = packed.reshape(n_tp, 1, cols // n_tp, DH)
 
 
-def blocks(here, pieces, k_cache, v_cache, block_req, block_fill, n_tp):
+def blocks(pieces, k_cache, v_cache, block_req, block_fill, n_tp):
     slots = k_cache.shape[0]
-    n_kv, _, per, _ = pieces[0].shape
-    cols = n_kv * per
+    cols = n_tp * pieces[0].shape[2]
     return pl.pallas_call(
         block_kernel,
         out_shape=jax.ShapeDtypeStruct((n_tp, slots + 1, cols // n_tp, DH), jnp.bfloat16),
-        in_specs=[pl.BlockSpec(memory_space=pltpu.SMEM)] * 3
+        in_specs=[pl.BlockSpec(memory_space=pltpu.SMEM)] * 2
         + [pl.BlockSpec(memory_space=pl.ANY)] * (2 + len(pieces)),
         out_specs=pl.BlockSpec(memory_space=pltpu.VMEM),
         scratch_shapes=[
             pltpu.VMEM(k_cache.shape, k_cache.dtype),
             pltpu.VMEM(v_cache.shape, v_cache.dtype),
-            pltpu.VMEM((slots, n_kv, per, DH), pieces[0].dtype),
+            pltpu.VMEM((slots,) + pieces[0].shape[:1] + pieces[0].shape[2:], pieces[0].dtype),
             pltpu.VMEM((DH, cols), jnp.float32),
             pltpu.SemaphoreType.DMA((3, slots)),
         ],
@@ -157,17 +136,19 @@
             flops=4 * slots * BLK * DH * 128, bytes_accessed=9 * 1024 * 1024, transcendentals=slots * BLK * 128
         ),
         name="blocks",
-    )(here, block_req, block_fill, k_cache, v_cache, *pieces)
+    )(block_req, block_fill, k_cache, v_cache, *pieces)
 
 
 def combine(got, requests):
     n_src = got.shape[0]
     slots = got.shape[1] - 1
     n_cols = got.shape[2]
-    out = got[:, :slots].reshape(n_src * slots, n_cols, DH)
+    every = n_src * (slots + 1)
+    out = got.reshape(every, n_cols, DH)
     stats = got[:, slots, :, : 7 * slots].astype(jnp.float32)
     stats = stats.reshape(n_src, n_cols, 7, slots).transpose(2, 1, 0, 3)
-    stats = stats.reshape(7, n_cols, n_src * slots)
+    stats = jnp.pad(stats, ((0, 0), (0, 0), (0, 0), (0, 1)), constant_values=-1.0)
+    stats = stats.reshape(7, n_cols, every)
     peak = stats[0] + stats[1] + stats[2]
     total = stats[3] + stats[4] + stats[5]
     owner = stats[6, 0].astype(jnp.int32)
@@ -187,7 +168,7 @@
     return num / safe, jnp.where(some, top + jnp.log(safe), far_below)
 
 
-def fresh_kernel(q_ref, keys_ref, values_ref, out_ref):
+def fresh_kernel(kv, q_ref, keys_ref, values_ref, out_ref):
     n_steps, own_rows, width = q_ref.shape
     n_heads = width // DH
     lane = lax.broadcasted_iota(jnp.int32, (own_rows, DH), 1)
@@ -214,16 +195,22 @@
     out_ref[n_steps * n_heads] = levels
 
 
-def fresh_part(queries, keys, values):
+def fresh_part(kv, queries, new_keys, new_values):
     n_steps, own_rows, width = queries.shape
+    shape = (n_steps * (width // DH) + 1, own_rows, DH)
+    own_kv = pl.BlockSpec((n_steps, own_rows, DH), lambda i, kv: (0, 0, kv[0]))
     return pl.pallas_call(
         fresh_kernel,
-        out_shape=jax.ShapeDtypeStruct((n_steps * (width // DH) + 1, own_rows, DH), jnp.float32),
-        in_specs=[pl.BlockSpec(memory_space=pltpu.VMEM)] * 3,
-        out_specs=pl.BlockSpec(memory_space=pltpu.VMEM),
+        out_shape=jax.ShapeDtypeStruct(shape, jnp.float32),
+        grid_spec=pltpu.PrefetchScalarGridSpec(
+            num_scalar_prefetch=1,
+            grid=(1,),
+            in_specs=[pl.BlockSpec(queries.shape, lambda i, kv: (0, 0, 0)), own_kv, own_kv],
+            out_specs=pl.BlockSpec(shape, lambda i, kv: (0, 0, 0)),
+        ),
         cost_estimate=pl.CostEstimate(flops=1 << 17, bytes_accessed=1 << 16, transcendentals=1 << 8),
         name="fresh",
-    )(queries, keys, values)
+    )(kv, queries, new_keys, new_values)
 
 
 def finish_kernel(got, fresh, out_ref):
@@ -274,22 +261,16 @@
 
     rows = queries.reshape(n_steps, own_rows, own_heads, DH).transpose(1, 0, 2, 3)
     rows = rows.reshape(own_rows, n_steps * own_heads, DH)
-    rows = lax.all_to_all(
-        jnp.broadcast_to(rows[None], (n_z,) + rows.shape), "z", 0, 0, tiled=True
-    )
-    at_x = lax.axis_index("x").astype(jnp.int32).reshape(1)
-    own = lay(at_x, [rows] + [from_other(rows, "x", m) for m in range(1, n_x)])
-    at_kv = lax.axis_index("z") * DH
-    keys = lax.dynamic_slice_in_dim(new_keys, at_kv, DH, axis=2)
-    values = lax.dynamic_slice_in_dim(new_values, at_kv, DH, axis=2)
-    own, keys, values = lax.optimization_barrier((own, keys, values))
+    own = lax.all_to_all(
+        jnp.broadcast_to(rows[None], (n_z * n_x,) + rows.shape), ("z", "x"), 0, 0, tiled=True
+    )
     pieces = [own] + [from_other(own, "y", m) for m in range(1, n_y)]
     pieces = pieces + [from_other(p, "core", 1) for p in pieces]
-    here = jnp.stack([lax.axis_index("y"), lax.axis_index("core")]).astype(jnp.int32)
-    sent = blocks(here, pieces, k_cache, v_cache, block_req, block_fill, n_z * n_x)
-    sent, keys, values = lax.optimization_barrier((sent, keys, values))
+    sent = blocks(pieces, k_cache, v_cache, block_req, block_fill, n_z * n_x)
+    kv = lax.axis_index("z").astype(jnp.int32).reshape(1)
+    sent, kv = lax.optimization_barrier((sent, kv))
     got = lax.all_to_all(sent, ("z", "x"), split_axis=0, concat_axis=0, tiled=True)
-    got, fresh = lax.optimization_barrier((got, fresh_part(queries, keys, values)))
+    got, fresh = lax.optimization_barrier((got, fresh_part(kv, queries, new_keys, new_values)))
     part, level = combine(got, n_inst * own_rows)
     level = level[..., 0].reshape(4, n_inst, own_rows).transpose(1, 2, 0)
     level = jnp.pad(level, ((0, 0), (0, 0), (0, DH - 4)))[:, None]

time: 90.6 us -> 89 us (0.982)
  blocking collectives: 11.8 us -> 33.8 us
  waiting for transfers between devices: 32.3 us -> 18.8 us
  starting transfers between devices: 26.6 us -> 22.2 us
  local copies, waits for them, and re-layouts: 5.7 us -> 2.8 us
  Pallas kernels: 11.7 us -> 9.5 us
    all_to_all x0 -> x1, blocking collectives: none -> 22.9 us  [body(): lax.all_to_all(jnp.broadcast_to(rows[None], (n_z * n_x,) + rows.shape), (...]
    all_to_all x1 -> x0, starting transfers between devices: 9.01 us -> none  [body(): lax.all_to_all(jnp.broadcast_to(rows[None], (n_z,) + rows.shape), 'z', 0,...]
    all_to_all x1 -> x0, waiting for transfers between devices: 7.24 us -> none  [body(): lax.all_to_all(jnp.broadcast_to(rows[None], (n_z,) + rows.shape), 'z', 0,...]
    ppermute x10 -> x7, waiting for transfers between devices: 9.21 us -> 3.16 us  [from_other(): lax.ppermute(value, axis, [(j, j ^ m) for j in range(lax.axis_size(axis))])]
    ppermute x10 -> x7, starting transfers between devices: 13.7 us -> 17.4 us  [from_other(): lax.ppermute(value, axis, [(j, j ^ m) for j in range(lax.axis_size(axis))])]
    pallas_call x2 -> x1, Pallas kernels: 3.16 us -> 1.43 us  [fresh_part(): pl.pallas_call(fresh_kernel, out_shape=jax.ShapeDtypeStruct(shape, jnp.fl...]
    dynamic_slice x1 -> x0, local copies, waits for them, and re-layouts: 1.3 us -> none  [body(): values = lax.dynamic_slice_in_dim(new_values, at_kv, DH, axis=2)]
    unnamed x22 -> x16, local copies, waits for them, and re-layouts: 1.64 us -> 0.71 us
  transfers between devices with their start and end apart: 12 -> 8, of which waited for: 6 -> 4; matrix products, arithmetic and copies ran while one was open for 2% -> 0% of each run, Pallas kernels for 2% -> 2%
where the time goes in v2:
time: 89 us; the launch traced here: 88.6 us
  blocking collectives  33.8 us (38%)
  starting transfers between devices  22.2 us (25%)
  waiting for transfers between devices  18.8 us (21%)
  Pallas kernels  9.5 us (11%)
  local copies, waits for them, and re-layouts  2.8 us (3%)
    all_to_all x1, blocking collectives, body(): lax.all_to_all(jnp.broadcast_to(rows[None], (n_z * n_x,) + rows.shape), (...  22.9 us
    ppermute x7, starting transfers between devices, from_other(): lax.ppermute(value, axis, [(j, j ^ m) for j in range(lax.axis_size(axis))])  17.4 us
    all_to_all x1, waiting for transfers between devices, body(): lax.all_to_all(sent, ('z', 'x'), split_axis=0, concat_axis=0, tiled=True)  15.6 us
    all_to_all x1, blocking collectives, body(): lax.all_to_all(jnp.concatenate([part, level], axis=1), ('y', 'core'), 0,...  10.9 us
    pallas_call x1, Pallas kernels, blocks(): pl.pallas_call(block_kernel, out_shape=jax.ShapeDtypeStruct((n_tp, slots...  6.4 us
    all_to_all x1, starting transfers between devices, body(): lax.all_to_all(sent, ('z', 'x'), split_axis=0, concat_axis=0, tiled=True)  4.77 us
    ppermute x7, waiting for transfers between devices, from_other(): lax.ppermute(value, axis, [(j, j ^ m) for j in range(lax.axis_size(axis))])  3.16 us
  transfers between devices with their start and end apart: 8, of which 4 were waited for; matrix products, arithmetic and copies ran while one was open for 0% of the time, Pallas kernels for 2%

profile of v2, /device:TPU:1, one launch (start us, length us, event | category | flops | bytes accessed | tf_op | source)
XLA Modules:
  0.0 88.6 jit_solution(9219117569285365204)
XLA Ops:
  0.0 0.7 copy.23
  0.7 0.1 broadcast_in_dim.58
  0.8 22.9 %all_to_all.15.refs_0_ = bf16[32,8,4,128]{3,2,1,0:T(4,128)(2,1)S(1)} all-to-all(bf16[32,8,4,128]{3,2,1,0:T(4,128)(2,1)S(1)} %broadcast_in_dim.58), channel_id=1, replica_groups=mesh['y'=4,'core'=2,'z'=8,'x'=4] {'z','x'}, dimensions={0} | all-to-all | bytes 524288 | tf_op jit(solution)/shard_map/all_to_all | solution.py:264
  23.6 0.0 copy-start
  23.6 1.3 %collective-permute-start = (bf16[32,8,4,128]{3,2,1,0:T(4,128)(2,1)S(1)}, bf16[32,8,4,128]{3,2,1,0:T(4,128)(2,1)S(1)}, u32[]{:S(2)}, u32[]{:S(2)}) collective-permute-start(bf16[32,8,4,128]{3,2,1,0:T(4,128)(2,1)S(1)} %all_to_all.15.refs_0_), channel_id=1, source_target_pairs={{0,64},{64,0},{128,192},{192,128},{1,65},{65,1},{129,193},{193,129... | collective-permute-start | bytes 786440 | tf_op jit(solution)/shard_map/ppermute | solution.py:260
  24.9 2.6 %collective-permute-start.1 = (bf16[32,8,4,128]{3,2,1,0:T(4,128)(2,1)S(1)}, bf16[32,8,4,128]{3,2,1,0:T(4,128)(2,1)S(1)}, u32[]{:S(2)}, u32[]{:S(2)}) collective-permute-start(bf16[32,8,4,128]{3,2,1,0:T(4,128)(2,1)S(1)} %all_to_all.15.refs_0_), channel_id=1, source_target_pairs={{0,128},{64,192},{128,0},{192,64},{1,129},{65,193},{129,1},{193,65... | collective-permute-start | bytes 786440 | tf_op jit(solution)/shard_map/ppermute | solution.py:260
  27.6 0.0 collective-permute-start.2
  27.6 3.2 %collective-permute-start.3 = (bf16[32,8,4,128]{3,2,1,0:T(4,128)(2,1)S(1)}, bf16[32,8,4,128]{3,2,1,0:T(4,128)(2,1)S(1)}, u32[]{:S(2)}, u32[]{:S(2)}) collective-permute-start(bf16[32,8,4,128]{3,2,1,0:T(4,128)(2,1)S(1)} %all_to_all.15.refs_0_), channel_id=1, source_target_pairs={{0,32},{32,0},{1,33},{33,1},{2,34},{34,2},{3,35},{35,3},{4,36},{36... | collective-permute-start | bytes 786440 | tf_op jit(solution)/shard_map/ppermute | solution.py:260
  30.8 0.0 collective-permute-done.refs_1_
  30.8 4.4 %collective-permute-start.4 = (bf16[32,8,4,128]{3,2,1,0:T(4,128)(2,1)S(1)}, bf16[32,8,4,128]{3,2,1,0:T(4,128)(2,1)S(1)}, u32[]{:S(2)}, u32[]{:S(2)}) collective-permute-start(bf16[32,8,4,128]{3,2,1,0:T(4,128)(2,1)S(1)} %collective-permute-done.refs_1_), channel_id=1, source_target_pairs={{0,32},{32,0},{1,33},{33,1},{2,34},{34,2},{3,35},{35,3},{4,36},{36... | collective-permute-start | bytes 786440 | tf_op jit(solution)/shard_map/ppermute | solution.py:260
  35.2 1.6 %collective-permute-done.1.refs_2_ = bf16[32,8,4,128]{3,2,1,0:T(4,128)(2,1)S(1)} collective-permute-done((bf16[32,8,4,128]{3,2,1,0:T(4,128)(2,1)S(1)}, bf16[32,8,4,128]{3,2,1,0:T(4,128)(2,1)S(1)}, u32[]{:S(2)}, u32[]{:S(2)}) %collective-permute-start.1) | collective-permute-done | bytes 262176 | tf_op jit(solution)/shard_map/ppermute | solution.py:260
  36.8 3.7 %collective-permute-start.5 = (bf16[32,8,4,128]{3,2,1,0:T(4,128)(2,1)S(1)}, bf16[32,8,4,128]{3,2,1,0:T(4,128)(2,1)S(1)}, u32[]{:S(2)}, u32[]{:S(2)}) collective-permute-start(bf16[32,8,4,128]{3,2,1,0:T(4,128)(2,1)S(1)} %collective-permute-done.1.refs_2_), channel_id=1, source_target_pairs={{0,32},{32,0},{1,33},{33,1},{2,34},{34,2},{3,35},{35,3},{4,36},{36... | collective-permute-start | bytes 786440 | tf_op jit(solution)/shard_map/ppermute | solution.py:260
  40.5 0.4 collective-permute-done.2.refs_3_
  40.9 2.2 %collective-permute-start.6 = (bf16[32,8,4,128]{3,2,1,0:T(4,128)(2,1)S(1)}, bf16[32,8,4,128]{3,2,1,0:T(4,128)(2,1)S(1)}, u32[]{:S(2)}, u32[]{:S(2)}) collective-permute-start(bf16[32,8,4,128]{3,2,1,0:T(4,128)(2,1)S(1)} %collective-permute-done.2.refs_3_), channel_id=1, source_target_pairs={{0,32},{32,0},{1,33},{33,1},{2,34},{34,2},{3,35},{35,3},{4,36},{36... | collective-permute-start | bytes 786440 | tf_op jit(solution)/shard_map/ppermute | solution.py:260
  43.1 0.0 collective-permute-done.3.refs_4_
  43.1 0.0 collective-permute-done.4.refs_5_
  43.1 0.0 copy-start.5
  43.1 0.0 collective-permute-done.5.refs_6_
  43.1 0.0 copy-start.6
  43.1 1.1 %collective-permute-done.6.refs_7_ = bf16[32,8,4,128]{3,2,1,0:T(4,128)(2,1)S(1)} collective-permute-done((bf16[32,8,4,128]{3,2,1,0:T(4,128)(2,1)S(1)}, bf16[32,8,4,128]{3,2,1,0:T(4,128)(2,1)S(1)}, u32[]{:S(2)}, u32[]{:S(2)}) %collective-permute-start.6) | collective-permute-done | bytes 262176 | tf_op jit(solution)/shard_map/ppermute | solution.py:260
  44.3 0.0 copy-done
  44.3 0.0 copy-done.1
  44.3 0.0 copy-done.2
  44.3 0.0 copy-done.3
  44.3 0.0 copy-done.4
  44.3 0.0 copy-done.5
  44.3 0.0 copy-done.6
  44.3 0.0 copy-start.7
  44.3 0.7 copy-done.7
  45.0 6.4 %blocks.1 = bf16[32,17,4,128]{3,2,1,0:T(4,128)(2,1)} custom-call(s32[16]{0:T(128)} %owner.1, s32[16]{0:T(128)} %fill.1, bf16[16,128,1024]{2,1,0:T(8,128)(2,1)} %k_hbm.1, bf16[16,128,1024]{2,1,0:T(8,128)(2,1)} %v_hbm.1, bf16[32,8,4,128]{3,2,1,0:T(4,128)(2,1)} %copy-done, bf16[32,8,4,128]{3,2,1,0:T(4,128)(2,1)} %copy-done.1, ...), custom_call_target="tpu_custom_call" | custom-call | flops 134217728 | bytes 9437184 | tf_op jit(solution)/shard_map/blocks/pallas_call | solution.py:121
  51.4 4.8 %all-to-all-start.1 = ((bf16[32,17,4,128]{3,2,1,0:T(4,128)(2,1)}), bf16[32,17,4,128]{3,2,1,0:T(4,128)(2,1)S(1)}, u32[]{:S(2)}, u32[]{:S(2)}) async-start(bf16[32,17,4,128]{3,2,1,0:T(4,128)(2,1)} %blocks.1), calls=%async_computation.1 | async-start | bytes 1114112 | tf_op jit(solution)/shard_map/all_to_all | solution.py:272
  56.2 1.4 %fresh.1 = f32[5,8,128]{2,1,0:T(8,128)} custom-call(s32[1]{0:T(128)} %bitcast.3.kv, bf16[2,8,256]{2,1,0:T(8,128)(2,1)} %q_ref.1, bf16[2,8,1024]{2,1,0:T(8,128)(2,1)} %keys_ref.1, bf16[2,8,1024]{2,1,0:T(8,128)(2,1)} %values_ref.1), custom_call_target="tpu_custom_call" | custom-call | flops 131072 | bytes 65536 | tf_op jit(solution)/shard_map/fresh/pallas_call | solution.py:202
  57.6 15.6 %all-to-all-done.1 = bf16[32,17,4,128]{3,2,1,0:T(4,128)(2,1)S(1)} async-done(((bf16[32,17,4,128]{3,2,1,0:T(4,128)(2,1)}), bf16[32,17,4,128]{3,2,1,0:T(4,128)(2,1)S(1)}, u32[]{:S(2)}, u32[]{:S(2)}) %all-to-all-start.1) | async-done | bytes 557088 | tf_op jit(solution)/shard_map/all_to_all | solution.py:272
  73.3 0.1 copy.24
  73.4 0.2 copy.25
  73.7 0.3 reshape.106
  74.1 0.1 copy.26
  74.2 0.1 add.51
  74.3 0.1 copy.29
  74.4 0.1 add.55
  74.5 0.1 select_reduce_fusion
  74.6 0.3 fusion.5
  75.0 0.1 copy.31
  75.1 0.1 copy.32
  75.2 0.3 fusion.8
  75.5 0.4 fusion.1
  76.0 10.9 %all_to_all.16.got = f32[8,5,8,128]{3,2,1,0:T(8,128)} all-to-all(f32[8,5,8,128]{3,2,1,0:T(8,128)S(1)} %pad_maximum_fusion), channel_id=1, replica_groups=mesh['y'=4,'core'=2,'z'=8,'x'=4] {'y','core'}, dimensions={0} | all-to-all | bytes 327680 | tf_op jit(solution)/shard_map/all_to_all | solution.py:278
  86.9 1.7 %finish.1 = bf16[2,8,256]{2,1,0:T(8,128)(2,1)} custom-call(f32[8,5,8,128]{3,2,1,0:T(8,128)} %all_to_all.16.got, f32[5,8,128]{2,1,0:T(8,128)} %fresh.1), custom_call_target="tpu_custom_call" | custom-call | tf_op jit(solution)/shard_map/finish/pallas_call | solution.py:243
  (14 shorter events, 0.2 us)
Async XLA Ops:
  23.6 20.6 %copy-start = (bf16[32,8,4,128]{3,2,1,0:T(4,128)(2,1)}, bf16[32,8,4,128]{3,2,1,0:T(4,128)(2,1)S(1)}, u32[]{:S(2)}) copy-start(bf16[32,8,4,128]{3,2,1,0:T(4,128)(2,1)S(1)} %all_to_all.15.refs_0_) | copy-start | bytes 786436
  23.6 7.2 %collective-permute-start = (bf16[32,8,4,128]{3,2,1,0:T(4,128)(2,1)S(1)}, bf16[32,8,4,128]{3,2,1,0:T(4,128)(2,1)S(1)}, u32[]{:S(2)}, u32[]{:S(2)}) collective-permute-start(bf16[32,8,4,128]{3,2,1,0:T(4,128)(2,1)S(1)} %all_to_all.15.refs_0_), channel_id=1, source_target_pairs={{0,64},{64,0},{128,192},{192,128},{1,65},{65,1},{129,193},{193,129... | collective-permute-start | bytes 786440 | tf_op jit(solution)/shard_map/ppermute | solution.py:260
  24.9 11.8 %collective-permute-start.1 = (bf16[32,8,4,128]{3,2,1,0:T(4,128)(2,1)S(1)}, bf16[32,8,4,128]{3,2,1,0:T(4,128)(2,1)S(1)}, u32[]{:S(2)}, u32[]{:S(2)}) collective-permute-start(bf16[32,8,4,128]{3,2,1,0:T(4,128)(2,1)S(1)} %all_to_all.15.refs_0_), channel_id=1, source_target_pairs={{0,128},{64,192},{128,0},{192,64},{1,129},{65,193},{129,1},{193,65... | collective-permute-start | bytes 786440 | tf_op jit(solution)/shard_map/ppermute | solution.py:260
  27.6 13.4 %collective-permute-start.2 = (bf16[32,8,4,128]{3,2,1,0:T(4,128)(2,1)S(1)}, bf16[32,8,4,128]{3,2,1,0:T(4,128)(2,1)S(1)}, u32[]{:S(2)}, u32[]{:S(2)}) collective-permute-start(bf16[32,8,4,128]{3,2,1,0:T(4,128)(2,1)S(1)} %all_to_all.15.refs_0_), channel_id=1, source_target_pairs={{0,192},{64,128},{128,64},{192,0},{1,193},{65,129},{129,65},{193,1... | collective-permute-start | bytes 786440 | tf_op jit(solution)/shard_map/ppermute | solution.py:260
  27.6 15.6 %collective-permute-start.3 = (bf16[32,8,4,128]{3,2,1,0:T(4,128)(2,1)S(1)}, bf16[32,8,4,128]{3,2,1,0:T(4,128)(2,1)S(1)}, u32[]{:S(2)}, u32[]{:S(2)}) collective-permute-start(bf16[32,8,4,128]{3,2,1,0:T(4,128)(2,1)S(1)} %all_to_all.15.refs_0_), channel_id=1, source_target_pairs={{0,32},{32,0},{1,33},{33,1},{2,34},{34,2},{3,35},{35,3},{4,36},{36... | collective-permute-start | bytes 786440 | tf_op jit(solution)/shard_map/ppermute | solution.py:260
  30.8 13.5 %copy-start.1 = (bf16[32,8,4,128]{3,2,1,0:T(4,128)(2,1)}, bf16[32,8,4,128]{3,2,1,0:T(4,128)(2,1)S(1)}, u32[]{:S(2)}) copy-start(bf16[32,8,4,128]{3,2,1,0:T(4,128)(2,1)S(1)} %collective-permute-done.refs_1_) | copy-start | bytes 786436
  30.8 12.3 %collective-permute-start.4 = (bf16[32,8,4,128]{3,2,1,0:T(4,128)(2,1)S(1)}, bf16[32,8,4,128]{3,2,1,0:T(4,128)(2,1)S(1)}, u32[]{:S(2)}, u32[]{:S(2)}) collective-permute-start(bf16[32,8,4,128]{3,2,1,0:T(4,128)(2,1)S(1)} %collective-permute-done.refs_1_), channel_id=1, source_target_pairs={{0,32},{32,0},{1,33},{33,1},{2,34},{34,2},{3,35},{35,3},{4,36},{36... | collective-permute-start | bytes 786440 | tf_op jit(solution)/shard_map/ppermute | solution.py:260
  36.8 7.5 %copy-start.2 = (bf16[32,8,4,128]{3,2,1,0:T(4,128)(2,1)}, bf16[32,8,4,128]{3,2,1,0:T(4,128)(2,1)S(1)}, u32[]{:S(2)}) copy-start(bf16[32,8,4,128]{3,2,1,0:T(4,128)(2,1)S(1)} %collective-permute-done.1.refs_2_) | copy-start | bytes 786436
  36.8 6.4 %collective-permute-start.5 = (bf16[32,8,4,128]{3,2,1,0:T(4,128)(2,1)S(1)}, bf16[32,8,4,128]{3,2,1,0:T(4,128)(2,1)S(1)}, u32[]{:S(2)}, u32[]{:S(2)}) collective-permute-start(bf16[32,8,4,128]{3,2,1,0:T(4,128)(2,1)S(1)} %collective-permute-done.1.refs_2_), channel_id=1, source_target_pairs={{0,32},{32,0},{1,33},{33,1},{2,34},{34,2},{3,35},{35,3},{4,36},{36... | collective-permute-start | bytes 786440 | tf_op jit(solution)/shard_map/ppermute | solution.py:260
  40.9 3.4 %copy-start.3 = (bf16[32,8,4,128]{3,2,1,0:T(4,128)(2,1)}, bf16[32,8,4,128]{3,2,1,0:T(4,128)(2,1)S(1)}, u32[]{:S(2)}) copy-start(bf16[32,8,4,128]{3,2,1,0:T(4,128)(2,1)S(1)} %collective-permute-done.2.refs_3_) | copy-start | bytes 786436
  40.9 3.3 %collective-permute-start.6 = (bf16[32,8,4,128]{3,2,1,0:T(4,128)(2,1)S(1)}, bf16[32,8,4,128]{3,2,1,0:T(4,128)(2,1)S(1)}, u32[]{:S(2)}, u32[]{:S(2)}) collective-permute-start(bf16[32,8,4,128]{3,2,1,0:T(4,128)(2,1)S(1)} %collective-permute-done.2.refs_3_), channel_id=1, source_target_pairs={{0,32},{32,0},{1,33},{33,1},{2,34},{34,2},{3,35},{35,3},{4,36},{36... | collective-permute-start | bytes 786440 | tf_op jit(solution)/shard_map/ppermute | solution.py:260
  43.1 1.2 %copy-start.4 = (bf16[32,8,4,128]{3,2,1,0:T(4,128)(2,1)}, bf16[32,8,4,128]{3,2,1,0:T(4,128)(2,1)S(1)}, u32[]{:S(2)}) copy-start(bf16[32,8,4,128]{3,2,1,0:T(4,128)(2,1)S(1)} %collective-permute-done.3.refs_4_) | copy-start | bytes 786436
  43.1 1.2 %copy-start.5 = (bf16[32,8,4,128]{3,2,1,0:T(4,128)(2,1)}, bf16[32,8,4,128]{3,2,1,0:T(4,128)(2,1)S(1)}, u32[]{:S(2)}) copy-start(bf16[32,8,4,128]{3,2,1,0:T(4,128)(2,1)S(1)} %collective-permute-done.4.refs_5_) | copy-start | bytes 786436
  43.1 1.2 %copy-start.6 = (bf16[32,8,4,128]{3,2,1,0:T(4,128)(2,1)}, bf16[32,8,4,128]{3,2,1,0:T(4,128)(2,1)S(1)}, u32[]{:S(2)}) copy-start(bf16[32,8,4,128]{3,2,1,0:T(4,128)(2,1)S(1)} %collective-permute-done.5.refs_6_) | copy-start | bytes 786436
  44.3 0.7 copy-start.7
  51.4 21.8 %all-to-all-start.1 = ((bf16[32,17,4,128]{3,2,1,0:T(4,128)(2,1)}), bf16[32,17,4,128]{3,2,1,0:T(4,128)(2,1)S(1)}, u32[]{:S(2)}, u32[]{:S(2)}) async-start(bf16[32,17,4,128]{3,2,1,0:T(4,128)(2,1)} %blocks.1), calls=%async_computation.1 | async-start | bytes 1114112 | tf_op jit(solution)/shard_map/all_to_all | solution.py:272

commit v3 on v2

--- a/solution.py
+++ b/solution.py
@@ -30,20 +30,23 @@
     n_kv = KVH
     per, n_x = cols // n_kv, n_tp // n_kv
     together = 4
-    rows = pieces[0].shape[1]
+    rows = pieces[0].shape[2]
     n_core = 2
-    n_y = len(pieces) // n_core
     here_y, here_core = lax.axis_index("y"), lax.axis_index("core")
 
     def fetch(b):
         home = owner[b] // rows
         row = lax.rem(owner[b], rows)
-        which = (home // n_core ^ here_y) + (lax.rem(home, n_core) ^ here_core) * n_y
+        core = lax.rem(home, n_core)
+        away = home // n_core ^ here_y
+        odd = lax.rem(away, 2)
+        half = (away // 2) ^ (odd * core)
+        which = odd + (core ^ here_core) * 2
         for p, piece in enumerate(pieces):
 
             @pl.when(which == p)
             def _(piece=piece):
-                pltpu.make_async_copy(piece.at[:, row], picked.at[b], sem.at[2, b]).start()
+                pltpu.make_async_copy(piece.at[:, half, row], picked.at[b], sem.at[2, b]).start()
 
     def copies(b):
         return (
@@ -57,7 +60,7 @@
             c.start()
         return 0
 
-    lax.fori_loop(0, slots, start, 0)
+    lax.fori_loop(0, 2 * together, start, 0)
     stats[...] = jnp.zeros_like(stats)
     slot_at = lax.broadcasted_iota(jnp.int32, (BLK, cols), 0)
     nothing = jnp.zeros((per, DH), jnp.bfloat16)
@@ -100,10 +103,15 @@
 
     def some_blocks(i, _):
         first = i * together
+
+        @pl.when(first + 2 * together < slots)
+        def _():
+            lax.fori_loop(first + 2 * together, first + 3 * together, start, 0)
+
         for j in range(together):
             for c in copies(first + j):
                 c.wait()
-            pltpu.make_async_copy(pieces[0].at[:, 0], picked.at[first + j], sem.at[2, first + j]).wait()
+            pltpu.make_async_copy(pieces[0].at[:, 0, 0], picked.at[first + j], sem.at[2, first + j]).wait()
         scores = [score(first + j) for j in range(together)]
         rounded = [soften(first + j, scores[j]) for j in range(together)]
         for j in range(together):
@@ -117,7 +125,7 @@
 
 def blocks(pieces, k_cache, v_cache, block_req, block_fill, n_tp):
     slots = k_cache.shape[0]
-    cols = n_tp * pieces[0].shape[2]
+    cols = n_tp * pieces[0].shape[3]
     return pl.pallas_call(
         block_kernel,
         out_shape=jax.ShapeDtypeStruct((n_tp, slots + 1, cols // n_tp, DH), jnp.bfloat16),
@@ -127,7 +135,7 @@
         scratch_shapes=[
             pltpu.VMEM(k_cache.shape, k_cache.dtype),
             pltpu.VMEM(v_cache.shape, v_cache.dtype),
-            pltpu.VMEM((slots,) + pieces[0].shape[:1] + pieces[0].shape[2:], pieces[0].dtype),
+            pltpu.VMEM((slots,) + pieces[0].shape[:1] + pieces[0].shape[3:], pieces[0].dtype),
             pltpu.VMEM((DH, cols), jnp.float32),
             pltpu.SemaphoreType.DMA((3, slots)),
         ],
@@ -261,10 +269,14 @@
 
     rows = queries.reshape(n_steps, own_rows, own_heads, DH).transpose(1, 0, 2, 3)
     rows = rows.reshape(own_rows, n_steps * own_heads, DH)
+    rows = jnp.stack([rows, from_other(rows, "y", 2)])
     own = lax.all_to_all(
         jnp.broadcast_to(rows[None], (n_z * n_x,) + rows.shape), ("z", "x"), 0, 0, tiled=True
     )
-    pieces = [own] + [from_other(own, "y", m) for m in range(1, n_y)]
+    partner = [
+        (y * n_core + c, (y ^ (1, 3)[c]) * n_core + c) for y in range(n_y) for c in range(n_core)
+    ]
+    pieces = [own, lax.ppermute(own, ("y", "core"), partner)]
     pieces = pieces + [from_other(p, "core", 1) for p in pieces]
     sent = blocks(pieces, k_cache, v_cache, block_req, block_fill, n_z * n_x)
     kv = lax.axis_index("z").astype(jnp.int32).reshape(1)

time: 89 us -> 92.1 us (1.035)
  starting transfers between devices: 22.2 us -> 17.6 us
  blocking collectives: 33.8 us -> 38 us
  waiting for transfers between devices: 18.8 us -> 21.9 us
    ppermute x7 -> x3, starting transfers between devices: 17.4 us -> 10.6 us  [from_other(): lax.ppermute(value, axis, [(j, j ^ m) for j in range(lax.axis_size(axis))])]
    ppermute x0 -> x1, waiting for transfers between devices: none -> 3.67 us  [body(): pieces = [own, lax.ppermute(own, ('y', 'core'), partner)]]
    all_to_all x1, blocking collectives: 22.9 us -> 25.6 us  [body(): lax.all_to_all(jnp.broadcast_to(rows[None], (n_z * n_x,) + rows.shape), (...]
    ppermute x0 -> x1, starting transfers between devices: none -> 2.73 us  [body(): pieces = [own, lax.ppermute(own, ('y', 'core'), partner)]]
    all_to_all x1, blocking collectives: 10.9 us -> 12.3 us  [body(): lax.all_to_all(jnp.concatenate([part, level], axis=1), ('y', 'core'), 0,...]
    ppermute x7 -> x3, waiting for transfers between devices: 3.16 us -> 2.57 us  [from_other(): lax.ppermute(value, axis, [(j, j ^ m) for j in range(lax.axis_size(axis))])]
  transfers between devices with their start and end apart: 8 -> 5, of which waited for: 4 -> 4; matrix products, arithmetic and copies ran while one was open for 0% -> 0% of each run, Pallas kernels for 2% -> 2%
where the time goes in v3:
time: 92.1 us; the launch traced here: 91.7 us
  blocking collectives  38 us (41%)
  waiting for transfers between devices  21.9 us (24%)
  starting transfers between devices  17.6 us (19%)
  Pallas kernels  9.81 us (11%)
  local copies, waits for them, and re-layouts  3.04 us (3%)
    all_to_all x1, blocking collectives, body(): lax.all_to_all(jnp.broadcast_to(rows[None], (n_z * n_x,) + rows.shape), (...  25.6 us
    all_to_all x1, waiting for transfers between devices, body(): lax.all_to_all(sent, ('z', 'x'), split_axis=0, concat_axis=0, tiled=True)  15.6 us
    all_to_all x1, blocking collectives, body(): lax.all_to_all(jnp.concatenate([part, level], axis=1), ('y', 'core'), 0,...  12.3 us
    ppermute x3, starting transfers between devices, from_other(): lax.ppermute(value, axis, [(j, j ^ m) for j in range(lax.axis_size(axis))])  10.6 us
    pallas_call x1, Pallas kernels, blocks(): pl.pallas_call(block_kernel, out_shape=jax.ShapeDtypeStruct((n_tp, slots...  6.71 us
    all_to_all x1, starting transfers between devices, body(): lax.all_to_all(sent, ('z', 'x'), split_axis=0, concat_axis=0, tiled=True)  4.27 us
    ppermute x1, waiting for transfers between devices, body(): pieces = [own, lax.ppermute(own, ('y', 'core'), partner)]  3.67 us
    ppermute x1, starting transfers between devices, body(): pieces = [own, lax.ppermute(own, ('y', 'core'), partner)]  2.73 us
  transfers between devices with their start and end apart: 5, of which 4 were waited for; matrix products, arithmetic and copies ran while one was open for 0% of the time, Pallas kernels for 2%

profile of v3, /device:TPU:1, one launch (start us, length us, event | category | flops | bytes accessed | tf_op | source)
XLA Modules:
  0.0 91.7 jit_solution(18387110258309778397)
XLA Ops:
  0.0 0.7 copy.25
  0.7 3.7 %collective-permute-start = (bf16[8,4,128]{2,1,0:T(4,128)(2,1)S(1)}, bf16[8,4,128]{2,1,0:T(4,128)(2,1)S(1)}, u32[]{:S(2)}, u32[]{:S(2)}) collective-permute-start(bf16[8,4,128]{2,1,0:T(4,128)(2,1)S(1)} %bitcast.35), channel_id=1, source_target_pairs={{0,128},{64,192},{128,0},{192,64},{1,129},{65,193},{129,1},{193,65... | collective-permute-start | bytes 24584 | tf_op jit(solution)/shard_map/ppermute | solution.py:268
  4.4 1.0 %collective-permute-done = bf16[8,4,128]{2,1,0:T(4,128)(2,1)S(1)} collective-permute-done((bf16[8,4,128]{2,1,0:T(4,128)(2,1)S(1)}, bf16[8,4,128]{2,1,0:T(4,128)(2,1)S(1)}, u32[]{:S(2)}, u32[]{:S(2)}) %collective-permute-start) | collective-permute-done | bytes 8224 | tf_op jit(solution)/shard_map/ppermute | solution.py:268
  5.5 0.2 broadcast_in_dim.56
  5.7 25.6 %all_to_all.15.refs_0_ = bf16[32,2,8,4,128]{4,3,2,1,0:T(4,128)(2,1)S(1)} all-to-all(bf16[32,2,8,4,128]{4,3,2,1,0:T(4,128)(2,1)S(1)} %broadcast_in_dim.56), channel_id=1, replica_groups=mesh['y'=4,'core'=2,'z'=8,'x'=4] {'z','x'}, dimensions={0} | all-to-all | bytes 1048576 | tf_op jit(solution)/shard_map/all_to_all | solution.py:273
  31.4 0.0 copy-start
  31.4 2.7 %collective-permute-start.1 = (bf16[32,2,8,4,128]{4,3,2,1,0:T(4,128)(2,1)S(1)}, bf16[32,2,8,4,128]{4,3,2,1,0:T(4,128)(2,1)S(1)}, u32[]{:S(2)}, u32[]{:S(2)}) collective-permute-start(bf16[32,2,8,4,128]{4,3,2,1,0:T(4,128)(2,1)S(1)} %all_to_all.15.refs_0_), channel_id=1, source_target_pairs={{0,64},{32,224},{64,0},{96,160},{128,192},{160,96},{192,128},{224,... | collective-permute-start | bytes 1572872 | tf_op jit(solution)/shard_map/ppermute | solution.py:279
  34.1 2.9 %collective-permute-start.2 = (bf16[32,2,8,4,128]{4,3,2,1,0:T(4,128)(2,1)S(1)}, bf16[32,2,8,4,128]{4,3,2,1,0:T(4,128)(2,1)S(1)}, u32[]{:S(2)}, u32[]{:S(2)}) collective-permute-start(bf16[32,2,8,4,128]{4,3,2,1,0:T(4,128)(2,1)S(1)} %all_to_all.15.refs_0_), channel_id=1, source_target_pairs={{0,32},{32,0},{1,33},{33,1},{2,34},{34,2},{3,35},{35,3},{4,36},{36... | collective-permute-start | bytes 1572872 | tf_op jit(solution)/shard_map/ppermute | solution.py:268
  37.0 3.7 %collective-permute-done.1.refs_1_ = bf16[32,2,8,4,128]{4,3,2,1,0:T(4,128)(2,1)S(1)} collective-permute-done((bf16[32,2,8,4,128]{4,3,2,1,0:T(4,128)(2,1)S(1)}, bf16[32,2,8,4,128]{4,3,2,1,0:T(4,128)(2,1)S(1)}, u32[]{:S(2)}, u32[]{:S(2)}) %collective-permute-start.1) | collective-permute-done | bytes 524320 | tf_op jit(solution)/shard_map/ppermute | solution.py:279
  40.7 0.0 copy-start.1
  40.7 3.9 %collective-permute-start.3 = (bf16[32,2,8,4,128]{4,3,2,1,0:T(4,128)(2,1)S(1)}, bf16[32,2,8,4,128]{4,3,2,1,0:T(4,128)(2,1)S(1)}, u32[]{:S(2)}, u32[]{:S(2)}) collective-permute-start(bf16[32,2,8,4,128]{4,3,2,1,0:T(4,128)(2,1)S(1)} %collective-permute-done.1.refs_1_), channel_id=1, source_target_pairs={{0,32},{32,0},{1,33},{33,1},{2,34},{34,2},{3,35},{35,3},{4,36},{36... | collective-permute-start | bytes 1572872 | tf_op jit(solution)/shard_map/ppermute | solution.py:268
  44.6 0.0 collective-permute-done.2.refs_2_
  44.6 0.0 copy-start.2
  44.6 1.5 %collective-permute-done.3.refs_3_ = bf16[32,2,8,4,128]{4,3,2,1,0:T(4,128)(2,1)S(1)} collective-permute-done((bf16[32,2,8,4,128]{4,3,2,1,0:T(4,128)(2,1)S(1)}, bf16[32,2,8,4,128]{4,3,2,1,0:T(4,128)(2,1)S(1)}, u32[]{:S(2)}, u32[]{:S(2)}) %collective-permute-start.3) | collective-permute-done | bytes 524320 | tf_op jit(solution)/shard_map/ppermute | solution.py:268
  46.2 0.0 copy-done
  46.2 0.0 copy-done.1
  46.2 0.0 copy-done.2
  46.2 0.0 copy-start.3
  46.2 0.8 copy-done.3
  47.0 6.7 %blocks.1 = bf16[32,17,4,128]{3,2,1,0:T(4,128)(2,1)} custom-call(s32[16]{0:T(128)} %owner.1, s32[16]{0:T(128)} %fill.1, bf16[16,128,1024]{2,1,0:T(8,128)(2,1)} %k_hbm.1, bf16[16,128,1024]{2,1,0:T(8,128)(2,1)} %v_hbm.1, bf16[32,2,8,4,128]{4,3,2,1,0:T(4,128)(2,1)} %copy-done, bf16[32,2,8,4,128]{4,3,2,1,0:T(4,128)(2,1)} %copy-done.1, ...), custom_call_target="tpu_custom_call" | custom-call | flops 134217728 | bytes 9437184 | tf_op jit(solution)/shard_map/blocks/pallas_call | solution.py:129
  53.7 4.3 %all-to-all-start.1 = ((bf16[32,17,4,128]{3,2,1,0:T(4,128)(2,1)}), bf16[32,17,4,128]{3,2,1,0:T(4,128)(2,1)S(1)}, u32[]{:S(2)}, u32[]{:S(2)}) async-start(bf16[32,17,4,128]{3,2,1,0:T(4,128)(2,1)} %blocks.1), calls=%async_computation.1 | async-start | bytes 1114112 | tf_op jit(solution)/shard_map/all_to_all | solution.py:284
  58.0 1.4 %fresh.1 = f32[5,8,128]{2,1,0:T(8,128)} custom-call(s32[1]{0:T(128)} %bitcast.6.kv, bf16[2,8,256]{2,1,0:T(8,128)(2,1)} %q_ref.1, bf16[2,8,1024]{2,1,0:T(8,128)(2,1)} %keys_ref.1, bf16[2,8,1024]{2,1,0:T(8,128)(2,1)} %values_ref.1), custom_call_target="tpu_custom_call" | custom-call | flops 131072 | bytes 65536 | tf_op jit(solution)/shard_map/fresh/pallas_call | solution.py:210
  59.4 15.6 %all-to-all-done.1 = bf16[32,17,4,128]{3,2,1,0:T(4,128)(2,1)S(1)} async-done(((bf16[32,17,4,128]{3,2,1,0:T(4,128)(2,1)}), bf16[32,17,4,128]{3,2,1,0:T(4,128)(2,1)S(1)}, u32[]{:S(2)}, u32[]{:S(2)}) %all-to-all-start.1) | async-done | bytes 557088 | tf_op jit(solution)/shard_map/all_to_all | solution.py:284
  75.0 0.1 copy.27
  75.2 0.2 copy.28
  75.5 0.1 copy.29
  75.6 0.1 add.51
  75.7 0.3 reshape.110
  76.0 0.1 copy.32
  76.1 0.1 add.55
  76.2 0.1 select_reduce_fusion
  76.4 0.3 fusion.5
  76.7 0.1 copy.34
  76.8 0.1 copy.35
  76.9 0.3 fusion.8
  77.3 0.4 fusion.1
  77.8 12.3 %all_to_all.16.got = f32[8,5,8,128]{3,2,1,0:T(8,128)} all-to-all(f32[8,5,8,128]{3,2,1,0:T(8,128)S(1)} %pad_maximum_fusion), channel_id=1, replica_groups=mesh['y'=4,'core'=2,'z'=8,'x'=4] {'y','core'}, dimensions={0} | all-to-all | bytes 327680 | tf_op jit(solution)/shard_map/all_to_all | solution.py:290
  90.1 1.7 %finish.1 = bf16[2,8,256]{2,1,0:T(8,128)(2,1)} custom-call(f32[8,5,8,128]{3,2,1,0:T(8,128)} %all_to_all.16.got, f32[5,8,128]{2,1,0:T(8,128)} %fresh.1), custom_call_target="tpu_custom_call" | custom-call | tf_op jit(solution)/shard_map/finish/pallas_call | solution.py:251
  (11 shorter events, 0.2 us)
Async XLA Ops:
  0.7 4.8 %collective-permute-start = (bf16[8,4,128]{2,1,0:T(4,128)(2,1)S(1)}, bf16[8,4,128]{2,1,0:T(4,128)(2,1)S(1)}, u32[]{:S(2)}, u32[]{:S(2)}) collective-permute-start(bf16[8,4,128]{2,1,0:T(4,128)(2,1)S(1)} %bitcast.35), channel_id=1, source_target_pairs={{0,128},{64,192},{128,0},{192,64},{1,129},{65,193},{129,1},{193,65... | collective-permute-start | bytes 24584 | tf_op jit(solution)/shard_map/ppermute | solution.py:268
  31.4 14.8 %copy-start = (bf16[32,2,8,4,128]{4,3,2,1,0:T(4,128)(2,1)}, bf16[32,2,8,4,128]{4,3,2,1,0:T(4,128)(2,1)S(1)}, u32[]{:S(2)}) copy-start(bf16[32,2,8,4,128]{4,3,2,1,0:T(4,128)(2,1)S(1)} %all_to_all.15.refs_0_) | copy-start | bytes 1572868
  31.4 9.3 %collective-permute-start.1 = (bf16[32,2,8,4,128]{4,3,2,1,0:T(4,128)(2,1)S(1)}, bf16[32,2,8,4,128]{4,3,2,1,0:T(4,128)(2,1)S(1)}, u32[]{:S(2)}, u32[]{:S(2)}) collective-permute-start(bf16[32,2,8,4,128]{4,3,2,1,0:T(4,128)(2,1)S(1)} %all_to_all.15.refs_0_), channel_id=1, source_target_pairs={{0,64},{32,224},{64,0},{96,160},{128,192},{160,96},{192,128},{224,... | collective-permute-start | bytes 1572872 | tf_op jit(solution)/shard_map/ppermute | solution.py:279
  34.1 10.5 %collective-permute-start.2 = (bf16[32,2,8,4,128]{4,3,2,1,0:T(4,128)(2,1)S(1)}, bf16[32,2,8,4,128]{4,3,2,1,0:T(4,128)(2,1)S(1)}, u32[]{:S(2)}, u32[]{:S(2)}) collective-permute-start(bf16[32,2,8,4,128]{4,3,2,1,0:T(4,128)(2,1)S(1)} %all_to_all.15.refs_0_), channel_id=1, source_target_pairs={{0,32},{32,0},{1,33},{33,1},{2,34},{34,2},{3,35},{35,3},{4,36},{36... | collective-permute-start | bytes 1572872 | tf_op jit(solution)/shard_map/ppermute | solution.py:268
  40.7 5.5 %copy-start.1 = (bf16[32,2,8,4,128]{4,3,2,1,0:T(4,128)(2,1)}, bf16[32,2,8,4,128]{4,3,2,1,0:T(4,128)(2,1)S(1)}, u32[]{:S(2)}) copy-start(bf16[32,2,8,4,128]{4,3,2,1,0:T(4,128)(2,1)S(1)} %collective-permute-done.1.refs_1_) | copy-start | bytes 1572868
  40.7 5.5 %collective-permute-start.3 = (bf16[32,2,8,4,128]{4,3,2,1,0:T(4,128)(2,1)S(1)}, bf16[32,2,8,4,128]{4,3,2,1,0:T(4,128)(2,1)S(1)}, u32[]{:S(2)}, u32[]{:S(2)}) collective-permute-start(bf16[32,2,8,4,128]{4,3,2,1,0:T(4,128)(2,1)S(1)} %collective-permute-done.1.refs_1_), channel_id=1, source_target_pairs={{0,32},{32,0},{1,33},{33,1},{2,34},{34,2},{3,35},{35,3},{4,36},{36... | collective-permute-start | bytes 1572872 | tf_op jit(solution)/shard_map/ppermute | solution.py:268
  44.6 1.5 %copy-start.2 = (bf16[32,2,8,4,128]{4,3,2,1,0:T(4,128)(2,1)}, bf16[32,2,8,4,128]{4,3,2,1,0:T(4,128)(2,1)S(1)}, u32[]{:S(2)}) copy-start(bf16[32,2,8,4,128]{4,3,2,1,0:T(4,128)(2,1)S(1)} %collective-permute-done.2.refs_2_) | copy-start | bytes 1572868
  46.2 0.8 copy-start.3
  53.7 21.3 %all-to-all-start.1 = ((bf16[32,17,4,128]{3,2,1,0:T(4,128)(2,1)}), bf16[32,17,4,128]{3,2,1,0:T(4,128)(2,1)S(1)}, u32[]{:S(2)}, u32[]{:S(2)}) async-start(bf16[32,17,4,128]{3,2,1,0:T(4,128)(2,1)} %blocks.1), calls=%async_computation.1 | async-start | bytes 1114112 | tf_op jit(solution)/shard_map/all_to_all | solution.py:284

commit v4 on v2

--- a/solution.py
+++ b/solution.py
@@ -1,3 +1,4 @@
+import math
 import jax
 import jax.numpy as jnp
 from jax import lax
@@ -38,7 +39,8 @@
     def fetch(b):
         home = owner[b] // rows
         row = lax.rem(owner[b], rows)
-        which = (home // n_core ^ here_y) + (lax.rem(home, n_core) ^ here_core) * n_y
+        away = home // n_core ^ here_y
+        which = lax.rem(n_y - away, n_y) + (lax.rem(home, n_core) ^ here_core) * n_y
         for p, piece in enumerate(pieces):
 
             @pl.when(which == p)
@@ -60,28 +62,22 @@
     lax.fori_loop(0, slots, start, 0)
     stats[...] = jnp.zeros_like(stats)
     slot_at = lax.broadcasted_iota(jnp.int32, (BLK, cols), 0)
-    nothing = jnp.zeros((per, DH), jnp.bfloat16)
+    head = lax.broadcasted_iota(jnp.int32, (DH, cols), 1) // per
 
     def score(b):
-        spread = []
-        for g in range(n_kv):
-            mine = picked[b, g * n_x : (g + 1) * n_x].reshape(per, DH)
-            spread.append(
-                jnp.concatenate([nothing] * g + [mine] + [nothing] * (n_kv - 1 - g), axis=1)
-            )
-        scores = lax.dot_general(
-            k_all[b],
-            jnp.concatenate(spread, axis=0),
-            (((1,), (1,)), ((), ())),
-            preferred_element_type=jnp.float32,
+        query = picked[b].reshape(cols, DH).T
+        nothing = jnp.zeros_like(query)
+        spread = [jnp.where(head == g, query, nothing) for g in range(n_kv)]
+        scores = jnp.dot(
+            k_all[b], jnp.concatenate(spread, axis=0), preferred_element_type=jnp.float32
         )
-        return jnp.where(slot_at < fill[b], scores * SCALE, far_below)
+        return jnp.where(slot_at < fill[b], scores, far_below)
 
     def soften(b, scores):
         peak = jnp.max(scores, axis=0, keepdims=True)
-        chances = jnp.exp(scores - peak)
+        chances = jnp.exp2((scores - peak) * (SCALE * math.log2(math.e)))
         total = jnp.sum(chances, axis=0, keepdims=True)
-        for p, piece in enumerate(split_three(peak) + split_three(total)):
+        for p, piece in enumerate(split_three(peak * SCALE) + split_three(total)):
             stats[pl.ds(p * slots + b, 1)] = piece.astype(jnp.float32)
         stats[pl.ds(6 * slots + b, 1)] = jnp.broadcast_to(owner[b].astype(jnp.float32), (1, cols))
         return chances.astype(jnp.bfloat16).T
@@ -145,13 +141,17 @@
     n_cols = got.shape[2]
     every = n_src * (slots + 1)
     out = got.reshape(every, n_cols, DH)
-    stats = got[:, slots, :, : 7 * slots].astype(jnp.float32)
-    stats = stats.reshape(n_src, n_cols, 7, slots).transpose(2, 1, 0, 3)
-    stats = jnp.pad(stats, ((0, 0), (0, 0), (0, 0), (0, 1)), constant_values=-1.0)
-    stats = stats.reshape(7, n_cols, every)
-    peak = stats[0] + stats[1] + stats[2]
-    total = stats[3] + stats[4] + stats[5]
-    owner = stats[6, 0].astype(jnp.int32)
+    stats = got[:, slots]
+
+    def three(first):
+        pieces = [stats[:, :, (first + p) * slots : (first + p + 1) * slots] for p in range(3)]
+        hi, mid, lo = [piece.astype(jnp.float32) for piece in pieces]
+        value = jnp.pad(hi + mid + lo, ((0, 0), (0, 0), (0, 1)))
+        return value.transpose(1, 0, 2).reshape(n_cols, every)
+
+    peak, total = three(0), three(3)
+    owner = stats[:, 0, 6 * slots : 7 * slots].astype(jnp.int32)
+    owner = jnp.pad(owner, ((0, 0), (0, 1)), constant_values=-1).reshape(every)
     hot = owner[None, :] == jnp.arange(requests, dtype=jnp.int32)[:, None]
     masked = jnp.where(hot[None], peak[:, None, :], far_below)
     top = jnp.max(masked, axis=-1, keepdims=True)
@@ -264,7 +264,7 @@
     own = lax.all_to_all(
         jnp.broadcast_to(rows[None], (n_z * n_x,) + rows.shape), ("z", "x"), 0, 0, tiled=True
     )
-    pieces = [own] + [from_other(own, "y", m) for m in range(1, n_y)]
+    pieces = [own] + [from_other(own, "y", m) for m in range(n_y - 1, 0, -1)]
     pieces = pieces + [from_other(p, "core", 1) for p in pieces]
     sent = blocks(pieces, k_cache, v_cache, block_req, block_fill, n_z * n_x)
     kv = lax.axis_index("z").astype(jnp.int32).reshape(1)

time: 89 us -> 87.1 us (0.979)
  starting transfers between devices: 22.2 us -> 13.7 us
  waiting for transfers between devices: 18.8 us -> 24.2 us
  blocking collectives: 33.8 us -> 35 us
    ppermute x7, starting transfers between devices: 17.4 us -> 8.76 us  [from_other(): lax.ppermute(value, axis, [(j, j ^ m) for j in range(lax.axis_size(axis))])]
    ppermute x7, waiting for transfers between devices: 3.16 us -> 8.61 us  [from_other(): lax.ppermute(value, axis, [(j, j ^ m) for j in range(lax.axis_size(axis))])]
    all_to_all x1, blocking collectives: 10.9 us -> 12.1 us  [body(): lax.all_to_all(jnp.concatenate([part, level], axis=1), ('y', 'core'), 0,...]
where the time goes in v4:
time: 87.1 us; the launch traced here: 86.7 us
  blocking collectives  35 us (40%)
  waiting for transfers between devices  24.2 us (28%)
  starting transfers between devices  13.7 us (16%)
  Pallas kernels  9.63 us (11%)
  local copies, waits for them, and re-layouts  2.59 us (3%)
    all_to_all x1, blocking collectives, body(): lax.all_to_all(jnp.broadcast_to(rows[None], (n_z * n_x,) + rows.shape), (...  22.9 us
    all_to_all x1, waiting for transfers between devices, body(): lax.all_to_all(sent, ('z', 'x'), split_axis=0, concat_axis=0, tiled=True)  15.6 us
    all_to_all x1, blocking collectives, body(): lax.all_to_all(jnp.concatenate([part, level], axis=1), ('y', 'core'), 0,...  12.1 us
    ppermute x7, starting transfers between devices, from_other(): lax.ppermute(value, axis, [(j, j ^ m) for j in range(lax.axis_size(axis))])  8.76 us
    ppermute x7, waiting for transfers between devices, from_other(): lax.ppermute(value, axis, [(j, j ^ m) for j in range(lax.axis_size(axis))])  8.61 us
    pallas_call x1, Pallas kernels, blocks(): pl.pallas_call(block_kernel, out_shape=jax.ShapeDtypeStruct((n_tp, slots...  6.54 us
    all_to_all x1, starting transfers between devices, body(): lax.all_to_all(sent, ('z', 'x'), split_axis=0, concat_axis=0, tiled=True)  4.93 us
  transfers between devices with their start and end apart: 8, of which 4 were waited for; matrix products, arithmetic and copies ran while one was open for 0% of the time, Pallas kernels for 2%

profile of v4, /device:TPU:1, one launch (start us, length us, event | category | flops | bytes accessed | tf_op | source)
XLA Modules:
  0.0 86.7 jit_solution(1174591398767379605)
XLA Ops:
  0.0 0.7 copy.23
  0.7 0.1 broadcast_in_dim.57
  0.8 22.9 %all_to_all.15.refs_0_ = bf16[32,8,4,128]{3,2,1,0:T(4,128)(2,1)S(1)} all-to-all(bf16[32,8,4,128]{3,2,1,0:T(4,128)(2,1)S(1)} %broadcast_in_dim.57), channel_id=1, replica_groups=mesh['y'=4,'core'=2,'z'=8,'x'=4] {'z','x'}, dimensions={0} | all-to-all | bytes 524288 | tf_op jit(solution)/shard_map/all_to_all | solution.py:264
  23.6 0.0 copy-start
  23.6 2.7 %collective-permute-start = (bf16[32,8,4,128]{3,2,1,0:T(4,128)(2,1)S(1)}, bf16[32,8,4,128]{3,2,1,0:T(4,128)(2,1)S(1)}, u32[]{:S(2)}, u32[]{:S(2)}) collective-permute-start(bf16[32,8,4,128]{3,2,1,0:T(4,128)(2,1)S(1)} %all_to_all.15.refs_0_), channel_id=1, source_target_pairs={{0,192},{64,128},{128,64},{192,0},{1,193},{65,129},{129,65},{193,1... | collective-permute-start | bytes 786440 | tf_op jit(solution)/shard_map/ppermute | solution.py:260
  26.4 0.3 collective-permute-start.1
  26.7 0.2 collective-permute-start.2
  27.0 3.2 %collective-permute-start.3 = (bf16[32,8,4,128]{3,2,1,0:T(4,128)(2,1)S(1)}, bf16[32,8,4,128]{3,2,1,0:T(4,128)(2,1)S(1)}, u32[]{:S(2)}, u32[]{:S(2)}) collective-permute-start(bf16[32,8,4,128]{3,2,1,0:T(4,128)(2,1)S(1)} %all_to_all.15.refs_0_), channel_id=1, source_target_pairs={{0,32},{32,0},{1,33},{33,1},{2,34},{34,2},{3,35},{35,3},{4,36},{36... | collective-permute-start | bytes 786440 | tf_op jit(solution)/shard_map/ppermute | solution.py:260
  30.2 7.5 %collective-permute-done.refs_1_ = bf16[32,8,4,128]{3,2,1,0:T(4,128)(2,1)S(1)} collective-permute-done((bf16[32,8,4,128]{3,2,1,0:T(4,128)(2,1)S(1)}, bf16[32,8,4,128]{3,2,1,0:T(4,128)(2,1)S(1)}, u32[]{:S(2)}, u32[]{:S(2)}) %collective-permute-start) | collective-permute-done | bytes 262176 | tf_op jit(solution)/shard_map/ppermute | solution.py:260
  37.6 0.0 copy-start.1
  37.6 1.1 %collective-permute-start.4 = (bf16[32,8,4,128]{3,2,1,0:T(4,128)(2,1)S(1)}, bf16[32,8,4,128]{3,2,1,0:T(4,128)(2,1)S(1)}, u32[]{:S(2)}, u32[]{:S(2)}) collective-permute-start(bf16[32,8,4,128]{3,2,1,0:T(4,128)(2,1)S(1)} %collective-permute-done.refs_1_), channel_id=1, source_target_pairs={{0,32},{32,0},{1,33},{33,1},{2,34},{34,2},{3,35},{35,3},{4,36},{36... | collective-permute-start | bytes 786440 | tf_op jit(solution)/shard_map/ppermute | solution.py:260
  38.7 0.0 collective-permute-done.1.refs_2_
  38.7 0.0 copy-start.2
  38.7 0.7 collective-permute-start.5
  39.5 0.0 collective-permute-done.2.refs_3_
  39.5 0.4 collective-permute-start.6
  39.9 0.0 collective-permute-done.3.refs_4_
  39.9 0.0 collective-permute-done.4.refs_5_
  39.9 0.0 copy-start.5
  39.9 0.7 collective-permute-done.5.refs_6_
  40.6 0.4 collective-permute-done.6.refs_7_
  41.0 0.0 copy-done
  41.0 0.0 copy-done.1
  41.0 0.0 copy-done.2
  41.0 0.0 copy-done.3
  41.0 0.0 copy-done.4
  41.1 0.0 copy-done.5
  41.1 0.2 copy-done.6
  41.3 0.7 copy-done.7
  42.0 6.5 %blocks.1 = bf16[32,17,4,128]{3,2,1,0:T(4,128)(2,1)} custom-call(s32[16]{0:T(128)} %owner.1, s32[16]{0:T(128)} %fill.1, bf16[16,128,1024]{2,1,0:T(8,128)(2,1)} %k_hbm.1, bf16[16,128,1024]{2,1,0:T(8,128)(2,1)} %v_hbm.1, bf16[32,8,4,128]{3,2,1,0:T(4,128)(2,1)} %copy-done, bf16[32,8,4,128]{3,2,1,0:T(4,128)(2,1)} %copy-done.1, ...), custom_call_target="tpu_custom_call" | custom-call | flops 134217728 | bytes 9437184 | tf_op jit(solution)/shard_map/blocks/pallas_call | solution.py:117
  48.6 4.9 %all-to-all-start.1 = ((bf16[32,17,4,128]{3,2,1,0:T(4,128)(2,1)}), bf16[32,17,4,128]{3,2,1,0:T(4,128)(2,1)S(1)}, u32[]{:S(2)}, u32[]{:S(2)}) async-start(bf16[32,17,4,128]{3,2,1,0:T(4,128)(2,1)} %blocks.1), calls=%async_computation.1 | async-start | bytes 1114112 | tf_op jit(solution)/shard_map/all_to_all | solution.py:272
  53.5 1.4 %fresh.1 = f32[5,8,128]{2,1,0:T(8,128)} custom-call(s32[1]{0:T(128)} %bitcast.3.kv, bf16[2,8,256]{2,1,0:T(8,128)(2,1)} %q_ref.1, bf16[2,8,1024]{2,1,0:T(8,128)(2,1)} %keys_ref.1, bf16[2,8,1024]{2,1,0:T(8,128)(2,1)} %values_ref.1), custom_call_target="tpu_custom_call" | custom-call | flops 131072 | bytes 65536 | tf_op jit(solution)/shard_map/fresh/pallas_call | solution.py:202
  54.9 15.6 %all-to-all-done.1 = bf16[32,17,4,128]{3,2,1,0:T(4,128)(2,1)S(1)} async-done(((bf16[32,17,4,128]{3,2,1,0:T(4,128)(2,1)}), bf16[32,17,4,128]{3,2,1,0:T(4,128)(2,1)S(1)}, u32[]{:S(2)}, u32[]{:S(2)}) %all-to-all-start.1) | async-done | bytes 557088 | tf_op jit(solution)/shard_map/all_to_all | solution.py:272
  70.6 0.2 convert_add_fusion
  70.7 0.1 slice.32
  70.9 0.1 broadcast_in_dim.59
  71.0 0.1 copy.24
  71.1 0.1 copy.25
  71.2 0.1 reshape.60
  71.3 0.1 mul.10
  71.4 0.1 select_reduce_fusion
  71.6 0.3 fusion.5
  71.9 0.1 copy.31
  72.0 0.1 copy.32
  72.1 0.3 fusion.8
  72.5 0.4 fusion.1
  72.9 12.1 %all_to_all.16.got = f32[8,5,8,128]{3,2,1,0:T(8,128)} all-to-all(f32[8,5,8,128]{3,2,1,0:T(8,128)S(1)} %pad_maximum_fusion), channel_id=1, replica_groups=mesh['y'=4,'core'=2,'z'=8,'x'=4] {'y','core'}, dimensions={0} | all-to-all | bytes 327680 | tf_op jit(solution)/shard_map/all_to_all | solution.py:278
  85.0 1.7 %finish.1 = bf16[2,8,256]{2,1,0:T(8,128)(2,1)} custom-call(f32[8,5,8,128]{3,2,1,0:T(8,128)} %all_to_all.16.got, f32[5,8,128]{2,1,0:T(8,128)} %fresh.1), custom_call_target="tpu_custom_call" | custom-call | tf_op jit(solution)/shard_map/finish/pallas_call | solution.py:243
  (15 shorter events, 0.2 us)
Async XLA Ops:
  23.6 17.4 %copy-start = (bf16[32,8,4,128]{3,2,1,0:T(4,128)(2,1)}, bf16[32,8,4,128]{3,2,1,0:T(4,128)(2,1)S(1)}, u32[]{:S(2)}) copy-start(bf16[32,8,4,128]{3,2,1,0:T(4,128)(2,1)S(1)} %all_to_all.15.refs_0_) | copy-start | bytes 786436
  23.6 14.0 %collective-permute-start = (bf16[32,8,4,128]{3,2,1,0:T(4,128)(2,1)S(1)}, bf16[32,8,4,128]{3,2,1,0:T(4,128)(2,1)S(1)}, u32[]{:S(2)}, u32[]{:S(2)}) collective-permute-start(bf16[32,8,4,128]{3,2,1,0:T(4,128)(2,1)S(1)} %all_to_all.15.refs_0_), channel_id=1, source_target_pairs={{0,192},{64,128},{128,64},{192,0},{1,193},{65,129},{129,65},{193,1... | collective-permute-start | bytes 786440 | tf_op jit(solution)/shard_map/ppermute | solution.py:260
  26.4 12.4 %collective-permute-start.1 = (bf16[32,8,4,128]{3,2,1,0:T(4,128)(2,1)S(1)}, bf16[32,8,4,128]{3,2,1,0:T(4,128)(2,1)S(1)}, u32[]{:S(2)}, u32[]{:S(2)}) collective-permute-start(bf16[32,8,4,128]{3,2,1,0:T(4,128)(2,1)S(1)} %all_to_all.15.refs_0_), channel_id=1, source_target_pairs={{0,128},{64,192},{128,0},{192,64},{1,129},{65,193},{129,1},{193,65... | collective-permute-start | bytes 786440 | tf_op jit(solution)/shard_map/ppermute | solution.py:260
  26.7 12.7 %collective-permute-start.2 = (bf16[32,8,4,128]{3,2,1,0:T(4,128)(2,1)S(1)}, bf16[32,8,4,128]{3,2,1,0:T(4,128)(2,1)S(1)}, u32[]{:S(2)}, u32[]{:S(2)}) collective-permute-start(bf16[32,8,4,128]{3,2,1,0:T(4,128)(2,1)S(1)} %all_to_all.15.refs_0_), channel_id=1, source_target_pairs={{0,64},{64,0},{128,192},{192,128},{1,65},{65,1},{129,193},{193,129... | collective-permute-start | bytes 786440 | tf_op jit(solution)/shard_map/ppermute | solution.py:260
  27.0 12.9 %collective-permute-start.3 = (bf16[32,8,4,128]{3,2,1,0:T(4,128)(2,1)S(1)}, bf16[32,8,4,128]{3,2,1,0:T(4,128)(2,1)S(1)}, u32[]{:S(2)}, u32[]{:S(2)}) collective-permute-start(bf16[32,8,4,128]{3,2,1,0:T(4,128)(2,1)S(1)} %all_to_all.15.refs_0_), channel_id=1, source_target_pairs={{0,32},{32,0},{1,33},{33,1},{2,34},{34,2},{3,35},{35,3},{4,36},{36... | collective-permute-start | bytes 786440 | tf_op jit(solution)/shard_map/ppermute | solution.py:260
  37.6 3.4 %copy-start.1 = (bf16[32,8,4,128]{3,2,1,0:T(4,128)(2,1)}, bf16[32,8,4,128]{3,2,1,0:T(4,128)(2,1)S(1)}, u32[]{:S(2)}) copy-start(bf16[32,8,4,128]{3,2,1,0:T(4,128)(2,1)S(1)} %collective-permute-done.refs_1_) | copy-start | bytes 786436
  37.6 2.2 %collective-permute-start.4 = (bf16[32,8,4,128]{3,2,1,0:T(4,128)(2,1)S(1)}, bf16[32,8,4,128]{3,2,1,0:T(4,128)(2,1)S(1)}, u32[]{:S(2)}, u32[]{:S(2)}) collective-permute-start(bf16[32,8,4,128]{3,2,1,0:T(4,128)(2,1)S(1)} %collective-permute-done.refs_1_), channel_id=1, source_target_pairs={{0,32},{32,0},{1,33},{33,1},{2,34},{34,2},{3,35},{35,3},{4,36},{36... | collective-permute-start | bytes 786440 | tf_op jit(solution)/shard_map/ppermute | solution.py:260
  38.7 2.3 %copy-start.2 = (bf16[32,8,4,128]{3,2,1,0:T(4,128)(2,1)}, bf16[32,8,4,128]{3,2,1,0:T(4,128)(2,1)S(1)}, u32[]{:S(2)}) copy-start(bf16[32,8,4,128]{3,2,1,0:T(4,128)(2,1)S(1)} %collective-permute-done.1.refs_2_) | copy-start | bytes 786436
  38.7 1.9 %collective-permute-start.5 = (bf16[32,8,4,128]{3,2,1,0:T(4,128)(2,1)S(1)}, bf16[32,8,4,128]{3,2,1,0:T(4,128)(2,1)S(1)}, u32[]{:S(2)}, u32[]{:S(2)}) collective-permute-start(bf16[32,8,4,128]{3,2,1,0:T(4,128)(2,1)S(1)} %collective-permute-done.1.refs_2_), channel_id=1, source_target_pairs={{0,32},{32,0},{1,33},{33,1},{2,34},{34,2},{3,35},{35,3},{4,36},{36... | collective-permute-start | bytes 786440 | tf_op jit(solution)/shard_map/ppermute | solution.py:260
  39.5 1.6 %copy-start.3 = (bf16[32,8,4,128]{3,2,1,0:T(4,128)(2,1)}, bf16[32,8,4,128]{3,2,1,0:T(4,128)(2,1)S(1)}, u32[]{:S(2)}) copy-start(bf16[32,8,4,128]{3,2,1,0:T(4,128)(2,1)S(1)} %collective-permute-done.2.refs_3_) | copy-start | bytes 786436
  39.5 1.6 %collective-permute-start.6 = (bf16[32,8,4,128]{3,2,1,0:T(4,128)(2,1)S(1)}, bf16[32,8,4,128]{3,2,1,0:T(4,128)(2,1)S(1)}, u32[]{:S(2)}, u32[]{:S(2)}) collective-permute-start(bf16[32,8,4,128]{3,2,1,0:T(4,128)(2,1)S(1)} %collective-permute-done.2.refs_3_), channel_id=1, source_target_pairs={{0,32},{32,0},{1,33},{33,1},{2,34},{34,2},{3,35},{35,3},{4,36},{36... | collective-permute-start | bytes 786440 | tf_op jit(solution)/shard_map/ppermute | solution.py:260
  39.9 1.2 %copy-start.4 = (bf16[32,8,4,128]{3,2,1,0:T(4,128)(2,1)}, bf16[32,8,4,128]{3,2,1,0:T(4,128)(2,1)S(1)}, u32[]{:S(2)}) copy-start(bf16[32,8,4,128]{3,2,1,0:T(4,128)(2,1)S(1)} %collective-permute-done.3.refs_4_) | copy-start | bytes 786436
  39.9 1.2 %copy-start.5 = (bf16[32,8,4,128]{3,2,1,0:T(4,128)(2,1)}, bf16[32,8,4,128]{3,2,1,0:T(4,128)(2,1)S(1)}, u32[]{:S(2)}) copy-start(bf16[32,8,4,128]{3,2,1,0:T(4,128)(2,1)S(1)} %collective-permute-done.4.refs_5_) | copy-start | bytes 786436
  40.6 0.7 copy-start.6
  41.3 0.7 copy-start.7
  48.6 22.0 %all-to-all-start.1 = ((bf16[32,17,4,128]{3,2,1,0:T(4,128)(2,1)}), bf16[32,17,4,128]{3,2,1,0:T(4,128)(2,1)S(1)}, u32[]{:S(2)}, u32[]{:S(2)}) async-start(bf16[32,17,4,128]{3,2,1,0:T(4,128)(2,1)} %blocks.1), calls=%async_computation.1 | async-start | bytes 1114112 | tf_op jit(solution)/shard_map/all_to_all | solution.py:272

commit v5 on v4

--- a/solution.py
+++ b/solution.py
@@ -47,19 +47,27 @@
             def _(piece=piece):
                 pltpu.make_async_copy(piece.at[:, row], picked.at[b], sem.at[2, b]).start()
 
-    def copies(b):
-        return (
-            pltpu.make_async_copy(k_hbm.at[b], k_all.at[b], sem.at[0, b]),
-            pltpu.make_async_copy(v_hbm.at[b], v_all.at[b], sem.at[1, b]),
-        )
+    def keys_of(b):
+        return pltpu.make_async_copy(k_hbm.at[b], k_all.at[b], sem.at[0, b])
+
+    def values_of(b):
+        return pltpu.make_async_copy(v_hbm.at[b], v_all.at[b], sem.at[1, b])
 
     def start(b, _):
+        keys_of(b).start()
         fetch(b)
-        for c in copies(b):
-            c.start()
         return 0
 
-    lax.fori_loop(0, slots, start, 0)
+    def start_values(b, _):
+        values_of(b).start()
+        return 0
+
+    groups = slots // together
+    for g in range(groups):
+        lax.fori_loop(g * together, (g + 1) * together, start, 0)
+        if g:
+            lax.fori_loop((g - 1) * together, g * together, start_values, 0)
+    lax.fori_loop((groups - 1) * together, slots, start_values, 0)
     stats[...] = jnp.zeros_like(stats)
     slot_at = lax.broadcasted_iota(jnp.int32, (BLK, cols), 0)
     head = lax.broadcasted_iota(jnp.int32, (DH, cols), 1) // per
@@ -94,19 +102,29 @@
         mixed = jnp.concatenate(mixed, axis=0)
         out_ref[:, pl.ds(b, 1)] = mixed.reshape(n_tp, 1, cols // n_tp, DH)
 
-    def some_blocks(i, _):
-        first = i * together
+    def weigh(first):
         for j in range(together):
-            for c in copies(first + j):
-                c.wait()
+            keys_of(first + j).wait()
             pltpu.make_async_copy(pieces[0].at[:, 0], picked.at[first + j], sem.at[2, first + j]).wait()
         scores = [score(first + j) for j in range(together)]
-        rounded = [soften(first + j, scores[j]) for j in range(together)]
+        return tuple(soften(first + j, scores[j]) for j in range(together))
+
+    def await_values(first):
+        for j in range(together):
+            values_of(first + j).wait()
+
+    def step(i, rounded):
+        first = i * together
+        await_values(first)
+        later = weigh(first + together)
         for j in range(together):
             mix(first + j, rounded[j])
-        return 0
-
-    lax.fori_loop(0, slots // together, some_blocks, 0)
+        return later
+
+    rounded = lax.fori_loop(0, groups - 1, step, weigh(0))
+    await_values(slots - together)
+    for j in range(together):
+        mix(slots - together + j, rounded[j])
     packed = stats[...].T.astype(jnp.bfloat16)
     out_ref[:, pl.ds(slots, 1)] = packed.reshape(n_tp, 1, cols // n_tp, DH)
 

time: 87.1 us -> 86.7 us (level)
  no operation moved by 1% of the time
where the time goes in v5:
time: 86.7 us; the launch traced here: 86.4 us
  blocking collectives  34.9 us (40%)
  waiting for transfers between devices  24.2 us (28%)
  starting transfers between devices  13.7 us (16%)
  Pallas kernels  9.29 us (11%)
  local copies, waits for them, and re-layouts  2.59 us (3%)
    all_to_all x1, blocking collectives, body(): lax.all_to_all(jnp.broadcast_to(rows[None], (n_z * n_x,) + rows.shape), (...  22.9 us
    all_to_all x1, waiting for transfers between devices, body(): lax.all_to_all(sent, ('z', 'x'), split_axis=0, concat_axis=0, tiled=True)  15.6 us
    all_to_all x1, blocking collectives, body(): lax.all_to_all(jnp.concatenate([part, level], axis=1), ('y', 'core'), 0,...  12.1 us
    ppermute x7, starting transfers between devices, from_other(): lax.ppermute(value, axis, [(j, j ^ m) for j in range(lax.axis_size(axis))])  8.76 us
    ppermute x7, waiting for transfers between devices, from_other(): lax.ppermute(value, axis, [(j, j ^ m) for j in range(lax.axis_size(axis))])  8.61 us
    pallas_call x1, Pallas kernels, blocks(): pl.pallas_call(block_kernel, out_shape=jax.ShapeDtypeStruct((n_tp, slots...  6.19 us
    all_to_all x1, starting transfers between devices, body(): lax.all_to_all(sent, ('z', 'x'), split_axis=0, concat_axis=0, tiled=True)  4.96 us
  transfers between devices with their start and end apart: 8, of which 4 were waited for; matrix products, arithmetic and copies ran while one was open for 0% of the time, Pallas kernels for 2%

profile of v5, /device:TPU:1, one launch (start us, length us, event | category | flops | bytes accessed | tf_op | source)
XLA Modules:
  0.0 86.4 jit_solution(6088925187230587217)
XLA Ops:
  0.0 0.7 copy.23
  0.7 0.1 broadcast_in_dim.57
  0.8 22.9 %all_to_all.15.refs_0_ = bf16[32,8,4,128]{3,2,1,0:T(4,128)(2,1)S(1)} all-to-all(bf16[32,8,4,128]{3,2,1,0:T(4,128)(2,1)S(1)} %broadcast_in_dim.57), channel_id=1, replica_groups=mesh['y'=4,'core'=2,'z'=8,'x'=4] {'z','x'}, dimensions={0} | all-to-all | bytes 524288 | tf_op jit(solution)/shard_map/all_to_all | solution.py:282
  23.6 0.0 copy-start
  23.6 2.7 %collective-permute-start = (bf16[32,8,4,128]{3,2,1,0:T(4,128)(2,1)S(1)}, bf16[32,8,4,128]{3,2,1,0:T(4,128)(2,1)S(1)}, u32[]{:S(2)}, u32[]{:S(2)}) collective-permute-start(bf16[32,8,4,128]{3,2,1,0:T(4,128)(2,1)S(1)} %all_to_all.15.refs_0_), channel_id=1, source_target_pairs={{0,192},{64,128},{128,64},{192,0},{1,193},{65,129},{129,65},{193,1... | collective-permute-start | bytes 786440 | tf_op jit(solution)/shard_map/ppermute | solution.py:278
  26.4 0.3 collective-permute-start.1
  26.7 0.2 collective-permute-start.2
  27.0 3.2 %collective-permute-start.3 = (bf16[32,8,4,128]{3,2,1,0:T(4,128)(2,1)S(1)}, bf16[32,8,4,128]{3,2,1,0:T(4,128)(2,1)S(1)}, u32[]{:S(2)}, u32[]{:S(2)}) collective-permute-start(bf16[32,8,4,128]{3,2,1,0:T(4,128)(2,1)S(1)} %all_to_all.15.refs_0_), channel_id=1, source_target_pairs={{0,32},{32,0},{1,33},{33,1},{2,34},{34,2},{3,35},{35,3},{4,36},{36... | collective-permute-start | bytes 786440 | tf_op jit(solution)/shard_map/ppermute | solution.py:278
  30.2 7.5 %collective-permute-done.refs_1_ = bf16[32,8,4,128]{3,2,1,0:T(4,128)(2,1)S(1)} collective-permute-done((bf16[32,8,4,128]{3,2,1,0:T(4,128)(2,1)S(1)}, bf16[32,8,4,128]{3,2,1,0:T(4,128)(2,1)S(1)}, u32[]{:S(2)}, u32[]{:S(2)}) %collective-permute-start) | collective-permute-done | bytes 262176 | tf_op jit(solution)/shard_map/ppermute | solution.py:278
  37.6 0.0 copy-start.1
  37.6 1.1 %collective-permute-start.4 = (bf16[32,8,4,128]{3,2,1,0:T(4,128)(2,1)S(1)}, bf16[32,8,4,128]{3,2,1,0:T(4,128)(2,1)S(1)}, u32[]{:S(2)}, u32[]{:S(2)}) collective-permute-start(bf16[32,8,4,128]{3,2,1,0:T(4,128)(2,1)S(1)} %collective-permute-done.refs_1_), channel_id=1, source_target_pairs={{0,32},{32,0},{1,33},{33,1},{2,34},{34,2},{3,35},{35,3},{4,36},{36... | collective-permute-start | bytes 786440 | tf_op jit(solution)/shard_map/ppermute | solution.py:278
  38.7 0.0 collective-permute-done.1.refs_2_
  38.7 0.0 copy-start.2
  38.7 0.7 collective-permute-start.5
  39.5 0.0 collective-permute-done.2.refs_3_
  39.5 0.4 collective-permute-start.6
  39.9 0.0 collective-permute-done.3.refs_4_
  39.9 0.0 collective-permute-done.4.refs_5_
  39.9 0.0 copy-start.5
  39.9 0.7 collective-permute-done.5.refs_6_
  40.6 0.4 collective-permute-done.6.refs_7_
  41.0 0.0 copy-done
  41.0 0.0 copy-done.1
  41.0 0.0 copy-done.2
  41.0 0.0 copy-done.3
  41.0 0.0 copy-done.4
  41.1 0.0 copy-done.5
  41.1 0.2 copy-done.6
  41.3 0.7 copy-done.7
  42.0 6.2 %blocks.1 = bf16[32,17,4,128]{3,2,1,0:T(4,128)(2,1)} custom-call(s32[16]{0:T(128)} %owner.1, s32[16]{0:T(128)} %fill.1, bf16[16,128,1024]{2,1,0:T(8,128)(2,1)} %k_hbm.1, bf16[16,128,1024]{2,1,0:T(8,128)(2,1)} %v_hbm.1, bf16[32,8,4,128]{3,2,1,0:T(4,128)(2,1)} %copy-done, bf16[32,8,4,128]{3,2,1,0:T(4,128)(2,1)} %copy-done.1, ...), custom_call_target="tpu_custom_call" | custom-call | flops 134217728 | bytes 9437184 | tf_op jit(solution)/shard_map/blocks/pallas_call | solution.py:135
  48.2 5.0 %all-to-all-start.1 = ((bf16[32,17,4,128]{3,2,1,0:T(4,128)(2,1)}), bf16[32,17,4,128]{3,2,1,0:T(4,128)(2,1)S(1)}, u32[]{:S(2)}, u32[]{:S(2)}) async-start(bf16[32,17,4,128]{3,2,1,0:T(4,128)(2,1)} %blocks.1), calls=%async_computation.1 | async-start | bytes 1114112 | tf_op jit(solution)/shard_map/all_to_all | solution.py:290
  53.2 1.4 %fresh.1 = f32[5,8,128]{2,1,0:T(8,128)} custom-call(s32[1]{0:T(128)} %bitcast.3.kv, bf16[2,8,256]{2,1,0:T(8,128)(2,1)} %q_ref.1, bf16[2,8,1024]{2,1,0:T(8,128)(2,1)} %keys_ref.1, bf16[2,8,1024]{2,1,0:T(8,128)(2,1)} %values_ref.1), custom_call_target="tpu_custom_call" | custom-call | flops 131072 | bytes 65536 | tf_op jit(solution)/shard_map/fresh/pallas_call | solution.py:220
  54.6 15.6 %all-to-all-done.1 = bf16[32,17,4,128]{3,2,1,0:T(4,128)(2,1)S(1)} async-done(((bf16[32,17,4,128]{3,2,1,0:T(4,128)(2,1)}), bf16[32,17,4,128]{3,2,1,0:T(4,128)(2,1)S(1)}, u32[]{:S(2)}, u32[]{:S(2)}) %all-to-all-start.1) | async-done | bytes 557088 | tf_op jit(solution)/shard_map/all_to_all | solution.py:290
  70.3 0.2 convert_add_fusion
  70.4 0.1 slice.32
  70.6 0.1 broadcast_in_dim.59
  70.7 0.1 copy.24
  70.8 0.1 copy.25
  70.9 0.1 reshape.60
  71.0 0.1 mul.10
  71.1 0.1 select_reduce_fusion
  71.3 0.3 fusion.5
  71.6 0.1 copy.31
  71.7 0.1 copy.32
  71.8 0.3 fusion.8
  72.1 0.4 fusion.1
  72.6 12.1 %all_to_all.16.got = f32[8,5,8,128]{3,2,1,0:T(8,128)} all-to-all(f32[8,5,8,128]{3,2,1,0:T(8,128)S(1)} %pad_maximum_fusion), channel_id=1, replica_groups=mesh['y'=4,'core'=2,'z'=8,'x'=4] {'y','core'}, dimensions={0} | all-to-all | bytes 327680 | tf_op jit(solution)/shard_map/all_to_all | solution.py:296
  84.7 1.7 %finish.1 = bf16[2,8,256]{2,1,0:T(8,128)(2,1)} custom-call(f32[8,5,8,128]{3,2,1,0:T(8,128)} %all_to_all.16.got, f32[5,8,128]{2,1,0:T(8,128)} %fresh.1), custom_call_target="tpu_custom_call" | custom-call | tf_op jit(solution)/shard_map/finish/pallas_call | solution.py:261
  (15 shorter events, 0.2 us)
Async XLA Ops:
  23.6 17.4 %copy-start = (bf16[32,8,4,128]{3,2,1,0:T(4,128)(2,1)}, bf16[32,8,4,128]{3,2,1,0:T(4,128)(2,1)S(1)}, u32[]{:S(2)}) copy-start(bf16[32,8,4,128]{3,2,1,0:T(4,128)(2,1)S(1)} %all_to_all.15.refs_0_) | copy-start | bytes 786436
  23.6 14.0 %collective-permute-start = (bf16[32,8,4,128]{3,2,1,0:T(4,128)(2,1)S(1)}, bf16[32,8,4,128]{3,2,1,0:T(4,128)(2,1)S(1)}, u32[]{:S(2)}, u32[]{:S(2)}) collective-permute-start(bf16[32,8,4,128]{3,2,1,0:T(4,128)(2,1)S(1)} %all_to_all.15.refs_0_), channel_id=1, source_target_pairs={{0,192},{64,128},{128,64},{192,0},{1,193},{65,129},{129,65},{193,1... | collective-permute-start | bytes 786440 | tf_op jit(solution)/shard_map/ppermute | solution.py:278
  26.4 12.4 %collective-permute-start.1 = (bf16[32,8,4,128]{3,2,1,0:T(4,128)(2,1)S(1)}, bf16[32,8,4,128]{3,2,1,0:T(4,128)(2,1)S(1)}, u32[]{:S(2)}, u32[]{:S(2)}) collective-permute-start(bf16[32,8,4,128]{3,2,1,0:T(4,128)(2,1)S(1)} %all_to_all.15.refs_0_), channel_id=1, source_target_pairs={{0,128},{64,192},{128,0},{192,64},{1,129},{65,193},{129,1},{193,65... | collective-permute-start | bytes 786440 | tf_op jit(solution)/shard_map/ppermute | solution.py:278
  26.7 12.7 %collective-permute-start.2 = (bf16[32,8,4,128]{3,2,1,0:T(4,128)(2,1)S(1)}, bf16[32,8,4,128]{3,2,1,0:T(4,128)(2,1)S(1)}, u32[]{:S(2)}, u32[]{:S(2)}) collective-permute-start(bf16[32,8,4,128]{3,2,1,0:T(4,128)(2,1)S(1)} %all_to_all.15.refs_0_), channel_id=1, source_target_pairs={{0,64},{64,0},{128,192},{192,128},{1,65},{65,1},{129,193},{193,129... | collective-permute-start | bytes 786440 | tf_op jit(solution)/shard_map/ppermute | solution.py:278
  27.0 12.9 %collective-permute-start.3 = (bf16[32,8,4,128]{3,2,1,0:T(4,128)(2,1)S(1)}, bf16[32,8,4,128]{3,2,1,0:T(4,128)(2,1)S(1)}, u32[]{:S(2)}, u32[]{:S(2)}) collective-permute-start(bf16[32,8,4,128]{3,2,1,0:T(4,128)(2,1)S(1)} %all_to_all.15.refs_0_), channel_id=1, source_target_pairs={{0,32},{32,0},{1,33},{33,1},{2,34},{34,2},{3,35},{35,3},{4,36},{36... | collective-permute-start | bytes 786440 | tf_op jit(solution)/shard_map/ppermute | solution.py:278
  37.6 3.4 %copy-start.1 = (bf16[32,8,4,128]{3,2,1,0:T(4,128)(2,1)}, bf16[32,8,4,128]{3,2,1,0:T(4,128)(2,1)S(1)}, u32[]{:S(2)}) copy-start(bf16[32,8,4,128]{3,2,1,0:T(4,128)(2,1)S(1)} %collective-permute-done.refs_1_) | copy-start | bytes 786436
  37.6 2.2 %collective-permute-start.4 = (bf16[32,8,4,128]{3,2,1,0:T(4,128)(2,1)S(1)}, bf16[32,8,4,128]{3,2,1,0:T(4,128)(2,1)S(1)}, u32[]{:S(2)}, u32[]{:S(2)}) collective-permute-start(bf16[32,8,4,128]{3,2,1,0:T(4,128)(2,1)S(1)} %collective-permute-done.refs_1_), channel_id=1, source_target_pairs={{0,32},{32,0},{1,33},{33,1},{2,34},{34,2},{3,35},{35,3},{4,36},{36... | collective-permute-start | bytes 786440 | tf_op jit(solution)/shard_map/ppermute | solution.py:278
  38.7 2.3 %copy-start.2 = (bf16[32,8,4,128]{3,2,1,0:T(4,128)(2,1)}, bf16[32,8,4,128]{3,2,1,0:T(4,128)(2,1)S(1)}, u32[]{:S(2)}) copy-start(bf16[32,8,4,128]{3,2,1,0:T(4,128)(2,1)S(1)} %collective-permute-done.1.refs_2_) | copy-start | bytes 786436
  38.7 1.9 %collective-permute-start.5 = (bf16[32,8,4,128]{3,2,1,0:T(4,128)(2,1)S(1)}, bf16[32,8,4,128]{3,2,1,0:T(4,128)(2,1)S(1)}, u32[]{:S(2)}, u32[]{:S(2)}) collective-permute-start(bf16[32,8,4,128]{3,2,1,0:T(4,128)(2,1)S(1)} %collective-permute-done.1.refs_2_), channel_id=1, source_target_pairs={{0,32},{32,0},{1,33},{33,1},{2,34},{34,2},{3,35},{35,3},{4,36},{36... | collective-permute-start | bytes 786440 | tf_op jit(solution)/shard_map/ppermute | solution.py:278
  39.5 1.6 %copy-start.3 = (bf16[32,8,4,128]{3,2,1,0:T(4,128)(2,1)}, bf16[32,8,4,128]{3,2,1,0:T(4,128)(2,1)S(1)}, u32[]{:S(2)}) copy-start(bf16[32,8,4,128]{3,2,1,0:T(4,128)(2,1)S(1)} %collective-permute-done.2.refs_3_) | copy-start | bytes 786436
  39.5 1.6 %collective-permute-start.6 = (bf16[32,8,4,128]{3,2,1,0:T(4,128)(2,1)S(1)}, bf16[32,8,4,128]{3,2,1,0:T(4,128)(2,1)S(1)}, u32[]{:S(2)}, u32[]{:S(2)}) collective-permute-start(bf16[32,8,4,128]{3,2,1,0:T(4,128)(2,1)S(1)} %collective-permute-done.2.refs_3_), channel_id=1, source_target_pairs={{0,32},{32,0},{1,33},{33,1},{2,34},{34,2},{3,35},{35,3},{4,36},{36... | collective-permute-start | bytes 786440 | tf_op jit(solution)/shard_map/ppermute | solution.py:278
  39.9 1.2 %copy-start.4 = (bf16[32,8,4,128]{3,2,1,0:T(4,128)(2,1)}, bf16[32,8,4,128]{3,2,1,0:T(4,128)(2,1)S(1)}, u32[]{:S(2)}) copy-start(bf16[32,8,4,128]{3,2,1,0:T(4,128)(2,1)S(1)} %collective-permute-done.3.refs_4_) | copy-start | bytes 786436
  39.9 1.2 %copy-start.5 = (bf16[32,8,4,128]{3,2,1,0:T(4,128)(2,1)}, bf16[32,8,4,128]{3,2,1,0:T(4,128)(2,1)S(1)}, u32[]{:S(2)}) copy-start(bf16[32,8,4,128]{3,2,1,0:T(4,128)(2,1)S(1)} %collective-permute-done.4.refs_5_) | copy-start | bytes 786436
  40.6 0.7 copy-start.6
  41.3 0.7 copy-start.7
  48.2 22.0 %all-to-all-start.1 = ((bf16[32,17,4,128]{3,2,1,0:T(4,128)(2,1)}), bf16[32,17,4,128]{3,2,1,0:T(4,128)(2,1)S(1)}, u32[]{:S(2)}, u32[]{:S(2)}) async-start(bf16[32,17,4,128]{3,2,1,0:T(4,128)(2,1)} %blocks.1), calls=%async_computation.1 | async-start | bytes 1114112 | tf_op jit(solution)/shard_map/all_to_all | solution.py:290

commit v6 on v5

--- a/solution.py
+++ b/solution.py
@@ -23,9 +23,34 @@
     return hi, mid, lo
 
 
-def block_kernel(owner, fill, k_hbm, v_hbm, *refs):
-    pieces = refs[:-6]
-    out_ref, k_all, v_all, picked, stats, sem = refs[-6:]
+def hold_kernel(*refs):
+    n = len(refs) // 2
+    copies = [
+        pltpu.make_async_copy(refs[i], refs[n + i], refs[-1].at[i]) for i in range(n)
+    ]
+    for c in copies:
+        c.start()
+    for c in copies:
+        c.wait()
+
+
+def hold(*arrays):
+    size = sum(x.size * x.dtype.itemsize for x in arrays)
+    return pl.pallas_call(
+        hold_kernel,
+        out_shape=[jax.ShapeDtypeStruct(x.shape, x.dtype) for x in arrays],
+        in_specs=[pl.BlockSpec(memory_space=pl.ANY)] * len(arrays),
+        out_specs=[pl.BlockSpec(memory_space=pl.ANY)] * len(arrays),
+        scratch_shapes=[pltpu.SemaphoreType.DMA((len(arrays),))],
+        compiler_params=pltpu.CompilerParams(vmem_limit_bytes=44 * 1024 * 1024),
+        cost_estimate=pl.CostEstimate(flops=0, bytes_accessed=2 * size, transcendentals=0),
+        name="hold",
+    )(*arrays)
+
+
+def block_kernel(meta, k_all, v_all, *refs):
+    pieces = refs[:-4]
+    out_ref, picked, stats, sem = refs[-4:]
     slots, n_tp, depth, _ = picked.shape
     cols = n_tp * depth
     n_kv = KVH
@@ -37,37 +62,22 @@
     here_y, here_core = lax.axis_index("y"), lax.axis_index("core")
 
     def fetch(b):
-        home = owner[b] // rows
-        row = lax.rem(owner[b], rows)
+        home = meta[b] // rows
+        row = lax.rem(meta[b], rows)
         away = home // n_core ^ here_y
-        which = lax.rem(n_y - away, n_y) + (lax.rem(home, n_core) ^ here_core) * n_y
+        which = away + (lax.rem(home, n_core) ^ here_core) * n_y
         for p, piece in enumerate(pieces):
 
             @pl.when(which == p)
             def _(piece=piece):
-                pltpu.make_async_copy(piece.at[:, row], picked.at[b], sem.at[2, b]).start()
-
-    def keys_of(b):
-        return pltpu.make_async_copy(k_hbm.at[b], k_all.at[b], sem.at[0, b])
-
-    def values_of(b):
-        return pltpu.make_async_copy(v_hbm.at[b], v_all.at[b], sem.at[1, b])
+                pltpu.make_async_copy(piece.at[:, row], picked.at[b], sem.at[b]).start()
 
     def start(b, _):
-        keys_of(b).start()
         fetch(b)
         return 0
 
-    def start_values(b, _):
-        values_of(b).start()
-        return 0
-
     groups = slots // together
-    for g in range(groups):
-        lax.fori_loop(g * together, (g + 1) * together, start, 0)
-        if g:
-            lax.fori_loop((g - 1) * together, g * together, start_values, 0)
-    lax.fori_loop((groups - 1) * together, slots, start_values, 0)
+    lax.fori_loop(0, slots, start, 0)
     stats[...] = jnp.zeros_like(stats)
     slot_at = lax.broadcasted_iota(jnp.int32, (BLK, cols), 0)
     head = lax.broadcasted_iota(jnp.int32, (DH, cols), 1) // per
@@ -79,7 +89,7 @@
         scores = jnp.dot(
             k_all[b], jnp.concatenate(spread, axis=0), preferred_element_type=jnp.float32
         )
-        return jnp.where(slot_at < fill[b], scores, far_below)
+        return jnp.where(slot_at < meta[slots + b], scores, far_below)
 
     def soften(b, scores):
         peak = jnp.max(scores, axis=0, keepdims=True)
@@ -87,7 +97,7 @@
         total = jnp.sum(chances, axis=0, keepdims=True)
         for p, piece in enumerate(split_three(peak * SCALE) + split_three(total)):
             stats[pl.ds(p * slots + b, 1)] = piece.astype(jnp.float32)
-        stats[pl.ds(6 * slots + b, 1)] = jnp.broadcast_to(owner[b].astype(jnp.float32), (1, cols))
+        stats[pl.ds(6 * slots + b, 1)] = jnp.broadcast_to(meta[b].astype(jnp.float32), (1, cols))
         return chances.astype(jnp.bfloat16).T
 
     def mix(b, rounded):
@@ -104,53 +114,45 @@
 
     def weigh(first):
         for j in range(together):
-            keys_of(first + j).wait()
-            pltpu.make_async_copy(pieces[0].at[:, 0], picked.at[first + j], sem.at[2, first + j]).wait()
+            pltpu.make_async_copy(pieces[0].at[:, 0], picked.at[first + j], sem.at[first + j]).wait()
         scores = [score(first + j) for j in range(together)]
         return tuple(soften(first + j, scores[j]) for j in range(together))
 
-    def await_values(first):
-        for j in range(together):
-            values_of(first + j).wait()
-
     def step(i, rounded):
         first = i * together
-        await_values(first)
         later = weigh(first + together)
         for j in range(together):
             mix(first + j, rounded[j])
         return later
 
     rounded = lax.fori_loop(0, groups - 1, step, weigh(0))
-    await_values(slots - together)
     for j in range(together):
         mix(slots - together + j, rounded[j])
     packed = stats[...].T.astype(jnp.bfloat16)
     out_ref[:, pl.ds(slots, 1)] = packed.reshape(n_tp, 1, cols // n_tp, DH)
 
 
-def blocks(pieces, k_cache, v_cache, block_req, block_fill, n_tp):
+def blocks(pieces, k_cache, v_cache, meta, n_tp):
     slots = k_cache.shape[0]
     cols = n_tp * pieces[0].shape[2]
     return pl.pallas_call(
         block_kernel,
         out_shape=jax.ShapeDtypeStruct((n_tp, slots + 1, cols // n_tp, DH), jnp.bfloat16),
-        in_specs=[pl.BlockSpec(memory_space=pltpu.SMEM)] * 2
-        + [pl.BlockSpec(memory_space=pl.ANY)] * (2 + len(pieces)),
+        in_specs=[pl.BlockSpec(memory_space=pltpu.SMEM)]
+        + [pl.BlockSpec(memory_space=pltpu.VMEM)] * 2
+        + [pl.BlockSpec(memory_space=pl.ANY)] * len(pieces),
         out_specs=pl.BlockSpec(memory_space=pltpu.VMEM),
         scratch_shapes=[
-            pltpu.VMEM(k_cache.shape, k_cache.dtype),
-            pltpu.VMEM(v_cache.shape, v_cache.dtype),
             pltpu.VMEM((slots,) + pieces[0].shape[:1] + pieces[0].shape[2:], pieces[0].dtype),
             pltpu.VMEM((DH, cols), jnp.float32),
-            pltpu.SemaphoreType.DMA((3, slots)),
+            pltpu.SemaphoreType.DMA((slots,)),
         ],
-        compiler_params=pltpu.CompilerParams(vmem_limit_bytes=56 * 1024 * 1024),
+        compiler_params=pltpu.CompilerParams(vmem_limit_bytes=24 * 1024 * 1024),
         cost_estimate=pl.CostEstimate(
             flops=4 * slots * BLK * DH * 128, bytes_accessed=9 * 1024 * 1024, transcendentals=slots * BLK * 128
         ),
         name="blocks",
-    )(block_req, block_fill, k_cache, v_cache, *pieces)
+    )(meta, k_cache, v_cache, *pieces)
 
 
 def combine(got, requests):
@@ -186,9 +188,10 @@
     return num / safe, jnp.where(some, top + jnp.log(safe), far_below)
 
 
-def fresh_kernel(kv, q_ref, keys_ref, values_ref, out_ref):
+def fresh_kernel(q_ref, keys_ref, values_ref, out_ref):
     n_steps, own_rows, width = q_ref.shape
     n_heads = width // DH
+    own_kv = pl.ds(pl.multiple_of(lax.axis_index("z") * DH, DH), DH)
     lane = lax.broadcasted_iota(jnp.int32, (own_rows, DH), 1)
     levels = jnp.zeros((own_rows, DH), jnp.float32)
     for s in range(n_steps):
@@ -196,7 +199,7 @@
             c = s * n_heads + h
             query = q_ref[s, :, h * DH : (h + 1) * DH].astype(jnp.float32)
             fresh = [
-                jnp.sum(query * keys_ref[j].astype(jnp.float32), axis=1, keepdims=True) * SCALE
+                jnp.sum(query * keys_ref[j, :, own_kv].astype(jnp.float32), axis=1, keepdims=True) * SCALE
                 for j in range(s + 1)
             ]
             top = fresh[0]
@@ -206,29 +209,23 @@
             den = jnp.zeros((own_rows, 1), jnp.float32)
             for j in range(s + 1):
                 weight = jnp.exp(fresh[j] - top)
-                num = num + weight * values_ref[j].astype(jnp.float32)
+                num = num + weight * values_ref[j, :, own_kv].astype(jnp.float32)
                 den = den + weight
             out_ref[c] = num / den
             levels = jnp.where(lane == c, top + jnp.log(den), levels)
     out_ref[n_steps * n_heads] = levels
 
 
-def fresh_part(kv, queries, new_keys, new_values):
+def fresh_part(queries, new_keys, new_values):
     n_steps, own_rows, width = queries.shape
-    shape = (n_steps * (width // DH) + 1, own_rows, DH)
-    own_kv = pl.BlockSpec((n_steps, own_rows, DH), lambda i, kv: (0, 0, kv[0]))
     return pl.pallas_call(
         fresh_kernel,
-        out_shape=jax.ShapeDtypeStruct(shape, jnp.float32),
-        grid_spec=pltpu.PrefetchScalarGridSpec(
-            num_scalar_prefetch=1,
-            grid=(1,),
-            in_specs=[pl.BlockSpec(queries.shape, lambda i, kv: (0, 0, 0)), own_kv, own_kv],
-            out_specs=pl.BlockSpec(shape, lambda i, kv: (0, 0, 0)),
-        ),
+        out_shape=jax.ShapeDtypeStruct((n_steps * (width // DH) + 1, own_rows, DH), jnp.float32),
+        in_specs=[pl.BlockSpec(memory_space=pltpu.VMEM)] * 3,
+        out_specs=pl.BlockSpec(memory_space=pltpu.VMEM),
         cost_estimate=pl.CostEstimate(flops=1 << 17, bytes_accessed=1 << 16, transcendentals=1 << 8),
         name="fresh",
-    )(kv, queries, new_keys, new_values)
+    )(queries, new_keys, new_values)
 
 
 def finish_kernel(got, fresh, out_ref):
@@ -282,13 +279,16 @@
     own = lax.all_to_all(
         jnp.broadcast_to(rows[None], (n_z * n_x,) + rows.shape), ("z", "x"), 0, 0, tiled=True
     )
-    pieces = [own] + [from_other(own, "y", m) for m in range(n_y - 1, 0, -1)]
+    pieces = [own] + [from_other(own, "y", m) for m in range(1, n_y)]
+    held, keys, values = hold(own, k_cache, v_cache)
+    others, keys, values = lax.optimization_barrier((pieces[1:], keys, values))
+    pieces = [own] + others
     pieces = pieces + [from_other(p, "core", 1) for p in pieces]
-    sent = blocks(pieces, k_cache, v_cache, block_req, block_fill, n_z * n_x)
-    kv = lax.axis_index("z").astype(jnp.int32).reshape(1)
-    sent, kv = lax.optimization_barrier((sent, kv))
+    meta = jnp.concatenate([block_req, block_fill])
+    sent = blocks([held] + pieces[1:], keys, values, meta, n_z * n_x)
+    sent, late_queries = lax.optimization_barrier((sent, queries))
     got = lax.all_to_all(sent, ("z", "x"), split_axis=0, concat_axis=0, tiled=True)
-    got, fresh = lax.optimization_barrier((got, fresh_part(kv, queries, new_keys, new_values)))
+    got, fresh = lax.optimization_barrier((got, fresh_part(late_queries, new_keys, new_values)))
     part, level = combine(got, n_inst * own_rows)
     level = level[..., 0].reshape(4, n_inst, own_rows).transpose(1, 2, 0)
     level = jnp.pad(level, ((0, 0), (0, 0), (0, DH - 4)))[:, None]

time: 86.7 us -> 85.7 us (0.988)
  waiting for transfers between devices: 24.2 us -> 20.8 us
  Pallas kernels: 9.29 us -> 12.1 us
  local copies, waits for them, and re-layouts: 2.59 us -> 1.62 us
    pallas_call x1 -> x2, Pallas kernels: 1.43 us -> 5.01 us  [the longest x1 3.51 us: hold(): pl.pallas_call(hold_kernel, out_shape=[jax.ShapeDtypeStruct(x.shape, x.dt...]
    ppermute x7, waiting for transfers between devices: 8.61 us -> 5.19 us  [from_other(): lax.ppermute(value, axis, [(j, j ^ m) for j in range(lax.axis_size(axis))])]
    unnamed x16 -> x4, local copies, waits for them, and re-layouts: 0.97 us -> 0.01 us
  transfers between devices with their start and end apart: 8 -> 8, of which waited for: 4 -> 5; matrix products, arithmetic and copies ran while one was open for 0% -> 0% of each run, Pallas kernels for 2% -> 6%
where the time goes in v6:
time: 85.7 us; the launch traced here: 85.3 us
  blocking collectives  35 us (41%)
  waiting for transfers between devices  20.8 us (24%)
  starting transfers between devices  14.2 us (17%)
  Pallas kernels  12.1 us (14%)
  local copies, waits for them, and re-layouts  1.62 us (2%)
    all_to_all x1, blocking collectives, body(): lax.all_to_all(jnp.broadcast_to(rows[None], (n_z * n_x,) + rows.shape), (...  22.9 us
    all_to_all x1, waiting for transfers between devices, body(): lax.all_to_all(sent, ('z', 'x'), split_axis=0, concat_axis=0, tiled=True)  15.6 us
    all_to_all x1, blocking collectives, body(): lax.all_to_all(jnp.concatenate([part, level], axis=1), ('y', 'core'), 0,...  12.1 us
    ppermute x7, starting transfers between devices, from_other(): lax.ppermute(value, axis, [(j, j ^ m) for j in range(lax.axis_size(axis))])  9.44 us
    pallas_call x1, Pallas kernels, blocks(): pl.pallas_call(block_kernel, out_shape=jax.ShapeDtypeStruct((n_tp, slots...  5.42 us
    ppermute x7, waiting for transfers between devices, from_other(): lax.ppermute(value, axis, [(j, j ^ m) for j in range(lax.axis_size(axis))])  5.19 us
    all_to_all x1, starting transfers between devices, body(): lax.all_to_all(sent, ('z', 'x'), split_axis=0, concat_axis=0, tiled=True)  4.78 us
    pallas_call x1, Pallas kernels, hold(): pl.pallas_call(hold_kernel, out_shape=[jax.ShapeDtypeStruct(x.shape, x.dt...  3.51 us
  transfers between devices with their start and end apart: 8, of which 5 were waited for; matrix products, arithmetic and copies ran while one was open for 0% of the time, Pallas kernels for 6%

profile of v6, /device:TPU:1, one launch (start us, length us, event | category | flops | bytes accessed | tf_op | source)
XLA Modules:
  0.0 85.3 jit_solution(6362925340060840773)
XLA Ops:
  0.0 0.7 copy.23
  0.7 0.1 broadcast_in_dim.57
  0.8 22.9 %all_to_all.15.refs_0_ = bf16[32,8,4,128]{3,2,1,0:T(4,128)(2,1)S(1)} all-to-all(bf16[32,8,4,128]{3,2,1,0:T(4,128)(2,1)S(1)} %broadcast_in_dim.57), channel_id=1, replica_groups=mesh['y'=4,'core'=2,'z'=8,'x'=4] {'z','x'}, dimensions={0} | all-to-all | bytes 524288 | tf_op jit(solution)/shard_map/all_to_all | solution.py:279
  23.6 0.0 copy-start
  23.6 0.0 copy-start.1
  23.6 2.7 %collective-permute-start.2 = (bf16[32,8,4,128]{3,2,1,0:T(4,128)(2,1)S(1)}, bf16[32,8,4,128]{3,2,1,0:T(4,128)(2,1)S(1)}, u32[]{:S(2)}, u32[]{:S(2)}) collective-permute-start(bf16[32,8,4,128]{3,2,1,0:T(4,128)(2,1)S(1)} %all_to_all.15.refs_0_), channel_id=1, source_target_pairs={{0,192},{64,128},{128,64},{192,0},{1,193},{65,129},{129,65},{193,1... | collective-permute-start | bytes 786440 | tf_op jit(solution)/shard_map/ppermute | solution.py:275
  26.4 0.3 collective-permute-start.1
  26.7 0.3 collective-permute-start
  27.0 3.1 %collective-permute-start.3 = (bf16[32,8,4,128]{3,2,1,0:T(4,128)(2,1)S(1)}, bf16[32,8,4,128]{3,2,1,0:T(4,128)(2,1)S(1)}, u32[]{:S(2)}, u32[]{:S(2)}) collective-permute-start(bf16[32,8,4,128]{3,2,1,0:T(4,128)(2,1)S(1)} %all_to_all.15.refs_0_), channel_id=1, source_target_pairs={{0,32},{32,0},{1,33},{33,1},{2,34},{34,2},{3,35},{35,3},{4,36},{36... | collective-permute-start | bytes 786440 | tf_op jit(solution)/shard_map/ppermute | solution.py:275
  30.2 3.5 %hold.1 = (bf16[32,8,4,128]{3,2,1,0:T(4,128)(2,1)S(1)}, bf16[16,128,1024]{2,1,0:T(8,128)(2,1)S(1)}, bf16[16,128,1024]{2,1,0:T(8,128)(2,1)S(1)}) custom-call(bf16[32,8,4,128]{3,2,1,0:T(4,128)(2,1)S(1)} %all_to_all.15.refs_0_, bf16[16,128,1024]{2,1,0:T(8,128)(2,1)} %refs_1_.1, bf16[16,128,1024]{2,1,0:T(8,128)(2,1)} %refs_2_.1), custom_call_target="tpu_custom_call" | custom-call | bytes 17301504 | tf_op jit(solution)/shard_map/hold/pallas_call | solution.py:39
  33.7 3.9 %collective-permute-done.2.refs_3_ = bf16[32,8,4,128]{3,2,1,0:T(4,128)(2,1)S(1)} collective-permute-done((bf16[32,8,4,128]{3,2,1,0:T(4,128)(2,1)S(1)}, bf16[32,8,4,128]{3,2,1,0:T(4,128)(2,1)S(1)}, u32[]{:S(2)}, u32[]{:S(2)}) %collective-permute-start.2) | collective-permute-done | bytes 262176 | tf_op jit(solution)/shard_map/ppermute | solution.py:275
  37.6 0.0 collective-permute-done.1.refs_2_
  37.6 0.0 collective-permute-done.refs_1_
  37.6 2.4 %collective-permute-start.4 = (bf16[32,8,4,128]{3,2,1,0:T(4,128)(2,1)S(1)}, bf16[32,8,4,128]{3,2,1,0:T(4,128)(2,1)S(1)}, u32[]{:S(2)}, u32[]{:S(2)}) collective-permute-start(bf16[32,8,4,128]{3,2,1,0:T(4,128)(2,1)S(1)} %collective-permute-done.refs_1_), channel_id=1, source_target_pairs={{0,32},{32,0},{1,33},{33,1},{2,34},{34,2},{3,35},{35,3},{4,36},{36... | collective-permute-start | bytes 786440 | tf_op jit(solution)/shard_map/ppermute | solution.py:275
  40.0 0.0 collective-permute-start.5
  40.0 0.5 collective-permute-start.6
  40.5 0.0 copy-done
  40.5 0.0 copy-done.1
  40.5 0.1 pad_add_fusion.meta
  40.5 0.0 collective-permute-done.3.refs_4_
  40.6 0.6 collective-permute-done.4.refs_5_
  41.1 0.4 collective-permute-done.5.refs_6_
  41.5 0.4 collective-permute-done.6.refs_7_
  41.9 5.4 %blocks.1 = bf16[32,17,4,128]{3,2,1,0:T(4,128)(2,1)} custom-call(s32[32]{0:T(128)S(1)} %pad_add_fusion.meta, bf16[16,128,1024]{2,1,0:T(8,128)(2,1)S(1)} %get-tuple-element.19.k_all, bf16[16,128,1024]{2,1,0:T(8,128)(2,1)S(1)} %get-tuple-element.20.v_all, bf16[32,8,4,128]{3,2,1,0:T(4,128)(2,1)S(1)} %get-tuple-element.21.refs_0_, ...), custom_call_target="tpu_custom_call" | custom-call | flops 134217728 | bytes 9437184 | tf_op jit(solution)/shard_map/blocks/pallas_call | solution.py:138
  47.3 4.8 %all-to-all-start.1 = ((bf16[32,17,4,128]{3,2,1,0:T(4,128)(2,1)}), bf16[32,17,4,128]{3,2,1,0:T(4,128)(2,1)S(1)}, u32[]{:S(2)}, u32[]{:S(2)}) async-start(bf16[32,17,4,128]{3,2,1,0:T(4,128)(2,1)} %blocks.1), calls=%async_computation.1 | async-start | bytes 1114112 | tf_op jit(solution)/shard_map/all_to_all | solution.py:290
  52.1 1.5 %fresh.1 = f32[5,8,128]{2,1,0:T(8,128)} custom-call(bf16[2,8,256]{2,1,0:T(8,128)(2,1)} %q_ref, bf16[2,8,1024]{2,1,0:T(8,128)(2,1)} %keys_ref.1, bf16[2,8,1024]{2,1,0:T(8,128)(2,1)} %values_ref.1), custom_call_target="tpu_custom_call" | custom-call | flops 131072 | bytes 65536 | tf_op jit(solution)/shard_map/fresh/pallas_call | solution.py:221
  53.6 15.6 %all-to-all-done.1 = bf16[32,17,4,128]{3,2,1,0:T(4,128)(2,1)S(1)} async-done(((bf16[32,17,4,128]{3,2,1,0:T(4,128)(2,1)}), bf16[32,17,4,128]{3,2,1,0:T(4,128)(2,1)S(1)}, u32[]{:S(2)}, u32[]{:S(2)}) %all-to-all-start.1) | async-done | bytes 557088 | tf_op jit(solution)/shard_map/all_to_all | solution.py:290
  69.2 0.1 slice.32
  69.3 0.2 convert_add_fusion
  69.4 0.1 copy.24
  69.5 0.1 copy.25
  69.6 0.1 reshape.56
  69.8 0.1 mul.10
  69.9 0.1 broadcast_in_dim.59
  70.0 0.1 select_reduce_fusion
  70.2 0.3 fusion.5
  70.5 0.1 copy.31
  70.6 0.1 copy.32
  70.7 0.3 fusion.8
  71.1 0.4 fusion.1
  71.5 12.1 %all_to_all.16.got = f32[8,5,8,128]{3,2,1,0:T(8,128)} all-to-all(f32[8,5,8,128]{3,2,1,0:T(8,128)S(1)} %pad_maximum_fusion), channel_id=1, replica_groups=mesh['y'=4,'core'=2,'z'=8,'x'=4] {'y','core'}, dimensions={0} | all-to-all | bytes 327680 | tf_op jit(solution)/shard_map/all_to_all | solution.py:296
  83.7 1.7 %finish.1 = bf16[2,8,256]{2,1,0:T(8,128)(2,1)} custom-call(f32[8,5,8,128]{3,2,1,0:T(8,128)} %all_to_all.16.got, f32[5,8,128]{2,1,0:T(8,128)} %fresh.1), custom_call_target="tpu_custom_call" | custom-call | tf_op jit(solution)/shard_map/finish/pallas_call | solution.py:258
  (11 shorter events, 0.1 us)
Async XLA Ops:
  23.6 16.8 %copy-start = (s32[16]{0:T(128)S(1)}, s32[16]{0:T(128)}, u32[]{:S(2)}) copy-start(s32[16]{0:T(128)} %param.13) | copy-start | bytes 196
  23.6 16.8 %copy-start.1 = (s32[16]{0:T(128)S(1)}, s32[16]{0:T(128)}, u32[]{:S(2)}) copy-start(s32[16]{0:T(128)} %param.12) | copy-start | bytes 196
  23.6 13.9 %collective-permute-start.2 = (bf16[32,8,4,128]{3,2,1,0:T(4,128)(2,1)S(1)}, bf16[32,8,4,128]{3,2,1,0:T(4,128)(2,1)S(1)}, u32[]{:S(2)}, u32[]{:S(2)}) collective-permute-start(bf16[32,8,4,128]{3,2,1,0:T(4,128)(2,1)S(1)} %all_to_all.15.refs_0_), channel_id=1, source_target_pairs={{0,192},{64,128},{128,64},{192,0},{1,193},{65,129},{129,65},{193,1... | collective-permute-start | bytes 786440 | tf_op jit(solution)/shard_map/ppermute | solution.py:275
  26.4 11.2 %collective-permute-start.1 = (bf16[32,8,4,128]{3,2,1,0:T(4,128)(2,1)S(1)}, bf16[32,8,4,128]{3,2,1,0:T(4,128)(2,1)S(1)}, u32[]{:S(2)}, u32[]{:S(2)}) collective-permute-start(bf16[32,8,4,128]{3,2,1,0:T(4,128)(2,1)S(1)} %all_to_all.15.refs_0_), channel_id=1, source_target_pairs={{0,128},{64,192},{128,0},{192,64},{1,129},{65,193},{129,1},{193,65... | collective-permute-start | bytes 786440 | tf_op jit(solution)/shard_map/ppermute | solution.py:275
  26.7 10.9 %collective-permute-start = (bf16[32,8,4,128]{3,2,1,0:T(4,128)(2,1)S(1)}, bf16[32,8,4,128]{3,2,1,0:T(4,128)(2,1)S(1)}, u32[]{:S(2)}, u32[]{:S(2)}) collective-permute-start(bf16[32,8,4,128]{3,2,1,0:T(4,128)(2,1)S(1)} %all_to_all.15.refs_0_), channel_id=1, source_target_pairs={{0,64},{64,0},{128,192},{192,128},{1,65},{65,1},{129,193},{193,129... | collective-permute-start | bytes 786440 | tf_op jit(solution)/shard_map/ppermute | solution.py:275
  27.0 13.5 %collective-permute-start.3 = (bf16[32,8,4,128]{3,2,1,0:T(4,128)(2,1)S(1)}, bf16[32,8,4,128]{3,2,1,0:T(4,128)(2,1)S(1)}, u32[]{:S(2)}, u32[]{:S(2)}) collective-permute-start(bf16[32,8,4,128]{3,2,1,0:T(4,128)(2,1)S(1)} %all_to_all.15.refs_0_), channel_id=1, source_target_pairs={{0,32},{32,0},{1,33},{33,1},{2,34},{34,2},{3,35},{35,3},{4,36},{36... | collective-permute-start | bytes 786440 | tf_op jit(solution)/shard_map/ppermute | solution.py:275
  37.6 3.5 %collective-permute-start.4 = (bf16[32,8,4,128]{3,2,1,0:T(4,128)(2,1)S(1)}, bf16[32,8,4,128]{3,2,1,0:T(4,128)(2,1)S(1)}, u32[]{:S(2)}, u32[]{:S(2)}) collective-permute-start(bf16[32,8,4,128]{3,2,1,0:T(4,128)(2,1)S(1)} %collective-permute-done.refs_1_), channel_id=1, source_target_pairs={{0,32},{32,0},{1,33},{33,1},{2,34},{34,2},{3,35},{35,3},{4,36},{36... | collective-permute-start | bytes 786440 | tf_op jit(solution)/shard_map/ppermute | solution.py:275
  40.0 1.5 %collective-permute-start.5 = (bf16[32,8,4,128]{3,2,1,0:T(4,128)(2,1)S(1)}, bf16[32,8,4,128]{3,2,1,0:T(4,128)(2,1)S(1)}, u32[]{:S(2)}, u32[]{:S(2)}) collective-permute-start(bf16[32,8,4,128]{3,2,1,0:T(4,128)(2,1)S(1)} %collective-permute-done.1.refs_2_), channel_id=1, source_target_pairs={{0,32},{32,0},{1,33},{33,1},{2,34},{34,2},{3,35},{35,3},{4,36},{36... | collective-permute-start | bytes 786440 | tf_op jit(solution)/shard_map/ppermute | solution.py:275
  40.0 1.9 %collective-permute-start.6 = (bf16[32,8,4,128]{3,2,1,0:T(4,128)(2,1)S(1)}, bf16[32,8,4,128]{3,2,1,0:T(4,128)(2,1)S(1)}, u32[]{:S(2)}, u32[]{:S(2)}) collective-permute-start(bf16[32,8,4,128]{3,2,1,0:T(4,128)(2,1)S(1)} %collective-permute-done.2.refs_3_), channel_id=1, source_target_pairs={{0,32},{32,0},{1,33},{33,1},{2,34},{34,2},{3,35},{35,3},{4,36},{36... | collective-permute-start | bytes 786440 | tf_op jit(solution)/shard_map/ppermute | solution.py:275
  47.3 21.8 %all-to-all-start.1 = ((bf16[32,17,4,128]{3,2,1,0:T(4,128)(2,1)}), bf16[32,17,4,128]{3,2,1,0:T(4,128)(2,1)S(1)}, u32[]{:S(2)}, u32[]{:S(2)}) async-start(bf16[32,17,4,128]{3,2,1,0:T(4,128)(2,1)} %blocks.1), calls=%async_computation.1 | async-start | bytes 1114112 | tf_op jit(solution)/shard_map/all_to_all | solution.py:290

commit v7 on v6

--- a/solution.py
+++ b/solution.py
@@ -57,20 +57,24 @@
     per, n_x = cols // n_kv, n_tp // n_kv
     together = 4
     rows = pieces[0].shape[1]
-    n_core = 2
-    n_y = len(pieces) // n_core
+    n_y, row_bits = len(pieces) // 2, rows.bit_length() - 1
     here_y, here_core = lax.axis_index("y"), lax.axis_index("core")
 
     def fetch(b):
-        home = meta[b] // rows
-        row = lax.rem(meta[b], rows)
-        away = home // n_core ^ here_y
-        which = away + (lax.rem(home, n_core) ^ here_core) * n_y
-        for p, piece in enumerate(pieces):
-
-            @pl.when(which == p)
-            def _(piece=piece):
-                pltpu.make_async_copy(piece.at[:, row], picked.at[b], sem.at[b]).start()
+        home = meta[b] >> row_bits
+        row = meta[b] & (rows - 1)
+        which = (home >> 1 ^ here_y) + (home & 1 ^ here_core) * n_y
+
+        def choose(first, last):
+            if last - first == 1:
+                pltpu.make_async_copy(pieces[first].at[:, row], picked.at[b], sem.at[b]).start()
+                return 0
+            middle = (first + last) // 2
+            return lax.cond(
+                which < middle, lambda: choose(first, middle), lambda: choose(middle, last)
+            )
+
+        choose(0, len(pieces))
 
     def start(b, _):
         fetch(b)

time: 85.7 us -> 85.2 us (level)
  no operation moved by 1% of the time
where the time goes in v7:
time: 85.2 us; the launch traced here: 84.9 us
  blocking collectives  35 us (41%)
  waiting for transfers between devices  20.7 us (24%)
  starting transfers between devices  14.2 us (17%)
  Pallas kernels  11.6 us (14%)
  local copies, waits for them, and re-layouts  1.62 us (2%)
    all_to_all x1, blocking collectives, body(): lax.all_to_all(jnp.broadcast_to(rows[None], (n_z * n_x,) + rows.shape), (...  22.9 us
    all_to_all x1, waiting for transfers between devices, body(): lax.all_to_all(sent, ('z', 'x'), split_axis=0, concat_axis=0, tiled=True)  15.6 us
    all_to_all x1, blocking collectives, body(): lax.all_to_all(jnp.concatenate([part, level], axis=1), ('y', 'core'), 0,...  12.2 us
    ppermute x7, starting transfers between devices, from_other(): lax.ppermute(value, axis, [(j, j ^ m) for j in range(lax.axis_size(axis))])  9.44 us
    ppermute x7, waiting for transfers between devices, from_other(): lax.ppermute(value, axis, [(j, j ^ m) for j in range(lax.axis_size(axis))])  5.19 us
    pallas_call x1, Pallas kernels, blocks(): pl.pallas_call(block_kernel, out_shape=jax.ShapeDtypeStruct((n_tp, slots...  4.89 us
    all_to_all x1, starting transfers between devices, body(): lax.all_to_all(sent, ('z', 'x'), split_axis=0, concat_axis=0, tiled=True)  4.78 us
    pallas_call x1, Pallas kernels, hold(): pl.pallas_call(hold_kernel, out_shape=[jax.ShapeDtypeStruct(x.shape, x.dt...  3.51 us
  transfers between devices with their start and end apart: 8, of which 5 were waited for; matrix products, arithmetic and copies ran while one was open for 0% of the time, Pallas kernels for 6%

profile of v7, /device:TPU:1, one launch (start us, length us, event | category | flops | bytes accessed | tf_op | source)
XLA Modules:
  0.0 84.9 jit_solution(15598288524049959885)
XLA Ops:
  0.0 0.7 copy.23
  0.7 0.1 broadcast_in_dim.57
  0.8 22.9 %all_to_all.15.refs_0_ = bf16[32,8,4,128]{3,2,1,0:T(4,128)(2,1)S(1)} all-to-all(bf16[32,8,4,128]{3,2,1,0:T(4,128)(2,1)S(1)} %broadcast_in_dim.57), channel_id=1, replica_groups=mesh['y'=4,'core'=2,'z'=8,'x'=4] {'z','x'}, dimensions={0} | all-to-all | bytes 524288 | tf_op jit(solution)/shard_map/all_to_all | solution.py:283
  23.6 0.0 copy-start
  23.6 0.0 copy-start.1
  23.6 2.7 %collective-permute-start.2 = (bf16[32,8,4,128]{3,2,1,0:T(4,128)(2,1)S(1)}, bf16[32,8,4,128]{3,2,1,0:T(4,128)(2,1)S(1)}, u32[]{:S(2)}, u32[]{:S(2)}) collective-permute-start(bf16[32,8,4,128]{3,2,1,0:T(4,128)(2,1)S(1)} %all_to_all.15.refs_0_), channel_id=1, source_target_pairs={{0,192},{64,128},{128,64},{192,0},{1,193},{65,129},{129,65},{193,1... | collective-permute-start | bytes 786440 | tf_op jit(solution)/shard_map/ppermute | solution.py:279
  26.4 0.3 collective-permute-start.1
  26.7 0.3 collective-permute-start
  27.0 3.1 %collective-permute-start.3 = (bf16[32,8,4,128]{3,2,1,0:T(4,128)(2,1)S(1)}, bf16[32,8,4,128]{3,2,1,0:T(4,128)(2,1)S(1)}, u32[]{:S(2)}, u32[]{:S(2)}) collective-permute-start(bf16[32,8,4,128]{3,2,1,0:T(4,128)(2,1)S(1)} %all_to_all.15.refs_0_), channel_id=1, source_target_pairs={{0,32},{32,0},{1,33},{33,1},{2,34},{34,2},{3,35},{35,3},{4,36},{36... | collective-permute-start | bytes 786440 | tf_op jit(solution)/shard_map/ppermute | solution.py:279
  30.2 3.5 %hold.1 = (bf16[32,8,4,128]{3,2,1,0:T(4,128)(2,1)S(1)}, bf16[16,128,1024]{2,1,0:T(8,128)(2,1)S(1)}, bf16[16,128,1024]{2,1,0:T(8,128)(2,1)S(1)}) custom-call(bf16[32,8,4,128]{3,2,1,0:T(4,128)(2,1)S(1)} %all_to_all.15.refs_0_, bf16[16,128,1024]{2,1,0:T(8,128)(2,1)} %refs_1_.1, bf16[16,128,1024]{2,1,0:T(8,128)(2,1)} %refs_2_.1), custom_call_target="tpu_custom_call" | custom-call | bytes 17301504 | tf_op jit(solution)/shard_map/hold/pallas_call | solution.py:39
  33.7 3.9 %collective-permute-done.2.refs_3_ = bf16[32,8,4,128]{3,2,1,0:T(4,128)(2,1)S(1)} collective-permute-done((bf16[32,8,4,128]{3,2,1,0:T(4,128)(2,1)S(1)}, bf16[32,8,4,128]{3,2,1,0:T(4,128)(2,1)S(1)}, u32[]{:S(2)}, u32[]{:S(2)}) %collective-permute-start.2) | collective-permute-done | bytes 262176 | tf_op jit(solution)/shard_map/ppermute | solution.py:279
  37.6 0.0 collective-permute-done.1.refs_2_
  37.6 0.0 collective-permute-done.refs_1_
  37.6 2.4 %collective-permute-start.4 = (bf16[32,8,4,128]{3,2,1,0:T(4,128)(2,1)S(1)}, bf16[32,8,4,128]{3,2,1,0:T(4,128)(2,1)S(1)}, u32[]{:S(2)}, u32[]{:S(2)}) collective-permute-start(bf16[32,8,4,128]{3,2,1,0:T(4,128)(2,1)S(1)} %collective-permute-done.refs_1_), channel_id=1, source_target_pairs={{0,32},{32,0},{1,33},{33,1},{2,34},{34,2},{3,35},{35,3},{4,36},{36... | collective-permute-start | bytes 786440 | tf_op jit(solution)/shard_map/ppermute | solution.py:279
  40.0 0.0 collective-permute-start.5
  40.0 0.5 collective-permute-start.6
  40.5 0.0 copy-done
  40.5 0.0 copy-done.1
  40.5 0.1 pad_add_fusion.meta
  40.5 0.0 collective-permute-done.3.refs_4_
  40.6 0.6 collective-permute-done.4.refs_5_
  41.1 0.4 collective-permute-done.5.refs_6_
  41.5 0.4 collective-permute-done.6.refs_7_
  41.9 4.9 %blocks.1 = bf16[32,17,4,128]{3,2,1,0:T(4,128)(2,1)} custom-call(s32[32]{0:T(128)S(1)} %pad_add_fusion.meta, bf16[16,128,1024]{2,1,0:T(8,128)(2,1)S(1)} %get-tuple-element.19.k_all, bf16[16,128,1024]{2,1,0:T(8,128)(2,1)S(1)} %get-tuple-element.20.v_all, bf16[32,8,4,128]{3,2,1,0:T(4,128)(2,1)S(1)} %get-tuple-element.21.refs_0_, ...), custom_call_target="tpu_custom_call" | custom-call | flops 134217728 | bytes 9437184 | tf_op jit(solution)/shard_map/blocks/pallas_call | solution.py:142
  46.8 4.8 %all-to-all-start.1 = ((bf16[32,17,4,128]{3,2,1,0:T(4,128)(2,1)}), bf16[32,17,4,128]{3,2,1,0:T(4,128)(2,1)S(1)}, u32[]{:S(2)}, u32[]{:S(2)}) async-start(bf16[32,17,4,128]{3,2,1,0:T(4,128)(2,1)} %blocks.1), calls=%async_computation.1 | async-start | bytes 1114112 | tf_op jit(solution)/shard_map/all_to_all | solution.py:294
  51.6 1.5 %fresh.1 = f32[5,8,128]{2,1,0:T(8,128)} custom-call(bf16[2,8,256]{2,1,0:T(8,128)(2,1)} %q_ref, bf16[2,8,1024]{2,1,0:T(8,128)(2,1)} %keys_ref.1, bf16[2,8,1024]{2,1,0:T(8,128)(2,1)} %values_ref.1), custom_call_target="tpu_custom_call" | custom-call | flops 131072 | bytes 65536 | tf_op jit(solution)/shard_map/fresh/pallas_call | solution.py:225
  53.1 15.6 %all-to-all-done.1 = bf16[32,17,4,128]{3,2,1,0:T(4,128)(2,1)S(1)} async-done(((bf16[32,17,4,128]{3,2,1,0:T(4,128)(2,1)}), bf16[32,17,4,128]{3,2,1,0:T(4,128)(2,1)S(1)}, u32[]{:S(2)}, u32[]{:S(2)}) %all-to-all-start.1) | async-done | bytes 557088 | tf_op jit(solution)/shard_map/all_to_all | solution.py:294
  68.6 0.1 slice.32
  68.7 0.2 convert_add_fusion
  68.9 0.1 copy.24
  69.0 0.1 copy.25
  69.1 0.1 reshape.56
  69.3 0.1 mul.10
  69.4 0.1 broadcast_in_dim.59
  69.5 0.1 select_reduce_fusion
  69.6 0.3 fusion.5
  70.0 0.1 copy.31
  70.1 0.1 copy.32
  70.2 0.3 fusion.8
  70.6 0.4 fusion.1
  71.0 12.2 %all_to_all.16.got = f32[8,5,8,128]{3,2,1,0:T(8,128)} all-to-all(f32[8,5,8,128]{3,2,1,0:T(8,128)S(1)} %pad_maximum_fusion), channel_id=1, replica_groups=mesh['y'=4,'core'=2,'z'=8,'x'=4] {'y','core'}, dimensions={0} | all-to-all | bytes 327680 | tf_op jit(solution)/shard_map/all_to_all | solution.py:300
  83.2 1.7 %finish.1 = bf16[2,8,256]{2,1,0:T(8,128)(2,1)} custom-call(f32[8,5,8,128]{3,2,1,0:T(8,128)} %all_to_all.16.got, f32[5,8,128]{2,1,0:T(8,128)} %fresh.1), custom_call_target="tpu_custom_call" | custom-call | tf_op jit(solution)/shard_map/finish/pallas_call | solution.py:262
  (11 shorter events, 0.2 us)
Async XLA Ops:
  23.6 16.8 %copy-start = (s32[16]{0:T(128)S(1)}, s32[16]{0:T(128)}, u32[]{:S(2)}) copy-start(s32[16]{0:T(128)} %param.13) | copy-start | bytes 196
  23.6 16.8 %copy-start.1 = (s32[16]{0:T(128)S(1)}, s32[16]{0:T(128)}, u32[]{:S(2)}) copy-start(s32[16]{0:T(128)} %param.12) | copy-start | bytes 196
  23.6 13.9 %collective-permute-start.2 = (bf16[32,8,4,128]{3,2,1,0:T(4,128)(2,1)S(1)}, bf16[32,8,4,128]{3,2,1,0:T(4,128)(2,1)S(1)}, u32[]{:S(2)}, u32[]{:S(2)}) collective-permute-start(bf16[32,8,4,128]{3,2,1,0:T(4,128)(2,1)S(1)} %all_to_all.15.refs_0_), channel_id=1, source_target_pairs={{0,192},{64,128},{128,64},{192,0},{1,193},{65,129},{129,65},{193,1... | collective-permute-start | bytes 786440 | tf_op jit(solution)/shard_map/ppermute | solution.py:279
  26.4 11.2 %collective-permute-start.1 = (bf16[32,8,4,128]{3,2,1,0:T(4,128)(2,1)S(1)}, bf16[32,8,4,128]{3,2,1,0:T(4,128)(2,1)S(1)}, u32[]{:S(2)}, u32[]{:S(2)}) collective-permute-start(bf16[32,8,4,128]{3,2,1,0:T(4,128)(2,1)S(1)} %all_to_all.15.refs_0_), channel_id=1, source_target_pairs={{0,128},{64,192},{128,0},{192,64},{1,129},{65,193},{129,1},{193,65... | collective-permute-start | bytes 786440 | tf_op jit(solution)/shard_map/ppermute | solution.py:279
  26.7 10.9 %collective-permute-start = (bf16[32,8,4,128]{3,2,1,0:T(4,128)(2,1)S(1)}, bf16[32,8,4,128]{3,2,1,0:T(4,128)(2,1)S(1)}, u32[]{:S(2)}, u32[]{:S(2)}) collective-permute-start(bf16[32,8,4,128]{3,2,1,0:T(4,128)(2,1)S(1)} %all_to_all.15.refs_0_), channel_id=1, source_target_pairs={{0,64},{64,0},{128,192},{192,128},{1,65},{65,1},{129,193},{193,129... | collective-permute-start | bytes 786440 | tf_op jit(solution)/shard_map/ppermute | solution.py:279
  27.0 13.5 %collective-permute-start.3 = (bf16[32,8,4,128]{3,2,1,0:T(4,128)(2,1)S(1)}, bf16[32,8,4,128]{3,2,1,0:T(4,128)(2,1)S(1)}, u32[]{:S(2)}, u32[]{:S(2)}) collective-permute-start(bf16[32,8,4,128]{3,2,1,0:T(4,128)(2,1)S(1)} %all_to_all.15.refs_0_), channel_id=1, source_target_pairs={{0,32},{32,0},{1,33},{33,1},{2,34},{34,2},{3,35},{35,3},{4,36},{36... | collective-permute-start | bytes 786440 | tf_op jit(solution)/shard_map/ppermute | solution.py:279
  37.6 3.5 %collective-permute-start.4 = (bf16[32,8,4,128]{3,2,1,0:T(4,128)(2,1)S(1)}, bf16[32,8,4,128]{3,2,1,0:T(4,128)(2,1)S(1)}, u32[]{:S(2)}, u32[]{:S(2)}) collective-permute-start(bf16[32,8,4,128]{3,2,1,0:T(4,128)(2,1)S(1)} %collective-permute-done.refs_1_), channel_id=1, source_target_pairs={{0,32},{32,0},{1,33},{33,1},{2,34},{34,2},{3,35},{35,3},{4,36},{36... | collective-permute-start | bytes 786440 | tf_op jit(solution)/shard_map/ppermute | solution.py:279
  40.0 1.5 %collective-permute-start.5 = (bf16[32,8,4,128]{3,2,1,0:T(4,128)(2,1)S(1)}, bf16[32,8,4,128]{3,2,1,0:T(4,128)(2,1)S(1)}, u32[]{:S(2)}, u32[]{:S(2)}) collective-permute-start(bf16[32,8,4,128]{3,2,1,0:T(4,128)(2,1)S(1)} %collective-permute-done.1.refs_2_), channel_id=1, source_target_pairs={{0,32},{32,0},{1,33},{33,1},{2,34},{34,2},{3,35},{35,3},{4,36},{36... | collective-permute-start | bytes 786440 | tf_op jit(solution)/shard_map/ppermute | solution.py:279
  40.0 1.9 %collective-permute-start.6 = (bf16[32,8,4,128]{3,2,1,0:T(4,128)(2,1)S(1)}, bf16[32,8,4,128]{3,2,1,0:T(4,128)(2,1)S(1)}, u32[]{:S(2)}, u32[]{:S(2)}) collective-permute-start(bf16[32,8,4,128]{3,2,1,0:T(4,128)(2,1)S(1)} %collective-permute-done.2.refs_3_), channel_id=1, source_target_pairs={{0,32},{32,0},{1,33},{33,1},{2,34},{34,2},{3,35},{35,3},{4,36},{36... | collective-permute-start | bytes 786440 | tf_op jit(solution)/shard_map/ppermute | solution.py:279
  46.8 21.8 %all-to-all-start.1 = ((bf16[32,17,4,128]{3,2,1,0:T(4,128)(2,1)}), bf16[32,17,4,128]{3,2,1,0:T(4,128)(2,1)S(1)}, u32[]{:S(2)}, u32[]{:S(2)}) async-start(bf16[32,17,4,128]{3,2,1,0:T(4,128)(2,1)} %blocks.1), calls=%async_computation.1 | async-start | bytes 1114112 | tf_op jit(solution)/shard_map/all_to_all | solution.py:294

commit v8 on v7

--- a/solution.py
+++ b/solution.py
@@ -55,7 +55,7 @@
     cols = n_tp * depth
     n_kv = KVH
     per, n_x = cols // n_kv, n_tp // n_kv
-    together = 4
+    together = 8
     rows = pieces[0].shape[1]
     n_y, row_bits = len(pieces) // 2, rows.bit_length() - 1
     here_y, here_core = lax.axis_index("y"), lax.axis_index("core")
@@ -285,8 +285,7 @@
     )
     pieces = [own] + [from_other(own, "y", m) for m in range(1, n_y)]
     held, keys, values = hold(own, k_cache, v_cache)
-    others, keys, values = lax.optimization_barrier((pieces[1:], keys, values))
-    pieces = [own] + others
+    pieces = [own] + [lax.optimization_barrier((p, keys))[0] for p in pieces[1:]]
     pieces = pieces + [from_other(p, "core", 1) for p in pieces]
     meta = jnp.concatenate([block_req, block_fill])
     sent = blocks([held] + pieces[1:], keys, values, meta, n_z * n_x)

time: 85.2 us -> 84.6 us (level)
  no operation moved by 1% of the time
where the time goes in v8:
time: 84.6 us; the launch traced here: 84.3 us
  blocking collectives  35 us (41%)
  waiting for transfers between devices  20.7 us (24%)
  starting transfers between devices  14.2 us (17%)
  Pallas kernels  11 us (13%)
  local copies, waits for them, and re-layouts  1.62 us (2%)
    all_to_all x1, blocking collectives, body(): lax.all_to_all(jnp.broadcast_to(rows[None], (n_z * n_x,) + rows.shape), (...  22.9 us
    all_to_all x1, waiting for transfers between devices, body(): lax.all_to_all(sent, ('z', 'x'), split_axis=0, concat_axis=0, tiled=True)  15.6 us
    all_to_all x1, blocking collectives, body(): lax.all_to_all(jnp.concatenate([part, level], axis=1), ('y', 'core'), 0,...  12.2 us
    ppermute x7, starting transfers between devices, from_other(): lax.ppermute(value, axis, [(j, j ^ m) for j in range(lax.axis_size(axis))])  9.44 us
    ppermute x7, waiting for transfers between devices, from_other(): lax.ppermute(value, axis, [(j, j ^ m) for j in range(lax.axis_size(axis))])  5.19 us
    all_to_all x1, starting transfers between devices, body(): lax.all_to_all(sent, ('z', 'x'), split_axis=0, concat_axis=0, tiled=True)  4.78 us
    pallas_call x1, Pallas kernels, blocks(): pl.pallas_call(block_kernel, out_shape=jax.ShapeDtypeStruct((n_tp, slots...  4.32 us
    pallas_call x1, Pallas kernels, hold(): pl.pallas_call(hold_kernel, out_shape=[jax.ShapeDtypeStruct(x.shape, x.dt...  3.51 us
  transfers between devices with their start and end apart: 8, of which 5 were waited for; matrix products, arithmetic and copies ran while one was open for 0% of the time, Pallas kernels for 6%

profile of v8, /device:TPU:1, one launch (start us, length us, event | category | flops | bytes accessed | tf_op | source)
XLA Modules:
  0.0 84.3 jit_solution(11650397463666089802)
XLA Ops:
  0.0 0.7 copy.23
  0.7 0.1 broadcast_in_dim.57
  0.8 22.9 %all_to_all.15.refs_0_ = bf16[32,8,4,128]{3,2,1,0:T(4,128)(2,1)S(1)} all-to-all(bf16[32,8,4,128]{3,2,1,0:T(4,128)(2,1)S(1)} %broadcast_in_dim.57), channel_id=1, replica_groups=mesh['y'=4,'core'=2,'z'=8,'x'=4] {'z','x'}, dimensions={0} | all-to-all | bytes 524288 | tf_op jit(solution)/shard_map/all_to_all | solution.py:283
  23.6 0.0 copy-start
  23.6 0.0 copy-start.1
  23.6 2.7 %collective-permute-start.2 = (bf16[32,8,4,128]{3,2,1,0:T(4,128)(2,1)S(1)}, bf16[32,8,4,128]{3,2,1,0:T(4,128)(2,1)S(1)}, u32[]{:S(2)}, u32[]{:S(2)}) collective-permute-start(bf16[32,8,4,128]{3,2,1,0:T(4,128)(2,1)S(1)} %all_to_all.15.refs_0_), channel_id=1, source_target_pairs={{0,192},{64,128},{128,64},{192,0},{1,193},{65,129},{129,65},{193,1... | collective-permute-start | bytes 786440 | tf_op jit(solution)/shard_map/ppermute | solution.py:279
  26.4 0.3 collective-permute-start.1
  26.7 0.3 collective-permute-start
  27.0 3.1 %collective-permute-start.3 = (bf16[32,8,4,128]{3,2,1,0:T(4,128)(2,1)S(1)}, bf16[32,8,4,128]{3,2,1,0:T(4,128)(2,1)S(1)}, u32[]{:S(2)}, u32[]{:S(2)}) collective-permute-start(bf16[32,8,4,128]{3,2,1,0:T(4,128)(2,1)S(1)} %all_to_all.15.refs_0_), channel_id=1, source_target_pairs={{0,32},{32,0},{1,33},{33,1},{2,34},{34,2},{3,35},{35,3},{4,36},{36... | collective-permute-start | bytes 786440 | tf_op jit(solution)/shard_map/ppermute | solution.py:279
  30.2 3.5 %hold.1 = (bf16[32,8,4,128]{3,2,1,0:T(4,128)(2,1)S(1)}, bf16[16,128,1024]{2,1,0:T(8,128)(2,1)S(1)}, bf16[16,128,1024]{2,1,0:T(8,128)(2,1)S(1)}) custom-call(bf16[32,8,4,128]{3,2,1,0:T(4,128)(2,1)S(1)} %all_to_all.15.refs_0_, bf16[16,128,1024]{2,1,0:T(8,128)(2,1)} %refs_1_.1, bf16[16,128,1024]{2,1,0:T(8,128)(2,1)} %refs_2_.1), custom_call_target="tpu_custom_call" | custom-call | bytes 17301504 | tf_op jit(solution)/shard_map/hold/pallas_call | solution.py:39
  33.7 3.9 %collective-permute-done.2.refs_3_ = bf16[32,8,4,128]{3,2,1,0:T(4,128)(2,1)S(1)} collective-permute-done((bf16[32,8,4,128]{3,2,1,0:T(4,128)(2,1)S(1)}, bf16[32,8,4,128]{3,2,1,0:T(4,128)(2,1)S(1)}, u32[]{:S(2)}, u32[]{:S(2)}) %collective-permute-start.2) | collective-permute-done | bytes 262176 | tf_op jit(solution)/shard_map/ppermute | solution.py:279
  37.6 0.0 collective-permute-done.1.refs_2_
  37.6 0.0 collective-permute-done.refs_1_
  37.6 2.4 %collective-permute-start.4 = (bf16[32,8,4,128]{3,2,1,0:T(4,128)(2,1)S(1)}, bf16[32,8,4,128]{3,2,1,0:T(4,128)(2,1)S(1)}, u32[]{:S(2)}, u32[]{:S(2)}) collective-permute-start(bf16[32,8,4,128]{3,2,1,0:T(4,128)(2,1)S(1)} %collective-permute-done.refs_1_), channel_id=1, source_target_pairs={{0,32},{32,0},{1,33},{33,1},{2,34},{34,2},{3,35},{35,3},{4,36},{36... | collective-permute-start | bytes 786440 | tf_op jit(solution)/shard_map/ppermute | solution.py:279
  40.0 0.0 collective-permute-start.5
  40.0 0.5 collective-permute-start.6
  40.5 0.0 copy-done
  40.5 0.0 copy-done.1
  40.5 0.1 pad_add_fusion.meta
  40.5 0.0 collective-permute-done.3.refs_4_
  40.6 0.6 collective-permute-done.4.refs_5_
  41.1 0.4 collective-permute-done.5.refs_6_
  41.5 0.4 collective-permute-done.6.refs_7_
  41.9 4.3 %blocks.1 = bf16[32,17,4,128]{3,2,1,0:T(4,128)(2,1)} custom-call(s32[32]{0:T(128)S(1)} %pad_add_fusion.meta, bf16[16,128,1024]{2,1,0:T(8,128)(2,1)S(1)} %get-tuple-element.15.k_all, bf16[16,128,1024]{2,1,0:T(8,128)(2,1)S(1)} %get-tuple-element.16.v_all, bf16[32,8,4,128]{3,2,1,0:T(4,128)(2,1)S(1)} %get-tuple-element.17.refs_0_, ...), custom_call_target="tpu_custom_call" | custom-call | flops 134217728 | bytes 9437184 | tf_op jit(solution)/shard_map/blocks/pallas_call | solution.py:142
  46.2 4.8 %all-to-all-start.1 = ((bf16[32,17,4,128]{3,2,1,0:T(4,128)(2,1)}), bf16[32,17,4,128]{3,2,1,0:T(4,128)(2,1)S(1)}, u32[]{:S(2)}, u32[]{:S(2)}) async-start(bf16[32,17,4,128]{3,2,1,0:T(4,128)(2,1)} %blocks.1), calls=%async_computation.1 | async-start | bytes 1114112 | tf_op jit(solution)/shard_map/all_to_all | solution.py:293
  51.0 1.5 %fresh.1 = f32[5,8,128]{2,1,0:T(8,128)} custom-call(bf16[2,8,256]{2,1,0:T(8,128)(2,1)} %q_ref, bf16[2,8,1024]{2,1,0:T(8,128)(2,1)} %keys_ref.1, bf16[2,8,1024]{2,1,0:T(8,128)(2,1)} %values_ref.1), custom_call_target="tpu_custom_call" | custom-call | flops 131072 | bytes 65536 | tf_op jit(solution)/shard_map/fresh/pallas_call | solution.py:225
  52.5 15.6 %all-to-all-done.1 = bf16[32,17,4,128]{3,2,1,0:T(4,128)(2,1)S(1)} async-done(((bf16[32,17,4,128]{3,2,1,0:T(4,128)(2,1)}), bf16[32,17,4,128]{3,2,1,0:T(4,128)(2,1)S(1)}, u32[]{:S(2)}, u32[]{:S(2)}) %all-to-all-start.1) | async-done | bytes 557088 | tf_op jit(solution)/shard_map/all_to_all | solution.py:293
  68.1 0.1 slice.32
  68.2 0.2 convert_add_fusion
  68.3 0.1 copy.24
  68.4 0.1 copy.25
  68.5 0.1 reshape.56
  68.7 0.1 mul.10
  68.8 0.1 broadcast_in_dim.59
  68.9 0.1 select_reduce_fusion
  69.1 0.3 fusion.5
  69.4 0.1 copy.31
  69.5 0.1 copy.32
  69.6 0.3 fusion.8
  70.0 0.4 fusion.1
  70.4 12.2 %all_to_all.16.got = f32[8,5,8,128]{3,2,1,0:T(8,128)} all-to-all(f32[8,5,8,128]{3,2,1,0:T(8,128)S(1)} %pad_maximum_fusion), channel_id=1, replica_groups=mesh['y'=4,'core'=2,'z'=8,'x'=4] {'y','core'}, dimensions={0} | all-to-all | bytes 327680 | tf_op jit(solution)/shard_map/all_to_all | solution.py:299
  82.6 1.7 %finish.1 = bf16[2,8,256]{2,1,0:T(8,128)(2,1)} custom-call(f32[8,5,8,128]{3,2,1,0:T(8,128)} %all_to_all.16.got, f32[5,8,128]{2,1,0:T(8,128)} %fresh.1), custom_call_target="tpu_custom_call" | custom-call | tf_op jit(solution)/shard_map/finish/pallas_call | solution.py:262
  (11 shorter events, 0.1 us)
Async XLA Ops:
  23.6 16.8 %copy-start = (s32[16]{0:T(128)S(1)}, s32[16]{0:T(128)}, u32[]{:S(2)}) copy-start(s32[16]{0:T(128)} %param.13) | copy-start | bytes 196
  23.6 16.8 %copy-start.1 = (s32[16]{0:T(128)S(1)}, s32[16]{0:T(128)}, u32[]{:S(2)}) copy-start(s32[16]{0:T(128)} %param.12) | copy-start | bytes 196
  23.6 13.9 %collective-permute-start.2 = (bf16[32,8,4,128]{3,2,1,0:T(4,128)(2,1)S(1)}, bf16[32,8,4,128]{3,2,1,0:T(4,128)(2,1)S(1)}, u32[]{:S(2)}, u32[]{:S(2)}) collective-permute-start(bf16[32,8,4,128]{3,2,1,0:T(4,128)(2,1)S(1)} %all_to_all.15.refs_0_), channel_id=1, source_target_pairs={{0,192},{64,128},{128,64},{192,0},{1,193},{65,129},{129,65},{193,1... | collective-permute-start | bytes 786440 | tf_op jit(solution)/shard_map/ppermute | solution.py:279
  26.4 11.2 %collective-permute-start.1 = (bf16[32,8,4,128]{3,2,1,0:T(4,128)(2,1)S(1)}, bf16[32,8,4,128]{3,2,1,0:T(4,128)(2,1)S(1)}, u32[]{:S(2)}, u32[]{:S(2)}) collective-permute-start(bf16[32,8,4,128]{3,2,1,0:T(4,128)(2,1)S(1)} %all_to_all.15.refs_0_), channel_id=1, source_target_pairs={{0,128},{64,192},{128,0},{192,64},{1,129},{65,193},{129,1},{193,65... | collective-permute-start | bytes 786440 | tf_op jit(solution)/shard_map/ppermute | solution.py:279
  26.7 10.9 %collective-permute-start = (bf16[32,8,4,128]{3,2,1,0:T(4,128)(2,1)S(1)}, bf16[32,8,4,128]{3,2,1,0:T(4,128)(2,1)S(1)}, u32[]{:S(2)}, u32[]{:S(2)}) collective-permute-start(bf16[32,8,4,128]{3,2,1,0:T(4,128)(2,1)S(1)} %all_to_all.15.refs_0_), channel_id=1, source_target_pairs={{0,64},{64,0},{128,192},{192,128},{1,65},{65,1},{129,193},{193,129... | collective-permute-start | bytes 786440 | tf_op jit(solution)/shard_map/ppermute | solution.py:279
  27.0 13.5 %collective-permute-start.3 = (bf16[32,8,4,128]{3,2,1,0:T(4,128)(2,1)S(1)}, bf16[32,8,4,128]{3,2,1,0:T(4,128)(2,1)S(1)}, u32[]{:S(2)}, u32[]{:S(2)}) collective-permute-start(bf16[32,8,4,128]{3,2,1,0:T(4,128)(2,1)S(1)} %all_to_all.15.refs_0_), channel_id=1, source_target_pairs={{0,32},{32,0},{1,33},{33,1},{2,34},{34,2},{3,35},{35,3},{4,36},{36... | collective-permute-start | bytes 786440 | tf_op jit(solution)/shard_map/ppermute | solution.py:279
  37.6 3.5 %collective-permute-start.4 = (bf16[32,8,4,128]{3,2,1,0:T(4,128)(2,1)S(1)}, bf16[32,8,4,128]{3,2,1,0:T(4,128)(2,1)S(1)}, u32[]{:S(2)}, u32[]{:S(2)}) collective-permute-start(bf16[32,8,4,128]{3,2,1,0:T(4,128)(2,1)S(1)} %collective-permute-done.refs_1_), channel_id=1, source_target_pairs={{0,32},{32,0},{1,33},{33,1},{2,34},{34,2},{3,35},{35,3},{4,36},{36... | collective-permute-start | bytes 786440 | tf_op jit(solution)/shard_map/ppermute | solution.py:279
  40.0 1.5 %collective-permute-start.5 = (bf16[32,8,4,128]{3,2,1,0:T(4,128)(2,1)S(1)}, bf16[32,8,4,128]{3,2,1,0:T(4,128)(2,1)S(1)}, u32[]{:S(2)}, u32[]{:S(2)}) collective-permute-start(bf16[32,8,4,128]{3,2,1,0:T(4,128)(2,1)S(1)} %collective-permute-done.1.refs_2_), channel_id=1, source_target_pairs={{0,32},{32,0},{1,33},{33,1},{2,34},{34,2},{3,35},{35,3},{4,36},{36... | collective-permute-start | bytes 786440 | tf_op jit(solution)/shard_map/ppermute | solution.py:279
  40.0 1.9 %collective-permute-start.6 = (bf16[32,8,4,128]{3,2,1,0:T(4,128)(2,1)S(1)}, bf16[32,8,4,128]{3,2,1,0:T(4,128)(2,1)S(1)}, u32[]{:S(2)}, u32[]{:S(2)}) collective-permute-start(bf16[32,8,4,128]{3,2,1,0:T(4,128)(2,1)S(1)} %collective-permute-done.2.refs_3_), channel_id=1, source_target_pairs={{0,32},{32,0},{1,33},{33,1},{2,34},{34,2},{3,35},{35,3},{4,36},{36... | collective-permute-start | bytes 786440 | tf_op jit(solution)/shard_map/ppermute | solution.py:279
  46.2 21.8 %all-to-all-start.1 = ((bf16[32,17,4,128]{3,2,1,0:T(4,128)(2,1)}), bf16[32,17,4,128]{3,2,1,0:T(4,128)(2,1)S(1)}, u32[]{:S(2)}, u32[]{:S(2)}) async-start(bf16[32,17,4,128]{3,2,1,0:T(4,128)(2,1)} %blocks.1), calls=%async_computation.1 | async-start | bytes 1114112 | tf_op jit(solution)/shard_map/all_to_all | solution.py:293

commit v9 on v8

--- a/solution.py
+++ b/solution.py
@@ -55,7 +55,7 @@
     cols = n_tp * depth
     n_kv = KVH
     per, n_x = cols // n_kv, n_tp // n_kv
-    together = 8
+    together = 16
     rows = pieces[0].shape[1]
     n_y, row_bits = len(pieces) // 2, rows.bit_length() - 1
     here_y, here_core = lax.axis_index("y"), lax.axis_index("core")
@@ -129,7 +129,9 @@
             mix(first + j, rounded[j])
         return later
 
-    rounded = lax.fori_loop(0, groups - 1, step, weigh(0))
+    rounded = weigh(0)
+    if groups > 1:
+        rounded = lax.fori_loop(0, groups - 1, step, rounded)
     for j in range(together):
         mix(slots - together + j, rounded[j])
     packed = stats[...].T.astype(jnp.bfloat16)

time: 84.6 us -> 84.4 us (level)
  no operation moved by 1% of the time
where the time goes in v9:
time: 84.4 us; the launch traced here: 84 us
  blocking collectives  35 us (41%)
  waiting for transfers between devices  20.7 us (25%)
  starting transfers between devices  14.2 us (17%)
  Pallas kernels  10.7 us (13%)
  local copies, waits for them, and re-layouts  1.62 us (2%)
    all_to_all x1, blocking collectives, body(): lax.all_to_all(jnp.broadcast_to(rows[None], (n_z * n_x,) + rows.shape), (...  22.9 us
    all_to_all x1, waiting for transfers between devices, body(): lax.all_to_all(sent, ('z', 'x'), split_axis=0, concat_axis=0, tiled=True)  15.5 us
    all_to_all x1, blocking collectives, body(): lax.all_to_all(jnp.concatenate([part, level], axis=1), ('y', 'core'), 0,...  12.2 us
    ppermute x7, starting transfers between devices, from_other(): lax.ppermute(value, axis, [(j, j ^ m) for j in range(lax.axis_size(axis))])  9.44 us
    ppermute x7, waiting for transfers between devices, from_other(): lax.ppermute(value, axis, [(j, j ^ m) for j in range(lax.axis_size(axis))])  5.19 us
    all_to_all x1, starting transfers between devices, body(): lax.all_to_all(sent, ('z', 'x'), split_axis=0, concat_axis=0, tiled=True)  4.78 us
    pallas_call x1, Pallas kernels, blocks(): pl.pallas_call(block_kernel, out_shape=jax.ShapeDtypeStruct((n_tp, slots...  4.05 us
    pallas_call x1, Pallas kernels, hold(): pl.pallas_call(hold_kernel, out_shape=[jax.ShapeDtypeStruct(x.shape, x.dt...  3.51 us
  transfers between devices with their start and end apart: 8, of which 5 were waited for; matrix products, arithmetic and copies ran while one was open for 0% of the time, Pallas kernels for 6%

profile of v9, /device:TPU:1, one launch (start us, length us, event | category | flops | bytes accessed | tf_op | source)
XLA Modules:
  0.0 84.0 jit_solution(13970680826386329135)
XLA Ops:
  0.0 0.7 copy.23
  0.7 0.1 broadcast_in_dim.57
  0.8 22.9 %all_to_all.15.refs_0_ = bf16[32,8,4,128]{3,2,1,0:T(4,128)(2,1)S(1)} all-to-all(bf16[32,8,4,128]{3,2,1,0:T(4,128)(2,1)S(1)} %broadcast_in_dim.57), channel_id=1, replica_groups=mesh['y'=4,'core'=2,'z'=8,'x'=4] {'z','x'}, dimensions={0} | all-to-all | bytes 524288 | tf_op jit(solution)/shard_map/all_to_all | solution.py:285
  23.6 0.0 copy-start
  23.6 0.0 copy-start.1
  23.6 2.7 %collective-permute-start.2 = (bf16[32,8,4,128]{3,2,1,0:T(4,128)(2,1)S(1)}, bf16[32,8,4,128]{3,2,1,0:T(4,128)(2,1)S(1)}, u32[]{:S(2)}, u32[]{:S(2)}) collective-permute-start(bf16[32,8,4,128]{3,2,1,0:T(4,128)(2,1)S(1)} %all_to_all.15.refs_0_), channel_id=1, source_target_pairs={{0,192},{64,128},{128,64},{192,0},{1,193},{65,129},{129,65},{193,1... | collective-permute-start | bytes 786440 | tf_op jit(solution)/shard_map/ppermute | solution.py:281
  26.4 0.3 collective-permute-start.1
  26.7 0.3 collective-permute-start
  27.0 3.1 %collective-permute-start.3 = (bf16[32,8,4,128]{3,2,1,0:T(4,128)(2,1)S(1)}, bf16[32,8,4,128]{3,2,1,0:T(4,128)(2,1)S(1)}, u32[]{:S(2)}, u32[]{:S(2)}) collective-permute-start(bf16[32,8,4,128]{3,2,1,0:T(4,128)(2,1)S(1)} %all_to_all.15.refs_0_), channel_id=1, source_target_pairs={{0,32},{32,0},{1,33},{33,1},{2,34},{34,2},{3,35},{35,3},{4,36},{36... | collective-permute-start | bytes 786440 | tf_op jit(solution)/shard_map/ppermute | solution.py:281
  30.2 3.5 %hold.1 = (bf16[32,8,4,128]{3,2,1,0:T(4,128)(2,1)S(1)}, bf16[16,128,1024]{2,1,0:T(8,128)(2,1)S(1)}, bf16[16,128,1024]{2,1,0:T(8,128)(2,1)S(1)}) custom-call(bf16[32,8,4,128]{3,2,1,0:T(4,128)(2,1)S(1)} %all_to_all.15.refs_0_, bf16[16,128,1024]{2,1,0:T(8,128)(2,1)} %refs_1_.1, bf16[16,128,1024]{2,1,0:T(8,128)(2,1)} %refs_2_.1), custom_call_target="tpu_custom_call" | custom-call | bytes 17301504 | tf_op jit(solution)/shard_map/hold/pallas_call | solution.py:39
  33.7 3.9 %collective-permute-done.2.refs_3_ = bf16[32,8,4,128]{3,2,1,0:T(4,128)(2,1)S(1)} collective-permute-done((bf16[32,8,4,128]{3,2,1,0:T(4,128)(2,1)S(1)}, bf16[32,8,4,128]{3,2,1,0:T(4,128)(2,1)S(1)}, u32[]{:S(2)}, u32[]{:S(2)}) %collective-permute-start.2) | collective-permute-done | bytes 262176 | tf_op jit(solution)/shard_map/ppermute | solution.py:281
  37.6 0.0 collective-permute-done.1.refs_2_
  37.6 0.0 collective-permute-done.refs_1_
  37.6 2.4 %collective-permute-start.4 = (bf16[32,8,4,128]{3,2,1,0:T(4,128)(2,1)S(1)}, bf16[32,8,4,128]{3,2,1,0:T(4,128)(2,1)S(1)}, u32[]{:S(2)}, u32[]{:S(2)}) collective-permute-start(bf16[32,8,4,128]{3,2,1,0:T(4,128)(2,1)S(1)} %collective-permute-done.refs_1_), channel_id=1, source_target_pairs={{0,32},{32,0},{1,33},{33,1},{2,34},{34,2},{3,35},{35,3},{4,36},{36... | collective-permute-start | bytes 786440 | tf_op jit(solution)/shard_map/ppermute | solution.py:281
  40.0 0.0 collective-permute-start.5
  40.0 0.5 collective-permute-start.6
  40.5 0.0 copy-done
  40.5 0.0 copy-done.1
  40.5 0.1 pad_add_fusion.meta
  40.5 0.0 collective-permute-done.3.refs_4_
  40.6 0.6 collective-permute-done.4.refs_5_
  41.1 0.4 collective-permute-done.5.refs_6_
  41.5 0.4 collective-permute-done.6.refs_7_
  41.9 4.0 %blocks.1 = bf16[32,17,4,128]{3,2,1,0:T(4,128)(2,1)} custom-call(s32[32]{0:T(128)S(1)} %pad_add_fusion.meta, bf16[16,128,1024]{2,1,0:T(8,128)(2,1)S(1)} %get-tuple-element.15.k_all, bf16[16,128,1024]{2,1,0:T(8,128)(2,1)S(1)} %get-tuple-element.16.v_all, bf16[32,8,4,128]{3,2,1,0:T(4,128)(2,1)S(1)} %get-tuple-element.17.refs_0_, ...), custom_call_target="tpu_custom_call" | custom-call | flops 134217728 | bytes 9437184 | tf_op jit(solution)/shard_map/blocks/pallas_call | solution.py:144
  45.9 4.8 %all-to-all-start.1 = ((bf16[32,17,4,128]{3,2,1,0:T(4,128)(2,1)}), bf16[32,17,4,128]{3,2,1,0:T(4,128)(2,1)S(1)}, u32[]{:S(2)}, u32[]{:S(2)}) async-start(bf16[32,17,4,128]{3,2,1,0:T(4,128)(2,1)} %blocks.1), calls=%async_computation.1 | async-start | bytes 1114112 | tf_op jit(solution)/shard_map/all_to_all | solution.py:295
  50.7 1.5 %fresh.1 = f32[5,8,128]{2,1,0:T(8,128)} custom-call(bf16[2,8,256]{2,1,0:T(8,128)(2,1)} %q_ref, bf16[2,8,1024]{2,1,0:T(8,128)(2,1)} %keys_ref.1, bf16[2,8,1024]{2,1,0:T(8,128)(2,1)} %values_ref.1), custom_call_target="tpu_custom_call" | custom-call | flops 131072 | bytes 65536 | tf_op jit(solution)/shard_map/fresh/pallas_call | solution.py:227
  52.2 15.5 %all-to-all-done.1 = bf16[32,17,4,128]{3,2,1,0:T(4,128)(2,1)S(1)} async-done(((bf16[32,17,4,128]{3,2,1,0:T(4,128)(2,1)}), bf16[32,17,4,128]{3,2,1,0:T(4,128)(2,1)S(1)}, u32[]{:S(2)}, u32[]{:S(2)}) %all-to-all-start.1) | async-done | bytes 557088 | tf_op jit(solution)/shard_map/all_to_all | solution.py:295
  67.8 0.1 slice.32
  67.9 0.2 convert_add_fusion
  68.0 0.1 copy.24
  68.1 0.1 copy.25
  68.2 0.1 reshape.56
  68.4 0.1 mul.10
  68.5 0.1 broadcast_in_dim.59
  68.6 0.1 select_reduce_fusion
  68.8 0.3 fusion.5
  69.1 0.1 copy.31
  69.2 0.1 copy.32
  69.3 0.3 fusion.8
  69.7 0.4 fusion.1
  70.1 12.2 %all_to_all.16.got = f32[8,5,8,128]{3,2,1,0:T(8,128)} all-to-all(f32[8,5,8,128]{3,2,1,0:T(8,128)S(1)} %pad_maximum_fusion), channel_id=1, replica_groups=mesh['y'=4,'core'=2,'z'=8,'x'=4] {'y','core'}, dimensions={0} | all-to-all | bytes 327680 | tf_op jit(solution)/shard_map/all_to_all | solution.py:301
  82.3 1.7 %finish.1 = bf16[2,8,256]{2,1,0:T(8,128)(2,1)} custom-call(f32[8,5,8,128]{3,2,1,0:T(8,128)} %all_to_all.16.got, f32[5,8,128]{2,1,0:T(8,128)} %fresh.1), custom_call_target="tpu_custom_call" | custom-call | tf_op jit(solution)/shard_map/finish/pallas_call | solution.py:264
  (11 shorter events, 0.1 us)
Async XLA Ops:
  23.6 16.8 %copy-start = (s32[16]{0:T(128)S(1)}, s32[16]{0:T(128)}, u32[]{:S(2)}) copy-start(s32[16]{0:T(128)} %param.13) | copy-start | bytes 196
  23.6 16.8 %copy-start.1 = (s32[16]{0:T(128)S(1)}, s32[16]{0:T(128)}, u32[]{:S(2)}) copy-start(s32[16]{0:T(128)} %param.12) | copy-start | bytes 196
  23.6 13.9 %collective-permute-start.2 = (bf16[32,8,4,128]{3,2,1,0:T(4,128)(2,1)S(1)}, bf16[32,8,4,128]{3,2,1,0:T(4,128)(2,1)S(1)}, u32[]{:S(2)}, u32[]{:S(2)}) collective-permute-start(bf16[32,8,4,128]{3,2,1,0:T(4,128)(2,1)S(1)} %all_to_all.15.refs_0_), channel_id=1, source_target_pairs={{0,192},{64,128},{128,64},{192,0},{1,193},{65,129},{129,65},{193,1... | collective-permute-start | bytes 786440 | tf_op jit(solution)/shard_map/ppermute | solution.py:281
  26.4 11.2 %collective-permute-start.1 = (bf16[32,8,4,128]{3,2,1,0:T(4,128)(2,1)S(1)}, bf16[32,8,4,128]{3,2,1,0:T(4,128)(2,1)S(1)}, u32[]{:S(2)}, u32[]{:S(2)}) collective-permute-start(bf16[32,8,4,128]{3,2,1,0:T(4,128)(2,1)S(1)} %all_to_all.15.refs_0_), channel_id=1, source_target_pairs={{0,128},{64,192},{128,0},{192,64},{1,129},{65,193},{129,1},{193,65... | collective-permute-start | bytes 786440 | tf_op jit(solution)/shard_map/ppermute | solution.py:281
  26.7 10.9 %collective-permute-start = (bf16[32,8,4,128]{3,2,1,0:T(4,128)(2,1)S(1)}, bf16[32,8,4,128]{3,2,1,0:T(4,128)(2,1)S(1)}, u32[]{:S(2)}, u32[]{:S(2)}) collective-permute-start(bf16[32,8,4,128]{3,2,1,0:T(4,128)(2,1)S(1)} %all_to_all.15.refs_0_), channel_id=1, source_target_pairs={{0,64},{64,0},{128,192},{192,128},{1,65},{65,1},{129,193},{193,129... | collective-permute-start | bytes 786440 | tf_op jit(solution)/shard_map/ppermute | solution.py:281
  27.0 13.5 %collective-permute-start.3 = (bf16[32,8,4,128]{3,2,1,0:T(4,128)(2,1)S(1)}, bf16[32,8,4,128]{3,2,1,0:T(4,128)(2,1)S(1)}, u32[]{:S(2)}, u32[]{:S(2)}) collective-permute-start(bf16[32,8,4,128]{3,2,1,0:T(4,128)(2,1)S(1)} %all_to_all.15.refs_0_), channel_id=1, source_target_pairs={{0,32},{32,0},{1,33},{33,1},{2,34},{34,2},{3,35},{35,3},{4,36},{36... | collective-permute-start | bytes 786440 | tf_op jit(solution)/shard_map/ppermute | solution.py:281
  37.6 3.5 %collective-permute-start.4 = (bf16[32,8,4,128]{3,2,1,0:T(4,128)(2,1)S(1)}, bf16[32,8,4,128]{3,2,1,0:T(4,128)(2,1)S(1)}, u32[]{:S(2)}, u32[]{:S(2)}) collective-permute-start(bf16[32,8,4,128]{3,2,1,0:T(4,128)(2,1)S(1)} %collective-permute-done.refs_1_), channel_id=1, source_target_pairs={{0,32},{32,0},{1,33},{33,1},{2,34},{34,2},{3,35},{35,3},{4,36},{36... | collective-permute-start | bytes 786440 | tf_op jit(solution)/shard_map/ppermute | solution.py:281
  40.0 1.5 %collective-permute-start.5 = (bf16[32,8,4,128]{3,2,1,0:T(4,128)(2,1)S(1)}, bf16[32,8,4,128]{3,2,1,0:T(4,128)(2,1)S(1)}, u32[]{:S(2)}, u32[]{:S(2)}) collective-permute-start(bf16[32,8,4,128]{3,2,1,0:T(4,128)(2,1)S(1)} %collective-permute-done.1.refs_2_), channel_id=1, source_target_pairs={{0,32},{32,0},{1,33},{33,1},{2,34},{34,2},{3,35},{35,3},{4,36},{36... | collective-permute-start | bytes 786440 | tf_op jit(solution)/shard_map/ppermute | solution.py:281
  40.0 1.9 %collective-permute-start.6 = (bf16[32,8,4,128]{3,2,1,0:T(4,128)(2,1)S(1)}, bf16[32,8,4,128]{3,2,1,0:T(4,128)(2,1)S(1)}, u32[]{:S(2)}, u32[]{:S(2)}) collective-permute-start(bf16[32,8,4,128]{3,2,1,0:T(4,128)(2,1)S(1)} %collective-permute-done.2.refs_3_), channel_id=1, source_target_pairs={{0,32},{32,0},{1,33},{33,1},{2,34},{34,2},{3,35},{35,3},{4,36},{36... | collective-permute-start | bytes 786440 | tf_op jit(solution)/shard_map/ppermute | solution.py:281
  45.9 21.8 %all-to-all-start.1 = ((bf16[32,17,4,128]{3,2,1,0:T(4,128)(2,1)}), bf16[32,17,4,128]{3,2,1,0:T(4,128)(2,1)S(1)}, u32[]{:S(2)}, u32[]{:S(2)}) async-start(bf16[32,17,4,128]{3,2,1,0:T(4,128)(2,1)} %blocks.1), calls=%async_computation.1 | async-start | bytes 1114112 | tf_op jit(solution)/shard_map/all_to_all | solution.py:295
